TPU v7x, 32 devices: a whole 2x2x4 slice. The times are simulated.
32 devices in a mesh: space: 2 (over x), blk: 16 (over z, y, core).
Axes of the slice: x: 2, y: 2, z: 4, core: 2. Of those that a mesh axis runs over, the one named last changes fastest.
Arguments:
- snapshots: bfloat16 [20480, 1024], P('blk', 'space'), may hold values from -6 to 6
- row_scales: float32 [20480], P('blk'), may hold values from 0.3 to 3
- block_offsets: int32 [64], P('blk'), may hold values from 0 to 768, as said below
- freq_index: int32 [16], replicated, may hold values from 1 to 255
Outputs:
- modes: float32 [16, 1024, 128], P('blk', 'space')
- r_factor: float32 [16, 2, 64, 64], P('blk')
Inputs may be any that keep to these rules, and one draw needn't show every extreme that they name: `block_offsets`: block offsets index the snapshots held by the block's own index of blk; within every group of 4 blocks they are distinct and increasing, block i of a group lies between i * 256 - 512 / 4 and i * 256 + 512 / 4; in the first group the first is 0 and the last is 768.
All inputs are finite; a program needn't handle non-finite values.
Results may differ from a plain program's by a relative error of at most 0.0064.
Values may be sent and summed in bfloat16 or wider, within the bound.
No kernel may reach another device: no remote copies, remote signals or barrier semaphores. Data moves between devices by JAX's collectives and lax.ppermute only.
A program may use at most 64 MiB of HBM per device.

v0:
```python
import math

import jax
import jax.numpy as jnp
from jax import lax
from jax.sharding import PartitionSpec as P

NFFT = 512


def merged(value, axis, combine):
    everything = lax.all_gather(value, axis)
    initial = everything[0]

    def lap(k, so_far):
        return combine(so_far, everything[k])

    return lax.fori_loop(1, lax.axis_size(axis), lap, initial)


def trig_table(freq_index):
    times = jnp.arange(NFFT, dtype=jnp.int32)
    phase = freq_index[:, None] * times[None, :] % NFFT
    angle = 2.0 * math.pi / NFFT * phase.astype(jnp.float32)
    inv_root = 1.0 / math.sqrt(NFFT)
    table = (
        jnp.stack([jnp.cos(angle), -jnp.sin(angle)], 1).reshape(2 * freq_index.shape[0], NFFT)
        * inv_root
    )
    hann = 0.5 - 0.5 * jnp.cos(2.0 * math.pi / NFFT * times.astype(jnp.float32))
    return (table, hann)


def upper_of(matrix):
    return jnp.swapaxes(jnp.linalg.cholesky(matrix), -1, -2)


def merge_pair(first_r, second_r):
    summed = jnp.einsum("fka,fkb->fab", first_r, first_r, precision=lax.Precision.HIGHEST)
    summed = summed + jnp.einsum(
        "fka,fkb->fab", second_r, second_r, precision=lax.Precision.HIGHEST
    )
    return upper_of(summed)


def stacked_gram(regrouped, total_points):
    pairs = regrouped.reshape(regrouped.shape[0], regrouped.shape[1], -1, 2)
    rotated = jnp.stack([-pairs[..., 1], pairs[..., 0]], -1).reshape(regrouped.shape)
    stacked = jnp.concatenate([regrouped, rotated], 1)
    return (
        jnp.einsum("fpa,fpb->fab", stacked, stacked, preferred_element_type=jnp.float32)
        / total_points
    )


def local(snapshots, row_scales, block_offsets, freq_index):
    table, hann = trig_table(freq_index)
    blocks_here = block_offsets.shape[0]
    points_here = snapshots.shape[1]
    freq_count = freq_index.shape[0]
    windows = jax.vmap(lambda start: lax.dynamic_slice_in_dim(snapshots, start, NFFT, 0))(
        block_offsets
    )
    scaled = jax.vmap(lambda start: lax.dynamic_slice_in_dim(row_scales, start, NFFT, 0))(
        block_offsets
    )
    coeffs = (table[None, :, :] * (hann[None, :] * scaled)[:, None, :]).astype(jnp.bfloat16)
    spectra = jnp.einsum(
        "bkt,btp->bkp", coeffs, windows, preferred_element_type=jnp.float32
    ).astype(jnp.bfloat16)
    spectra = spectra.reshape(blocks_here, freq_count, 2, points_here).transpose(1, 3, 0, 2)
    spectra = spectra.reshape(freq_count, points_here, 2 * blocks_here)
    regrouped = lax.all_to_all(spectra, "blk", split_axis=0, concat_axis=2, tiled=True)
    total_points = points_here * lax.axis_size("space")
    upper = merged(upper_of(stacked_gram(regrouped, total_points)), "space", merge_pair)
    lower_factor = jnp.swapaxes(upper, 1, 2)
    width = lower_factor.shape[-1]
    identity = jnp.broadcast_to(jnp.eye(width, dtype=jnp.float32), lower_factor.shape)
    inverse_lower = jax.scipy.linalg.solve_triangular(lower_factor, identity, lower=True)
    modes = jnp.einsum(
        "fpa,fba->fpb",
        regrouped.astype(jnp.float32),
        inverse_lower,
        precision=lax.Precision.HIGHEST,
    )
    r_factor = jnp.stack([upper[:, 0::2, 0::2], upper[:, 0::2, 1::2]], 1)
    return (modes, r_factor)


def solution(mesh):
    return jax.shard_map(
        local,
        mesh=mesh,
        in_specs=(P("blk", "space"), P("blk"), P("blk"), P()),
        out_specs=(P("blk", "space", None), P("blk", None, None, None)),
        check_vma=False,
    )
```

profile of v0, /device:TPU:0, one launch (start us, length us, event | category | flops | bytes accessed | tf_op | source)
XLA Modules:
  0.0 82.1 jit_solution(9541408215473388479)
XLA Ops:
  0.7 0.7 fusion.21
  1.4 10.2 %while.3 = (s32[]{:T(128)}, bf16[1280,512]{1,0:T(8,128)(2,1)}, s32[4,2]{0,1:T(2,128)S(1)}, bf16[4,512,512]{2,1,0:T(8,128)(2,1)S(1)}, s32[]{:T(128)}) while((s32[]{:T(128)}, bf16[1280,512]{1,0:T(8,128)(2,1)}, s32[4,2]{0,1:T(2,128)S(1)}, bf16[4,512,512]{2,1,0:T(8,128)(2,1)S(1)}, s32[]{:T(128)}) %tuple.42), condition=%wide.while_cond.1, body=%wide.while_body.1.sunk | while | flops 2 | bytes 1048681 | solution.py:61
  1.5 0.6 slice.61
  2.0 1.9 %bitcast_dynamic-update-slice_fusion.2 = bf16[4,512,512]{2,1,0:T(8,128)(2,1)S(1)} fusion(bf16[4,512,512]{2,1,0:T(8,128)(2,1)S(1)} %get-tuple-element.121, s32[]{:T(128)S(6)} %copy.57, bf16[1280,512]{1,0:T(8,128)(2,1)} %get-tuple-element.124, s32[]{:T(128)} %bitcast.66), kind=kLoop, calls=%fused_computation.1.clone.1 | loop fusion | bytes 1048584 | tf_op jit(solution)/shard_map/vmap()/gather
  4.0 0.6 slice.61
  4.6 1.9 %bitcast_dynamic-update-slice_fusion.2 = bf16[4,512,512]{2,1,0:T(8,128)(2,1)S(1)} fusion(bf16[4,512,512]{2,1,0:T(8,128)(2,1)S(1)} %get-tuple-element.121, s32[]{:T(128)S(6)} %copy.57, bf16[1280,512]{1,0:T(8,128)(2,1)} %get-tuple-element.124, s32[]{:T(128)} %bitcast.66), kind=kLoop, calls=%fused_computation.1.clone.1 | loop fusion | bytes 1048584 | tf_op jit(solution)/shard_map/vmap()/gather
  6.6 0.6 slice.61
  7.1 1.9 %bitcast_dynamic-update-slice_fusion.2 = bf16[4,512,512]{2,1,0:T(8,128)(2,1)S(1)} fusion(bf16[4,512,512]{2,1,0:T(8,128)(2,1)S(1)} %get-tuple-element.121, s32[]{:T(128)S(6)} %copy.57, bf16[1280,512]{1,0:T(8,128)(2,1)} %get-tuple-element.124, s32[]{:T(128)} %bitcast.66), kind=kLoop, calls=%fused_computation.1.clone.1 | loop fusion | bytes 1048584 | tf_op jit(solution)/shard_map/vmap()/gather
  9.1 0.6 slice.61
  9.7 1.9 %bitcast_dynamic-update-slice_fusion.2 = bf16[4,512,512]{2,1,0:T(8,128)(2,1)S(1)} fusion(bf16[4,512,512]{2,1,0:T(8,128)(2,1)S(1)} %get-tuple-element.121, s32[]{:T(128)S(6)} %copy.57, bf16[1280,512]{1,0:T(8,128)(2,1)} %get-tuple-element.124, s32[]{:T(128)} %bitcast.66), kind=kLoop, calls=%fused_computation.1.clone.1 | loop fusion | bytes 1048584 | tf_op jit(solution)/shard_map/vmap()/gather
  11.6 8.2 %while.2 = (s32[]{:T(128)}, f32[1280]{0:T(1024)}, s32[4,1]{0,1:T(1,128)S(1)}, f32[4,512]{1,0:T(4,128)S(1)}, s32[]{:T(128)}, /*index=5*/s32[]{:T(128)}) while((s32[]{:T(128)}, f32[1280]{0:T(1024)}, s32[4,1]{0,1:T(1,128)S(1)}, f32[4,512]{1,0:T(4,128)S(1)}, s32[]{:T(128)}, /*index=5*/s32[]{:T(128)}) %tuple.45), condition=%wide.while_cond, body=%wide.while_body.sunk | while | flops 2 | bytes 8289 | solution.py:64
  11.6 0.6 constant_dynamic-slice_fusion.4
  12.2 1.4 %dynamic-slice.15 = f32[512]{0:T(512)S(1)} dynamic-slice(f32[1280]{0:T(1024)} %get-tuple-element.141, s32[]{:T(128)} %bitcast.63), dynamic_slice_sizes={512} | dynamic-slice | bytes 4100 | tf_op jit(solution)/shard_map/vmap()/gather
  13.6 0.6 constant_dynamic-slice_fusion.4
  14.2 1.4 %dynamic-slice.15 = f32[512]{0:T(512)S(1)} dynamic-slice(f32[1280]{0:T(1024)} %get-tuple-element.141, s32[]{:T(128)} %bitcast.63), dynamic_slice_sizes={512} | dynamic-slice | bytes 4100 | tf_op jit(solution)/shard_map/vmap()/gather
  15.7 0.6 constant_dynamic-slice_fusion.4
  16.3 1.4 %dynamic-slice.15 = f32[512]{0:T(512)S(1)} dynamic-slice(f32[1280]{0:T(1024)} %get-tuple-element.141, s32[]{:T(128)} %bitcast.63), dynamic_slice_sizes={512} | dynamic-slice | bytes 4100 | tf_op jit(solution)/shard_map/vmap()/gather
  17.7 0.6 constant_dynamic-slice_fusion.4
  18.3 1.4 %dynamic-slice.15 = f32[512]{0:T(512)S(1)} dynamic-slice(f32[1280]{0:T(1024)} %get-tuple-element.141, s32[]{:T(128)} %bitcast.63), dynamic_slice_sizes={512} | dynamic-slice | bytes 4100 | tf_op jit(solution)/shard_map/vmap()/gather
  20.8 15.1 %all_to_all.18 = bf16[16,512,8]{1,2,0:T(8,128)(2,1)S(1)} all-to-all(bf16[16,512,8]{1,2,0:T(8,128)(2,1)S(1)} %copy.42), channel_id=1, replica_groups=mesh['space'=2,'blk'=16] {'blk'}, dimensions={0} | all-to-all | bytes 262144 | tf_op jit(solution)/shard_map/all_to_all | solution.py:73
  37.0 11.7 %custom-call.9 = f32[1,128,128]{2,1,0:T(8,128)S(1)} custom-call(f32[1,128,128]{2,1,0:T(8,128)S(1)} %fusion.7), custom_call_target="Cholesky" | custom-call | tf_op jit(solution)/shard_map/jit(cholesky)/cholesky | solution.py:35
  48.8 0.6 compare_reduce_fusion.1
  49.4 0.7 select_bitcast_fusion
  50.2 5.1 %all-gather = f32[2,128,128]{2,1,0:T(8,128)S(1)} all-gather(f32[1,128,128]{2,1,0:T(8,128)S(1)} %copy.45), channel_id=2, replica_groups=mesh['space'=2,'blk'=16] {'space'}, dimensions={0}, use_global_device_ids=true | all-gather | bytes 196608 | tf_op jit(solution)/shard_map/all_gather | solution.py:12
  56.0 11.7 %custom-call.10 = f32[1,128,128]{2,1,0:T(8,128)S(1)} custom-call(f32[1,128,128]{2,1,0:T(8,128)S(1)} %fusion.6), custom_call_target="Cholesky" | custom-call | tf_op jit(solution)/shard_map/while/body/eval_jaxpr/jit(cholesky)/cholesky | solution.py:35
  67.8 0.6 compare_reduce_fusion
  68.4 0.7 fusion.13
  69.1 0.6 slice.30
  69.7 0.6 slice.29
  70.3 9.8 %custom-call.7 = f32[1,128,128]{1,2,0:T(8,128)S(1)} custom-call(f32[1,128,128]{2,1,0:T(8,128)S(1)} %get-tuple-element.60), custom_call_target="InvertDiagBlocksLowerTriangular" | custom-call | tf_op jit(solution)/shard_map/jit(_solve_triangular)/triangular_solve | solution.py:79
  80.4 0.7 copy.49
  81.1 1.0 %convolution_bitcast_fusion = f32[1,512,128]{2,1,0:T(8,128)} fusion(f32[128,128]{1,0:T(8,128)S(1)} %fusion.8, bf16[16,512,8]{1,2,0:T(8,128)(2,1)S(1)} %all_to_all.18), kind=kOutput, calls=%fused_computation.3 | convolution fusion | flops 100663296 | bytes 458752 | tf_op jit(solution)/shard_map/fpa,fba->fpb/dot_general | solution.py:80
  (39 shorter events, 3.6 us)
Async XLA Ops:
  1.4 18.4 %copy-start = (s32[16]{0:T(128)S(1)}, s32[16]{0:T(128)}, u32[]{:S(2)}) copy-start(s32[16]{0:T(128)} %param.8) | copy-start | bytes 196
where the time goes:
time: 82.7 us; the launch traced here: 82.1 us
  other arithmetic  37.5 us (45%)
  local copies, waits for them, and re-layouts  20.9 us (25%)
  blocking collectives  20.2 us (24%)
  matrix products  2.53 us (3%)
  between operations  0.85 us (1%)
    another operation x6, other arithmetic, upper_of(): return jnp.swapaxes(jnp.linalg.cholesky(matrix), -1, -2)  24.8 us
    gather x24, local copies, waits for them, and re-layouts  18.3 us
    all_to_all x1, blocking collectives, local(): lax.all_to_all(spectra, 'blk', split_axis=0, concat_axis=2, tiled=True)  15.1 us
    another operation x1, other arithmetic, local(): jax.scipy.linalg.solve_triangular(lower_factor, identity, lower=True)  9.81 us
    all_gather x1, blocking collectives, merged(): everything = lax.all_gather(value, axis)  5.12 us

commit v1 on v0

v1 whole, which is shorter than its diff:
```python
import functools
import math

import jax
import jax.numpy as jnp
from jax import lax
from jax.experimental import pallas as pl
from jax.experimental.pallas import tpu as pltpu
from jax.sharding import PartitionSpec as P

NFFT = 512
PANEL = 4
SUB = 8
SIN_COEFS = (
    0.9999999765895043,
    -0.1666664763439475,
    0.008332899819203531,
    -0.0001980089750772882,
    2.5904879854375602e-06,
)


def cos_of_phase(phase):
    folded = jnp.abs((phase & (NFFT - 1)) - NFFT // 2) - NFFT // 4
    x = folded.astype(jnp.float32) * (2.0 * math.pi / NFFT)
    square = x * x
    total = jnp.full_like(x, SIN_COEFS[-1])
    for coef in SIN_COEFS[-2::-1]:
        total = total * square + coef
    return total * x


def spectra_kernel(offsets_ref, freq_ref, scales_ref, snap_ref, out_ref, coef_ref):
    snaps = snap_ref.shape[0]
    blocks = offsets_ref.shape[0]
    rows = 2 * blocks
    freqs = freq_ref.shape[0]
    row = lax.broadcasted_iota(jnp.int32, (rows, snaps), 0)
    time = lax.broadcasted_iota(jnp.int32, (rows, snaps), 1)
    start = jnp.zeros((rows, snaps), jnp.int32)
    for b in range(blocks):
        start = jnp.where(row // 2 == b, offsets_ref[b], start)
    shifted = time - start
    hann = 0.5 - 0.5 * cos_of_phase(shifted)
    inside = (shifted >= 0) & (shifted < NFFT)
    scales = jnp.broadcast_to(scales_ref[...], (rows, snaps))
    weight = jnp.where(inside, hann * scales * (1.0 / math.sqrt(NFFT)), 0.0)
    base = shifted[:, :NFFT].astype(jnp.float32)
    quarter = (row[:, :NFFT] % 2) * (NFFT // 4)
    repeats = -(-snaps // NFFT)

    def rows_of(f):
        freq = freq_ref[f].astype(jnp.float32)
        table = cos_of_phase((base * freq).astype(jnp.int32) + quarter)
        return jnp.concatenate([table] * repeats, 1)[:, :snaps] * weight

    for f in range(0, freqs, 2):
        pair = jnp.concatenate([rows_of(f), rows_of(f + 1)], 0)
        coef_ref[f * rows:(f + 2) * rows, :] = pair.astype(jnp.bfloat16)
    out_ref[...] = jnp.dot(
        coef_ref[...], snap_ref[...], preferred_element_type=jnp.float32
    ).astype(jnp.bfloat16)


def block_spectra(snapshots, row_scales, block_offsets, freq_index):
    snaps, points = snapshots.shape
    rows = 2 * block_offsets.shape[0] * freq_index.shape[0]
    return pl.pallas_call(
        spectra_kernel,
        out_shape=jax.ShapeDtypeStruct((rows, points), jnp.bfloat16),
        in_specs=[
            pl.BlockSpec(memory_space=pltpu.SMEM),
            pl.BlockSpec(memory_space=pltpu.SMEM),
            pl.BlockSpec(memory_space=pltpu.VMEM),
            pl.BlockSpec(memory_space=pltpu.VMEM),
        ],
        out_specs=pl.BlockSpec(memory_space=pltpu.VMEM),
        scratch_shapes=[pltpu.VMEM((rows, snaps), jnp.bfloat16)],
        compiler_params=pltpu.CompilerParams(vmem_limit_bytes=24 * 2**20),
        name="spectra",
    )(block_offsets, freq_index, row_scales.reshape(1, snaps), snapshots)


def rotated(x, lane):
    axis = x.ndim - 1
    width = x.shape[axis]
    after = pltpu.roll(x, width - 1, axis)
    before = pltpu.roll(x, 1, axis)
    return jnp.where(lane % 2 == 0, -after, before)


def gram_kernel(x_ref, out_ref, full_ref):
    x = x_ref[...]
    width = x.shape[0]
    full_ref[...] = lax.dot_general(
        x, x, (((1,), (1,)), ((), ())), preferred_element_type=jnp.float32
    )
    even = full_ref[pl.ds(0, width // 2, stride=2), :]
    odd = full_ref[pl.ds(1, width // 2, stride=2), :]
    lane = lax.broadcasted_iota(jnp.int32, odd.shape, 1)
    out_ref[...] = even - rotated(odd, lane)


def complex_gram(x):
    width = x.shape[0]
    return pl.pallas_call(
        gram_kernel,
        out_shape=jax.ShapeDtypeStruct((width // 2, width), jnp.float32),
        in_specs=[pl.BlockSpec(memory_space=pltpu.VMEM)],
        out_specs=pl.BlockSpec(memory_space=pltpu.VMEM),
        scratch_shapes=[pltpu.VMEM((width, width), jnp.float32)],
        name="gram",
    )(x)


def eliminate(rows, panel):
    count = len(rows)
    shape = rows[0].shape
    sub = lax.broadcasted_iota(jnp.int32, shape, 0)
    lane = lax.broadcasted_iota(jnp.int32, shape, 1)

    def over_lanes(x, at):
        return jnp.broadcast_to(x[:, at:at + 1], shape)

    def over_rows(x, at):
        return jnp.broadcast_to(x[at:at + 1, :], shape)

    rows = list(rows)
    pivots = [jnp.ones(shape, jnp.float32) for _ in range(count)]
    for first in range(0, count * SUB, panel):
        own = first // SUB
        live = range(own, count)
        re = [{i: over_lanes(rows[i], 2 * (first + c)) for i in live} for c in range(panel)]
        im = [{i: over_lanes(rows[i], 2 * (first + c) + 1) for i in live} for c in range(panel)]
        head, turned = rows[own], rotated(rows[own], lane)
        for c in range(panel):
            at = (first + c) % SUB
            k = first + c
            pivot = over_rows(re[c][own], at)
            pivots[own] = jnp.where(sub == at, pivot, pivots[own])
            inverse = 1.0 / pivot
            upper = {
                later: (over_rows(re[later][own], at), over_rows(im[later][own], at))
                for later in range(c + 1, panel)
            }
            for i in live:
                re[c][i] = re[c][i] * inverse
                im[c][i] = im[c][i] * inverse
                for later, (u_re, u_im) in upper.items():
                    re[later][i] = re[later][i] - (re[c][i] * u_re - im[c][i] * u_im)
                    im[later][i] = im[later][i] - (re[c][i] * u_im + im[c][i] * u_re)
            below = sub > at
            m_re = jnp.where(below, re[c][own], 0.0)
            m_im = jnp.where(below, im[c][own], 0.0)
            on_re, on_im = lane == 2 * k, lane == 2 * k + 1
            p = jnp.where(on_re, 1.0, jnp.where(on_im, 0.0, over_rows(head, at)))
            q = jnp.where(on_im, 1.0, jnp.where(on_re, 0.0, over_rows(turned, at)))
            cleared = below & (on_re | on_im)
            head = jnp.where(cleared, 0.0, head) - (m_re * p + m_im * q)
            turned = jnp.where(cleared, 0.0, turned) - (m_re * q - m_im * p)
        rows[own] = head
        if own + 1 == count:
            continue
        inside = (lane >= 2 * first) & (lane < 2 * (first + panel))
        rest = {i: jnp.where(inside, 0.0, rows[i]) for i in range(own + 1, count)}
        for c in range(panel):
            at = (first + c) % SUB
            k = first + c
            on_re, on_im = lane == 2 * k, lane == 2 * k + 1
            drop = (lane >= 2 * k) & (lane < 2 * (first + panel))
            p = jnp.where(on_re, 1.0, jnp.where(drop, 0.0, over_rows(head, at)))
            q = jnp.where(on_im, 1.0, jnp.where(drop, 0.0, over_rows(turned, at)))
            for i in rest:
                rest[i] = rest[i] - (re[c][i] * p + im[c][i] * q)
        for i in rest:
            rows[i] = rest[i]
    return rows, pivots


def modes_kernel(scale, x_ref, own_ref, other_ref, modes_ref, factor_ref, basis_ref, upper_ref):
    size = own_ref.shape[0]
    count = size // SUB
    rows = [
        (own_ref[i * SUB:(i + 1) * SUB, :] + other_ref[i * SUB:(i + 1) * SUB, :]) * scale
        for i in range(count)
    ]
    rows, pivots = eliminate(rows, PANEL)
    shape = rows[0].shape
    sub = lax.broadcasted_iota(jnp.int32, shape, 0)
    lane = lax.broadcasted_iota(jnp.int32, shape, 1)
    for i in range(count):
        root = lax.rsqrt(pivots[i])
        diagonal = 2 * (i * SUB + sub)
        right = jnp.where(lane > diagonal + 1, rows[i], jnp.where(lane == diagonal, pivots[i], 0.0))
        left = jnp.where(lane < diagonal, rows[i], jnp.where(lane == diagonal, 1.0, 0.0))
        upper_ref[i * SUB:(i + 1) * SUB, :] = right * root
        left = left * root
        basis_ref[pl.ds(2 * i * SUB, SUB, stride=2), :] = left
        basis_ref[pl.ds(2 * i * SUB + 1, SUB, stride=2), :] = rotated(left, lane)
    points = jnp.transpose(x_ref[...])
    basis = basis_ref[...]
    high = basis.astype(jnp.bfloat16)
    low = (basis - high.astype(jnp.float32)).astype(jnp.bfloat16)
    contract = (((1,), (1,)), ((), ()))
    modes_ref[...] = lax.dot_general(
        points, high, contract, preferred_element_type=jnp.float32
    ) + lax.dot_general(points, low, contract, preferred_element_type=jnp.float32)
    lane_in = lax.broadcasted_iota(jnp.int32, (2 * size, size), 0)
    lane_out = lax.broadcasted_iota(jnp.int32, (2 * size, size), 1)
    for part in range(2):
        pick = (lane_in == 2 * lane_out + part).astype(jnp.float32)
        factor_ref[part] = jnp.dot(
            upper_ref[...], pick,
            precision=lax.Precision.HIGHEST, preferred_element_type=jnp.float32,
        )


def modes_and_factor(x, own, other, scale):
    width, points = x.shape
    size = width // 2
    return pl.pallas_call(
        functools.partial(modes_kernel, scale),
        out_shape=(
            jax.ShapeDtypeStruct((points, width), jnp.float32),
            jax.ShapeDtypeStruct((2, size, size), jnp.float32),
        ),
        in_specs=[pl.BlockSpec(memory_space=pltpu.VMEM)] * 3,
        out_specs=(pl.BlockSpec(memory_space=pltpu.VMEM),) * 2,
        scratch_shapes=[
            pltpu.VMEM((width, width), jnp.float32),
            pltpu.VMEM((size, width), jnp.float32),
        ],
        compiler_params=pltpu.CompilerParams(vmem_limit_bytes=24 * 2**20),
        name="factor_and_modes",
    )(x, own, other)


def local(slabs, snapshots, row_scales, block_offsets, freq_index):
    freqs = freq_index.shape[0]
    points = snapshots.shape[1]
    spectra = block_spectra(snapshots, row_scales, block_offsets, freq_index)
    chunks = spectra.reshape(freqs, -1, points)
    regrouped = lax.all_to_all(chunks, "blk", split_axis=0, concat_axis=0, tiled=True)
    x = regrouped.reshape(-1, points)
    own = complex_gram(x)
    if slabs == 2:
        other = lax.ppermute(own, "space", [(0, 1), (1, 0)])
    else:
        own, other = lax.psum(own, "space"), jnp.zeros_like(own)
    modes, factor = modes_and_factor(x, own, other, 1.0 / (points * slabs))
    return modes[None], factor[None]


def solution(mesh):
    return jax.shard_map(
        functools.partial(local, mesh.shape["space"]),
        mesh=mesh,
        in_specs=(P("blk", "space"), P("blk"), P("blk"), P()),
        out_specs=(P("blk", "space", None), P("blk", None, None, None)),
        check_vma=False,
    )
```

time: 82.7 us -> 32.3 us (0.39)
  other arithmetic: 37.5 us -> 0 us
  local copies, waits for them, and re-layouts: 20.9 us -> 4.99 us
  Pallas kernels: 0 us -> 7.01 us
  blocking collectives: 20.2 us -> 15.2 us
  waiting for transfers between devices: 0 us -> 2.63 us
  matrix products: 2.53 us -> 0 us
  starting transfers between devices: 0 us -> 1.49 us
    another operation x9 -> x0, other arithmetic: 34.9 us -> none  [the longest x6 24.8 us: upper_of(): return jnp.swapaxes(jnp.linalg.cholesky(matrix), -1, -2)]
    gather x24 -> x0, local copies, waits for them, and re-layouts: 18.3 us -> none
    pallas_call x0 -> x3, Pallas kernels: none -> 7.01 us  [the longest x1 4.21 us: modes_and_factor(): pl.pallas_call(functools.partial(modes_kernel, scale), out_shape=(jax.Sha...]
    all_gather x1 -> x0, blocking collectives: 5.12 us -> none  [merged(): everything = lax.all_gather(value, axis)]
    unnamed x3 -> x10, local copies, waits for them, and re-layouts: 0.72 us -> 4.29 us
    ppermute x0 -> x1, waiting for transfers between devices: none -> 2.63 us  [local(): other = lax.ppermute(own, 'space', [(0, 1), (1, 0)])]
    dot_general x5 -> x0, matrix products: 2.28 us -> none  [the longest x1 1.02 us: local(): jnp.einsum('fpa,fba->fpb', regrouped.astype(jnp.float32), inverse_lower,...]
    ppermute x0 -> x1, starting transfers between devices: none -> 1.49 us  [local(): other = lax.ppermute(own, 'space', [(0, 1), (1, 0)])]
  transfers between devices with their start and end apart: 0 -> 1, of which waited for: 0 -> 1; matrix products, arithmetic and copies ran while one was open for 0% -> 0% of each run, Pallas kernels for 0% -> 0%
where the time goes in v1:
time: 32.3 us; the launch traced here: 32 us
  blocking collectives  15.2 us (47%)
  Pallas kernels  7.01 us (22%)
  local copies, waits for them, and re-layouts  4.99 us (15%)
  waiting for transfers between devices  2.63 us (8%)
  starting transfers between devices  1.49 us (5%)
  between operations  0.65 us (2%)
    all_to_all x1, blocking collectives, local(): lax.all_to_all(chunks, 'blk', split_axis=0, concat_axis=0, tiled=True)  15.2 us
    unnamed x10, local copies, waits for them, and re-layouts  4.29 us
    pallas_call x1, Pallas kernels, modes_and_factor(): pl.pallas_call(functools.partial(modes_kernel, scale), out_shape=(jax.Sha...  4.21 us
    ppermute x1, waiting for transfers between devices, local(): other = lax.ppermute(own, 'space', [(0, 1), (1, 0)])  2.63 us
    pallas_call x1, Pallas kernels, complex_gram(): pl.pallas_call(gram_kernel, out_shape=jax.ShapeDtypeStruct((width // 2, w...  1.79 us
    ppermute x1, starting transfers between devices, local(): other = lax.ppermute(own, 'space', [(0, 1), (1, 0)])  1.49 us
    pallas_call x1, Pallas kernels, block_spectra(): pl.pallas_call(spectra_kernel, out_shape=jax.ShapeDtypeStruct((rows, poin...  1.01 us
    reshape x1, local copies, waits for them, and re-layouts, block_spectra(): row_scales.reshape(1, snaps)  0.7 us
  transfers between devices with their start and end apart: 1, of which 1 were waited for; matrix products, arithmetic and copies ran while one was open for 0% of the time, Pallas kernels for 0%

profile of v1, /device:TPU:0, one launch (start us, length us, event | category | flops | bytes accessed | tf_op | source)
XLA Modules:
  0.0 32.0 jit_solution(9804633390713639995)
XLA Ops:
  0.6 0.7 %reshape.13.scales_ref = f32[1,1280]{1,0:T(1,128)S(1)} reshape(f32[1280]{0:T(1024)} %param.5) | data formatting | bytes 10240 | tf_op jit(solution)/shard_map/reshape | solution.py:81
  1.3 0.0 copy-start
  1.3 1.3 %copy-done = bf16[1280,512]{1,0:T(8,128)(2,1)S(1)} copy-done((bf16[1280,512]{1,0:T(8,128)(2,1)S(1)}, bf16[1280,512]{1,0:T(8,128)(2,1)}, u32[]{:S(2)}) %copy-start) | copy-done | bytes 1310744
  2.6 0.0 copy-start.3
  2.7 0.7 %copy-done.3 = s32[4]{0:T(128)S(1)} copy-done((s32[4]{0:T(128)S(1)}, s32[4]{0:T(128)}, u32[]{:S(2)}) %copy-start.3) | copy-done | bytes 40
  3.3 0.0 copy-start.4
  3.3 0.7 %copy-done.4 = s32[16]{0:T(128)S(1)} copy-done((s32[16]{0:T(128)S(1)}, s32[16]{0:T(128)}, u32[]{:S(2)}) %copy-start.4) | copy-done | bytes 88
  4.0 1.0 %spectra.1 = bf16[128,512]{1,0:T(8,128)(2,1)S(1)} custom-call(s32[4]{0:T(128)S(1)} %copy-done.3, s32[16]{0:T(128)S(1)} %copy-done.4, f32[1,1280]{1,0:T(1,128)S(1)} %reshape.13.scales_ref, bf16[1280,512]{1,0:T(8,128)(2,1)S(1)} %copy-done), custom_call_target="tpu_custom_call" | custom-call | tf_op jit(solution)/shard_map/spectra/pallas_call | solution.py:68
  5.0 15.2 %all_to_all.5 = bf16[16,8,512]{2,1,0:T(8,128)(2,1)} all-to-all(bf16[16,8,512]{2,1,0:T(8,128)(2,1)S(1)} %bitcast.6), channel_id=1, replica_groups=mesh['space'=2,'blk'=16] {'blk'}, dimensions={0} | all-to-all | bytes 262144 | tf_op jit(solution)/shard_map/all_to_all | solution.py:243
  20.2 1.8 %gram.1.own_ref = f32[64,128]{1,0:T(8,128)} custom-call(bf16[128,512]{1,0:T(8,128)(2,1)} %bitcast.4), custom_call_target="tpu_custom_call" | custom-call | tf_op jit(solution)/shard_map/gram/pallas_call | solution.py:106
  22.0 1.5 %collective-permute-start = (f32[64,128]{1,0:T(8,128)}, f32[64,128]{1,0:T(8,128)S(1)}, u32[]{:S(2)}, u32[]{:S(2)}) collective-permute-start(f32[64,128]{1,0:T(8,128)} %gram.1.own_ref), channel_id=1, source_target_pairs={{0,16},{16,0},{1,17},{17,1},{2,18},{18,2},{3,19},{19,3},{4,20},{20... | collective-permute-start | bytes 98312 | tf_op jit(solution)/shard_map/ppermute | solution.py:247
  23.5 2.6 %collective-permute-done.other_ref = f32[64,128]{1,0:T(8,128)S(1)} collective-permute-done((f32[64,128]{1,0:T(8,128)}, f32[64,128]{1,0:T(8,128)S(1)}, u32[]{:S(2)}, u32[]{:S(2)}) %collective-permute-start) | collective-permute-done | bytes 32800 | tf_op jit(solution)/shard_map/ppermute | solution.py:247
  26.1 0.0 copy-start.1
  26.1 0.9 %copy-done.1 = bf16[16,8,512]{2,1,0:T(8,128)(2,1)S(1)} copy-done((bf16[16,8,512]{2,1,0:T(8,128)(2,1)S(1)}, bf16[16,8,512]{2,1,0:T(8,128)(2,1)}, u32[]{:S(2)}) %copy-start.1) | copy-done | bytes 131096
  27.0 0.0 copy-start.2
  27.0 0.8 %copy-done.2 = f32[64,128]{1,0:T(8,128)S(1)} copy-done((f32[64,128]{1,0:T(8,128)S(1)}, f32[64,128]{1,0:T(8,128)}, u32[]{:S(2)}) %copy-start.2) | copy-done | bytes 32792
  27.8 4.2 %factor_and_modes.1 = (f32[512,128]{1,0:T(8,128)}, f32[2,64,64]{2,1,0:T(8,128)}) custom-call(bf16[128,512]{1,0:T(8,128)(2,1)S(1)} %bitcast.5, f32[64,128]{1,0:T(8,128)S(1)} %copy-done.2, f32[64,128]{1,0:T(8,128)S(1)} %collective-permute-done.other_ref), custom_call_target="tpu_custom_call" | custom-call | tf_op jit(solution)/shard_map/factor_and_modes/pallas_call | solution.py:221
Async XLA Ops:
  1.3 1.3 %copy-start = (bf16[1280,512]{1,0:T(8,128)(2,1)S(1)}, bf16[1280,512]{1,0:T(8,128)(2,1)}, u32[]{:S(2)}) copy-start(bf16[1280,512]{1,0:T(8,128)(2,1)} %snap_ref.1) | copy-start | bytes 3932164
  2.6 0.7 %copy-start.3 = (s32[4]{0:T(128)S(1)}, s32[4]{0:T(128)}, u32[]{:S(2)}) copy-start(s32[4]{0:T(128)} %offsets_ref.1) | copy-start | bytes 52
  3.3 0.7 %copy-start.4 = (s32[16]{0:T(128)S(1)}, s32[16]{0:T(128)}, u32[]{:S(2)}) copy-start(s32[16]{0:T(128)} %freq_ref.1) | copy-start | bytes 196
  22.0 4.1 %collective-permute-start = (f32[64,128]{1,0:T(8,128)}, f32[64,128]{1,0:T(8,128)S(1)}, u32[]{:S(2)}, u32[]{:S(2)}) collective-permute-start(f32[64,128]{1,0:T(8,128)} %gram.1.own_ref), channel_id=1, source_target_pairs={{0,16},{16,0},{1,17},{17,1},{2,18},{18,2},{3,19},{19,3},{4,20},{20... | collective-permute-start | bytes 98312 | tf_op jit(solution)/shard_map/ppermute | solution.py:247
  26.1 0.9 %copy-start.1 = (bf16[16,8,512]{2,1,0:T(8,128)(2,1)S(1)}, bf16[16,8,512]{2,1,0:T(8,128)(2,1)}, u32[]{:S(2)}) copy-start(bf16[16,8,512]{2,1,0:T(8,128)(2,1)} %all_to_all.5) | copy-start | bytes 393220
  27.0 0.8 %copy-start.2 = (f32[64,128]{1,0:T(8,128)S(1)}, f32[64,128]{1,0:T(8,128)}, u32[]{:S(2)}) copy-start(f32[64,128]{1,0:T(8,128)} %gram.1.own_ref) | copy-start | bytes 98308

commit v2 on v1

--- a/solution.py
+++ b/solution.py
@@ -11,6 +11,7 @@
 NFFT = 512
 PANEL = 4
 SUB = 8
+PIECE = 256
 SIN_COEFS = (
     0.9999999765895043,
     -0.1666664763439475,
@@ -30,20 +31,38 @@
     return total * x
 
 
-def spectra_kernel(offsets_ref, freq_ref, scales_ref, snap_ref, out_ref, coef_ref):
+def spectra_kernel(
+    snap_hbm, scales_hbm, offsets_hbm, freq_hbm, out_ref,
+    snap_ref, scales_ref, offsets_ref, freq_ref, coef_ref, small_sems, snap_sems,
+):
     snaps = snap_ref.shape[0]
     blocks = offsets_ref.shape[0]
     rows = 2 * blocks
     freqs = freq_ref.shape[0]
+    small = [
+        pltpu.make_async_copy(src, dst, small_sems.at[i])
+        for i, (src, dst) in enumerate(
+            ((offsets_hbm, offsets_ref), (freq_hbm, freq_ref), (scales_hbm, scales_ref))
+        )
+    ]
+    pieces = [slice(at, min(at + PIECE, snaps)) for at in range(0, snaps, PIECE)]
+    large = [
+        pltpu.make_async_copy(snap_hbm.at[piece], snap_ref.at[piece], snap_sems.at[i])
+        for i, piece in enumerate(pieces)
+    ]
+    for copy in small + large:
+        copy.start()
     row = lax.broadcasted_iota(jnp.int32, (rows, snaps), 0)
     time = lax.broadcasted_iota(jnp.int32, (rows, snaps), 1)
+    for copy in small:
+        copy.wait()
     start = jnp.zeros((rows, snaps), jnp.int32)
     for b in range(blocks):
         start = jnp.where(row // 2 == b, offsets_ref[b], start)
     shifted = time - start
     hann = 0.5 - 0.5 * cos_of_phase(shifted)
     inside = (shifted >= 0) & (shifted < NFFT)
-    scales = jnp.broadcast_to(scales_ref[...], (rows, snaps))
+    scales = jnp.broadcast_to(scales_ref[...].reshape(1, snaps), (rows, snaps))
     weight = jnp.where(inside, hann * scales * (1.0 / math.sqrt(NFFT)), 0.0)
     base = shifted[:, :NFFT].astype(jnp.float32)
     quarter = (row[:, :NFFT] % 2) * (NFFT // 4)
@@ -57,28 +76,36 @@
     for f in range(0, freqs, 2):
         pair = jnp.concatenate([rows_of(f), rows_of(f + 1)], 0)
         coef_ref[f * rows:(f + 2) * rows, :] = pair.astype(jnp.bfloat16)
-    out_ref[...] = jnp.dot(
-        coef_ref[...], snap_ref[...], preferred_element_type=jnp.float32
-    ).astype(jnp.bfloat16)
+    total = jnp.zeros(out_ref.shape, jnp.float32)
+    for copy, piece in zip(large, pieces):
+        copy.wait()
+        total += jnp.dot(
+            coef_ref[:, piece], snap_ref[piece], preferred_element_type=jnp.float32
+        )
+    out_ref[...] = total.astype(jnp.bfloat16)
 
 
 def block_spectra(snapshots, row_scales, block_offsets, freq_index):
     snaps, points = snapshots.shape
     rows = 2 * block_offsets.shape[0] * freq_index.shape[0]
+    pieces = -(-snaps // PIECE)
     return pl.pallas_call(
         spectra_kernel,
         out_shape=jax.ShapeDtypeStruct((rows, points), jnp.bfloat16),
-        in_specs=[
-            pl.BlockSpec(memory_space=pltpu.SMEM),
-            pl.BlockSpec(memory_space=pltpu.SMEM),
-            pl.BlockSpec(memory_space=pltpu.VMEM),
-            pl.BlockSpec(memory_space=pltpu.VMEM),
+        in_specs=[pl.BlockSpec(memory_space=pltpu.HBM)] * 4,
+        out_specs=pl.BlockSpec(memory_space=pltpu.VMEM),
+        scratch_shapes=[
+            pltpu.VMEM((snaps, points), jnp.bfloat16),
+            pltpu.VMEM((snaps,), jnp.float32),
+            pltpu.SMEM(block_offsets.shape, jnp.int32),
+            pltpu.SMEM(freq_index.shape, jnp.int32),
+            pltpu.VMEM((rows, snaps), jnp.bfloat16),
+            pltpu.SemaphoreType.DMA((3,)),
+            pltpu.SemaphoreType.DMA((pieces,)),
         ],
-        out_specs=pl.BlockSpec(memory_space=pltpu.VMEM),
-        scratch_shapes=[pltpu.VMEM((rows, snaps), jnp.bfloat16)],
-        compiler_params=pltpu.CompilerParams(vmem_limit_bytes=24 * 2**20),
+        compiler_params=pltpu.CompilerParams(vmem_limit_bytes=60 * 2**20),
         name="spectra",
-    )(block_offsets, freq_index, row_scales.reshape(1, snaps), snapshots)
+    )(snapshots, row_scales, block_offsets, freq_index)
 
 
 def rotated(x, lane):
@@ -109,6 +136,7 @@
         in_specs=[pl.BlockSpec(memory_space=pltpu.VMEM)],
         out_specs=pl.BlockSpec(memory_space=pltpu.VMEM),
         scratch_shapes=[pltpu.VMEM((width, width), jnp.float32)],
+        compiler_params=pltpu.CompilerParams(vmem_limit_bytes=4 * 2**20),
         name="gram",
     )(x)
 
@@ -230,7 +258,7 @@
             pltpu.VMEM((width, width), jnp.float32),
             pltpu.VMEM((size, width), jnp.float32),
         ],
-        compiler_params=pltpu.CompilerParams(vmem_limit_bytes=24 * 2**20),
+        compiler_params=pltpu.CompilerParams(vmem_limit_bytes=8 * 2**20),
         name="factor_and_modes",
     )(x, own, other)
 

time: 32.3 us -> 27.1 us (0.84)
  local copies, waits for them, and re-layouts: 4.99 us -> 0 us
    unnamed x10 -> x0, local copies, waits for them, and re-layouts: 4.29 us -> none
    pallas_call x1, Pallas kernels: 1.79 us -> 0.26 us  [complex_gram(): pl.pallas_call(gram_kernel, out_shape=jax.ShapeDtypeStruct((width // 2, w...]
    pallas_call x1, Pallas kernels: 1.01 us -> 2.48 us  [block_spectra(): pl.pallas_call(spectra_kernel, out_shape=jax.ShapeDtypeStruct((rows, poin...]
    reshape x1 -> x0, local copies, waits for them, and re-layouts: 0.7 us -> none  [block_spectra(): row_scales.reshape(1, snaps)]
where the time goes in v2:
time: 27.1 us; the launch traced here: 26.9 us
  blocking collectives  15.3 us (56%)
  Pallas kernels  6.95 us (26%)
  waiting for transfers between devices  2.42 us (9%)
  starting transfers between devices  1.55 us (6%)
  between operations  0.65 us (2%)
    all_to_all x1, blocking collectives, local(): lax.all_to_all(chunks, 'blk', split_axis=0, concat_axis=0, tiled=True)  15.3 us
    pallas_call x1, Pallas kernels, modes_and_factor(): pl.pallas_call(functools.partial(modes_kernel, scale), out_shape=(jax.Sha...  4.21 us
    pallas_call x1, Pallas kernels, block_spectra(): pl.pallas_call(spectra_kernel, out_shape=jax.ShapeDtypeStruct((rows, poin...  2.48 us
    ppermute x1, waiting for transfers between devices, local(): other = lax.ppermute(own, 'space', [(0, 1), (1, 0)])  2.42 us
    ppermute x1, starting transfers between devices, local(): other = lax.ppermute(own, 'space', [(0, 1), (1, 0)])  1.55 us
  transfers between devices with their start and end apart: 1, of which 1 were waited for; matrix products, arithmetic and copies ran while one was open for 0% of the time, Pallas kernels for 0%

profile of v2, /device:TPU:0, one launch (start us, length us, event | category | flops | bytes accessed | tf_op | source)
XLA Modules:
  0.0 26.9 jit_solution(9849364486295966367)
XLA Ops:
  0.6 2.5 %spectra.1 = bf16[128,512]{1,0:T(8,128)(2,1)} custom-call(bf16[1280,512]{1,0:T(8,128)(2,1)} %snap_hbm.1, f32[1280]{0:T(1024)} %scales_hbm.1, s32[4]{0:T(128)} %offsets_hbm.1, s32[16]{0:T(128)} %freq_hbm.1), custom_call_target="tpu_custom_call" | custom-call | tf_op jit(solution)/shard_map/spectra/pallas_call | solution.py:92
  3.1 15.3 %all_to_all.5 = bf16[16,8,512]{2,1,0:T(8,128)(2,1)S(1)} all-to-all(bf16[16,8,512]{2,1,0:T(8,128)(2,1)} %bitcast.6), channel_id=1, replica_groups=mesh['space'=2,'blk'=16] {'blk'}, dimensions={0} | all-to-all | bytes 262144 | tf_op jit(solution)/shard_map/all_to_all | solution.py:271
  18.5 0.3 gram.1.own_ref
  18.7 1.6 %collective-permute-start = (f32[64,128]{1,0:T(8,128)S(1)}, f32[64,128]{1,0:T(8,128)S(1)}, u32[]{:S(2)}, u32[]{:S(2)}) collective-permute-start(f32[64,128]{1,0:T(8,128)S(1)} %gram.1.own_ref), channel_id=1, source_target_pairs={{0,16},{16,0},{1,17},{17,1},{2,18},{18,2},{3,19},{19,3},{4,20},{20... | collective-permute-start | bytes 98312 | tf_op jit(solution)/shard_map/ppermute | solution.py:275
  20.3 2.4 %collective-permute-done.other_ref = f32[64,128]{1,0:T(8,128)S(1)} collective-permute-done((f32[64,128]{1,0:T(8,128)S(1)}, f32[64,128]{1,0:T(8,128)S(1)}, u32[]{:S(2)}, u32[]{:S(2)}) %collective-permute-start) | collective-permute-done | bytes 32800 | tf_op jit(solution)/shard_map/ppermute | solution.py:275
  22.7 4.2 %factor_and_modes.1 = (f32[512,128]{1,0:T(8,128)}, f32[2,64,64]{2,1,0:T(8,128)}) custom-call(bf16[128,512]{1,0:T(8,128)(2,1)S(1)} %bitcast.5, f32[64,128]{1,0:T(8,128)S(1)} %gram.1.own_ref, f32[64,128]{1,0:T(8,128)S(1)} %collective-permute-done.other_ref), custom_call_target="tpu_custom_call" | custom-call | tf_op jit(solution)/shard_map/factor_and_modes/pallas_call | solution.py:249
Async XLA Ops:
  18.7 4.0 %collective-permute-start = (f32[64,128]{1,0:T(8,128)S(1)}, f32[64,128]{1,0:T(8,128)S(1)}, u32[]{:S(2)}, u32[]{:S(2)}) collective-permute-start(f32[64,128]{1,0:T(8,128)S(1)} %gram.1.own_ref), channel_id=1, source_target_pairs={{0,16},{16,0},{1,17},{17,1},{2,18},{18,2},{3,19},{19,3},{4,20},{20... | collective-permute-start | bytes 98312 | tf_op jit(solution)/shard_map/ppermute | solution.py:275

commit v3 on v2

--- a/solution.py
+++ b/solution.py
@@ -12,6 +12,7 @@
 PANEL = 4
 SUB = 8
 PIECE = 256
+INNER = 4
 SIN_COEFS = (
     0.9999999765895043,
     -0.1666664763439475,
@@ -32,7 +33,7 @@
 
 
 def spectra_kernel(
-    snap_hbm, scales_hbm, offsets_hbm, freq_hbm, out_ref,
+    outer, inner, snap_hbm, scales_hbm, offsets_hbm, freq_hbm, out_ref,
     snap_ref, scales_ref, offsets_ref, freq_ref, coef_ref, small_sems, snap_sems,
 ):
     snaps = snap_ref.shape[0]
@@ -68,7 +69,8 @@
     quarter = (row[:, :NFFT] % 2) * (NFFT // 4)
     repeats = -(-snaps // NFFT)
 
-    def rows_of(f):
+    def rows_of(g):
+        f = g % outer * inner + g // outer
         freq = freq_ref[f].astype(jnp.float32)
         table = cos_of_phase((base * freq).astype(jnp.int32) + quarter)
         return jnp.concatenate([table] * repeats, 1)[:, :snaps] * weight
@@ -85,12 +87,12 @@
     out_ref[...] = total.astype(jnp.bfloat16)
 
 
-def block_spectra(snapshots, row_scales, block_offsets, freq_index):
+def block_spectra(snapshots, row_scales, block_offsets, freq_index, outer, inner):
     snaps, points = snapshots.shape
     rows = 2 * block_offsets.shape[0] * freq_index.shape[0]
     pieces = -(-snaps // PIECE)
     return pl.pallas_call(
-        spectra_kernel,
+        functools.partial(spectra_kernel, outer, inner),
         out_shape=jax.ShapeDtypeStruct((rows, points), jnp.bfloat16),
         in_specs=[pl.BlockSpec(memory_space=pltpu.HBM)] * 4,
         out_specs=pl.BlockSpec(memory_space=pltpu.VMEM),
@@ -263,12 +265,18 @@
     )(x, own, other)
 
 
-def local(slabs, snapshots, row_scales, block_offsets, freq_index):
+def local(slabs, owners, snapshots, row_scales, block_offsets, freq_index):
     freqs = freq_index.shape[0]
     points = snapshots.shape[1]
-    spectra = block_spectra(snapshots, row_scales, block_offsets, freq_index)
-    chunks = spectra.reshape(freqs, -1, points)
-    regrouped = lax.all_to_all(chunks, "blk", split_axis=0, concat_axis=0, tiled=True)
+    inner = math.gcd(owners, INNER)
+    outer = owners // inner
+    spectra = block_spectra(snapshots, row_scales, block_offsets, freq_index, outer, inner)
+    chunks = spectra.reshape(inner, outer, -1, points)
+    near = [[o * inner + i for i in range(inner)] for o in range(outer)]
+    far = [[o * inner + i for o in range(outer)] for i in range(inner)]
+    swap = functools.partial(lax.all_to_all, axis_name="blk", split_axis=0, concat_axis=0, tiled=True)
+    chunks = swap(chunks, axis_index_groups=near).transpose(1, 0, 2, 3)
+    regrouped = swap(chunks, axis_index_groups=far)
     x = regrouped.reshape(-1, points)
     own = complex_gram(x)
     if slabs == 2:
@@ -281,7 +289,7 @@
 
 def solution(mesh):
     return jax.shard_map(
-        functools.partial(local, mesh.shape["space"]),
+        functools.partial(local, mesh.shape["space"], mesh.shape["blk"]),
         mesh=mesh,
         in_specs=(P("blk", "space"), P("blk"), P("blk"), P()),
         out_specs=(P("blk", "space", None), P("blk", None, None, None)),

time: 27.1 us -> 31.8 us (1.17)
  blocking collectives: 15.3 us -> 20 us
    all_to_all x1 -> x2, blocking collectives: 15.3 us -> 20 us  [the longest x1 11.1 us: local(): regrouped = swap(chunks, axis_index_groups=far)]
where the time goes in v3:
time: 31.8 us; the launch traced here: 31.6 us
  blocking collectives  20 us (63%)
  Pallas kernels  6.95 us (22%)
  waiting for transfers between devices  2.42 us (8%)
  starting transfers between devices  1.55 us (5%)
  between operations  0.65 us (2%)
    all_to_all x1, blocking collectives, local(): regrouped = swap(chunks, axis_index_groups=far)  11.1 us
    all_to_all x1, blocking collectives, local(): chunks = swap(chunks, axis_index_groups=near).transpose(1, 0, 2, 3)  8.88 us
    pallas_call x1, Pallas kernels, modes_and_factor(): pl.pallas_call(functools.partial(modes_kernel, scale), out_shape=(jax.Sha...  4.21 us
    pallas_call x1, Pallas kernels, block_spectra(): pl.pallas_call(functools.partial(spectra_kernel, outer, inner), out_shape...  2.48 us
    ppermute x1, waiting for transfers between devices, local(): other = lax.ppermute(own, 'space', [(0, 1), (1, 0)])  2.42 us
    ppermute x1, starting transfers between devices, local(): other = lax.ppermute(own, 'space', [(0, 1), (1, 0)])  1.55 us
  transfers between devices with their start and end apart: 1, of which 1 were waited for; matrix products, arithmetic and copies ran while one was open for 0% of the time, Pallas kernels for 0%

profile of v3, /device:TPU:0, one launch (start us, length us, event | category | flops | bytes accessed | tf_op | source)
XLA Modules:
  0.0 31.6 jit_solution(13874054963591219130)
XLA Ops:
  0.6 2.5 %spectra.1 = bf16[128,512]{1,0:T(8,128)(2,1)} custom-call(bf16[1280,512]{1,0:T(8,128)(2,1)} %snap_hbm.1, f32[1280]{0:T(1024)} %scales_hbm.1, s32[4]{0:T(128)} %offsets_hbm.1, s32[16]{0:T(128)} %freq_hbm.1), custom_call_target="tpu_custom_call" | custom-call | tf_op jit(solution)/shard_map/spectra/pallas_call | solution.py:94
  3.1 8.9 %all_to_all.10 = bf16[4,4,8,512]{3,2,1,0:T(8,128)(2,1)S(1)} all-to-all(bf16[4,4,8,512]{3,2,1,0:T(8,128)(2,1)} %bitcast.7), channel_id=1, replica_groups={{0,1,2,3},{4,5,6,7},{8,9,10,11},{12,13,14,15},{16,17,18,19},{20,21,22,2..., dimensions={0} | all-to-all | bytes 262144 | tf_op jit(solution)/shard_map/all_to_all | solution.py:278
  12.0 11.1 %all_to_all.11 = bf16[4,4,8,512]{3,2,1,0:T(8,128)(2,1)S(1)} all-to-all(bf16[4,4,8,512]{3,2,1,0:T(8,128)(2,1)S(1)} %copy.8), channel_id=1, replica_groups={{0,4,8,12},{1,5,9,13},{2,6,10,14},{3,7,11,15},{16,20,24,28},{17,21,25,2..., dimensions={0} | all-to-all | bytes 262144 | tf_op jit(solution)/shard_map/all_to_all | solution.py:279
  23.1 0.3 gram.1.own_ref
  23.4 1.6 %collective-permute-start = (f32[64,128]{1,0:T(8,128)S(1)}, f32[64,128]{1,0:T(8,128)S(1)}, u32[]{:S(2)}, u32[]{:S(2)}) collective-permute-start(f32[64,128]{1,0:T(8,128)S(1)} %gram.1.own_ref), channel_id=1, source_target_pairs={{0,16},{16,0},{1,17},{17,1},{2,18},{18,2},{3,19},{19,3},{4,20},{20... | collective-permute-start | bytes 98312 | tf_op jit(solution)/shard_map/ppermute | solution.py:283
  24.9 2.4 %collective-permute-done.other_ref = f32[64,128]{1,0:T(8,128)S(1)} collective-permute-done((f32[64,128]{1,0:T(8,128)S(1)}, f32[64,128]{1,0:T(8,128)S(1)}, u32[]{:S(2)}, u32[]{:S(2)}) %collective-permute-start) | collective-permute-done | bytes 32800 | tf_op jit(solution)/shard_map/ppermute | solution.py:283
  27.4 4.2 %factor_and_modes.1 = (f32[512,128]{1,0:T(8,128)}, f32[2,64,64]{2,1,0:T(8,128)}) custom-call(bf16[128,512]{1,0:T(8,128)(2,1)S(1)} %bitcast.6, f32[64,128]{1,0:T(8,128)S(1)} %gram.1.own_ref, f32[64,128]{1,0:T(8,128)S(1)} %collective-permute-done.other_ref), custom_call_target="tpu_custom_call" | custom-call | tf_op jit(solution)/shard_map/factor_and_modes/pallas_call | solution.py:251
  (1 shorter events, 0.0 us)
Async XLA Ops:
  23.4 4.0 %collective-permute-start = (f32[64,128]{1,0:T(8,128)S(1)}, f32[64,128]{1,0:T(8,128)S(1)}, u32[]{:S(2)}, u32[]{:S(2)}) collective-permute-start(f32[64,128]{1,0:T(8,128)S(1)} %gram.1.own_ref), channel_id=1, source_target_pairs={{0,16},{16,0},{1,17},{17,1},{2,18},{18,2},{3,19},{19,3},{4,20},{20... | collective-permute-start | bytes 98312 | tf_op jit(solution)/shard_map/ppermute | solution.py:283

commit v4 on v2

--- a/solution.py
+++ b/solution.py
@@ -12,6 +12,7 @@
 PANEL = 4
 SUB = 8
 PIECE = 256
+FEW_SLABS = 2
 SIN_COEFS = (
     0.9999999765895043,
     -0.1666664763439475,
@@ -76,22 +77,24 @@
     for f in range(0, freqs, 2):
         pair = jnp.concatenate([rows_of(f), rows_of(f + 1)], 0)
         coef_ref[f * rows:(f + 2) * rows, :] = pair.astype(jnp.bfloat16)
-    total = jnp.zeros(out_ref.shape, jnp.float32)
+    total = jnp.zeros(out_ref.shape[1:], jnp.float32)
     for copy, piece in zip(large, pieces):
         copy.wait()
         total += jnp.dot(
             coef_ref[:, piece], snap_ref[piece], preferred_element_type=jnp.float32
         )
-    out_ref[...] = total.astype(jnp.bfloat16)
-
-
-def block_spectra(snapshots, row_scales, block_offsets, freq_index):
+    result = total.astype(jnp.bfloat16)
+    for copy in range(out_ref.shape[0]):
+        out_ref[copy] = result
+
+
+def block_spectra(copies, snapshots, row_scales, block_offsets, freq_index):
     snaps, points = snapshots.shape
     rows = 2 * block_offsets.shape[0] * freq_index.shape[0]
     pieces = -(-snaps // PIECE)
     return pl.pallas_call(
         spectra_kernel,
-        out_shape=jax.ShapeDtypeStruct((rows, points), jnp.bfloat16),
+        out_shape=jax.ShapeDtypeStruct((copies, rows, points), jnp.bfloat16),
         in_specs=[pl.BlockSpec(memory_space=pltpu.HBM)] * 4,
         out_specs=pl.BlockSpec(memory_space=pltpu.VMEM),
         scratch_shapes=[
@@ -116,16 +119,20 @@
     return jnp.where(lane % 2 == 0, -after, before)
 
 
-def gram_kernel(x_ref, out_ref, full_ref):
-    x = x_ref[...]
-    width = x.shape[0]
-    full_ref[...] = lax.dot_general(
-        x, x, (((1,), (1,)), ((), ())), preferred_element_type=jnp.float32
+def gram_rows(slabs, full_ref):
+    width = full_ref.shape[0]
+    full_ref[...] = sum(
+        lax.dot_general(x, x, (((1,), (1,)), ((), ())), preferred_element_type=jnp.float32)
+        for x in slabs
     )
     even = full_ref[pl.ds(0, width // 2, stride=2), :]
     odd = full_ref[pl.ds(1, width // 2, stride=2), :]
     lane = lax.broadcasted_iota(jnp.int32, odd.shape, 1)
-    out_ref[...] = even - rotated(odd, lane)
+    return even - rotated(odd, lane)
+
+
+def gram_kernel(x_ref, out_ref, full_ref):
+    out_ref[...] = gram_rows([x_ref[...]], full_ref)
 
 
 def complex_gram(x):
@@ -205,14 +212,20 @@
     return rows, pivots
 
 
-def modes_kernel(scale, x_ref, own_ref, other_ref, modes_ref, factor_ref, basis_ref, upper_ref):
-    size = own_ref.shape[0]
+def modes_kernel(scale, slabs, x_ref, *refs):
+    *given, modes_ref, factor_ref, basis_ref, upper_ref = refs
+    width = basis_ref.shape[0]
+    size = width // 2
     count = size // SUB
-    rows = [
-        (own_ref[i * SUB:(i + 1) * SUB, :] + other_ref[i * SUB:(i + 1) * SUB, :]) * scale
-        for i in range(count)
-    ]
-    rows, pivots = eliminate(rows, PANEL)
+    if given:
+        gram = given[0][...]
+        mine = x_ref[...]
+    else:
+        gram = gram_rows([x_ref[i * width:(i + 1) * width] for i in range(slabs)], basis_ref)
+        own = lax.axis_index("space")
+        mine = x_ref[pl.ds(pl.multiple_of(own * width, width), width)]
+    gram = gram * scale
+    rows, pivots = eliminate([gram[i * SUB:(i + 1) * SUB] for i in range(count)], PANEL)
     shape = rows[0].shape
     sub = lax.broadcasted_iota(jnp.int32, shape, 0)
     lane = lax.broadcasted_iota(jnp.int32, shape, 1)
@@ -225,7 +238,7 @@
         left = left * root
         basis_ref[pl.ds(2 * i * SUB, SUB, stride=2), :] = left
         basis_ref[pl.ds(2 * i * SUB + 1, SUB, stride=2), :] = rotated(left, lane)
-    points = jnp.transpose(x_ref[...])
+    points = jnp.transpose(mine)
     basis = basis_ref[...]
     high = basis.astype(jnp.bfloat16)
     low = (basis - high.astype(jnp.float32)).astype(jnp.bfloat16)
@@ -243,16 +256,16 @@
         )
 
 
-def modes_and_factor(x, own, other, scale):
-    width, points = x.shape
+def modes_and_factor(x, grams, width, slabs, scale):
+    points = x.shape[1]
     size = width // 2
     return pl.pallas_call(
-        functools.partial(modes_kernel, scale),
+        functools.partial(modes_kernel, scale, slabs),
         out_shape=(
             jax.ShapeDtypeStruct((points, width), jnp.float32),
             jax.ShapeDtypeStruct((2, size, size), jnp.float32),
         ),
-        in_specs=[pl.BlockSpec(memory_space=pltpu.VMEM)] * 3,
+        in_specs=[pl.BlockSpec(memory_space=pltpu.VMEM)] * (1 + len(grams)),
         out_specs=(pl.BlockSpec(memory_space=pltpu.VMEM),) * 2,
         scratch_shapes=[
             pltpu.VMEM((width, width), jnp.float32),
@@ -260,22 +273,24 @@
         ],
         compiler_params=pltpu.CompilerParams(vmem_limit_bytes=8 * 2**20),
         name="factor_and_modes",
-    )(x, own, other)
+    )(x, *grams)
 
 
 def local(slabs, snapshots, row_scales, block_offsets, freq_index):
     freqs = freq_index.shape[0]
     points = snapshots.shape[1]
-    spectra = block_spectra(snapshots, row_scales, block_offsets, freq_index)
-    chunks = spectra.reshape(freqs, -1, points)
-    regrouped = lax.all_to_all(chunks, "blk", split_axis=0, concat_axis=0, tiled=True)
-    x = regrouped.reshape(-1, points)
-    own = complex_gram(x)
-    if slabs == 2:
-        other = lax.ppermute(own, "space", [(0, 1), (1, 0)])
+    width = 2 * block_offsets.shape[0] * lax.axis_size("blk")
+    copies = slabs if slabs <= FEW_SLABS else 1
+    spectra = block_spectra(copies, snapshots, row_scales, block_offsets, freq_index)
+    chunks = spectra.reshape(copies * freqs, -1, points)
+    swap = functools.partial(lax.all_to_all, split_axis=0, concat_axis=0, tiled=True)
+    if copies == slabs:
+        x = swap(chunks, ("space", "blk")).reshape(-1, points)
+        grams = []
     else:
-        own, other = lax.psum(own, "space"), jnp.zeros_like(own)
-    modes, factor = modes_and_factor(x, own, other, 1.0 / (points * slabs))
+        x = swap(chunks, "blk").reshape(-1, points)
+        grams = [lax.psum(complex_gram(x), "space")]
+    modes, factor = modes_and_factor(x, grams, width, slabs, 1.0 / (points * slabs))
     return modes[None], factor[None]
 
 

time: 27.1 us -> 25.5 us (0.941)
  waiting for transfers between devices: 2.42 us -> 0 us
  blocking collectives: 15.3 us -> 17.6 us
  starting transfers between devices: 1.55 us -> 0 us
    ppermute x1 -> x0, waiting for transfers between devices: 2.42 us -> none  [local(): other = lax.ppermute(own, 'space', [(0, 1), (1, 0)])]
    all_to_all x1, blocking collectives: 15.3 us -> 17.6 us  [local(): x = swap(chunks, ('space', 'blk')).reshape(-1, points)]
    ppermute x1 -> x0, starting transfers between devices: 1.55 us -> none  [local(): other = lax.ppermute(own, 'space', [(0, 1), (1, 0)])]
    pallas_call x3 -> x2, Pallas kernels: 6.95 us -> 7.08 us  [the longest x1 4.55 us: modes_and_factor(): pl.pallas_call(functools.partial(modes_kernel, scale, slabs), out_shape=(...]
  transfers between devices with their start and end apart: 1 -> 0, of which waited for: 1 -> 0; matrix products, arithmetic and copies ran while one was open for 0% -> 0% of each run, Pallas kernels for 0% -> 0%
where the time goes in v4:
time: 25.5 us; the launch traced here: 25.3 us
  blocking collectives  17.6 us (69%)
  Pallas kernels  7.08 us (28%)
  between operations  0.64 us (3%)
    all_to_all x1, blocking collectives, local(): x = swap(chunks, ('space', 'blk')).reshape(-1, points)  17.6 us
    pallas_call x1, Pallas kernels, modes_and_factor(): pl.pallas_call(functools.partial(modes_kernel, scale, slabs), out_shape=(...  4.55 us
    pallas_call x1, Pallas kernels, block_spectra(): pl.pallas_call(spectra_kernel, out_shape=jax.ShapeDtypeStruct((copies, ro...  2.53 us

profile of v4, /device:TPU:0, one launch (start us, length us, event | category | flops | bytes accessed | tf_op | source)
XLA Modules:
  0.0 25.3 jit_solution(7716839743381548152)
XLA Ops:
  0.6 2.5 %spectra.1 = bf16[2,128,512]{2,1,0:T(8,128)(2,1)} custom-call(bf16[1280,512]{1,0:T(8,128)(2,1)} %snap_hbm.1, f32[1280]{0:T(1024)} %scales_hbm.1, s32[4]{0:T(128)} %offsets_hbm.1, s32[16]{0:T(128)} %freq_hbm.1), custom_call_target="tpu_custom_call" | custom-call | tf_op jit(solution)/shard_map/spectra/pallas_call | solution.py:95
  3.2 17.6 %all_to_all.5 = bf16[32,8,512]{2,1,0:T(8,128)(2,1)S(1)} all-to-all(bf16[32,8,512]{2,1,0:T(8,128)(2,1)} %bitcast.5), channel_id=1, replica_groups=mesh['space'=2,'blk'=16] {'space','blk'}, dimensions={0} | all-to-all | bytes 524288 | tf_op jit(solution)/shard_map/all_to_all | solution.py:288
  20.8 4.5 %factor_and_modes.1 = (f32[512,128]{1,0:T(8,128)}, f32[2,64,64]{2,1,0:T(8,128)}) custom-call(bf16[256,512]{1,0:T(8,128)(2,1)S(1)} %bitcast.4), custom_call_target="tpu_custom_call" | custom-call | tf_op jit(solution)/shard_map/factor_and_modes/pallas_call | solution.py:262

commit v5 on v4

--- a/solution.py
+++ b/solution.py
@@ -173,7 +173,7 @@
             k = first + c
             pivot = over_rows(re[c][own], at)
             pivots[own] = jnp.where(sub == at, pivot, pivots[own])
-            inverse = 1.0 / pivot
+            inverse = pl.reciprocal(pivot, approx=True)
             upper = {
                 later: (over_rows(re[later][own], at), over_rows(im[later][own], at))
                 for later in range(c + 1, panel)
@@ -213,7 +213,7 @@
 
 
 def modes_kernel(scale, slabs, x_ref, *refs):
-    *given, modes_ref, factor_ref, basis_ref, upper_ref = refs
+    *given, modes_ref, factor_ref, basis_ref, points_ref = refs
     width = basis_ref.shape[0]
     size = width // 2
     count = size // SUB
@@ -224,36 +224,32 @@
         gram = gram_rows([x_ref[i * width:(i + 1) * width] for i in range(slabs)], basis_ref)
         own = lax.axis_index("space")
         mine = x_ref[pl.ds(pl.multiple_of(own * width, width), width)]
+    points = jnp.transpose(mine)
+    points_ref[...] = jnp.concatenate([points, points], 1)
     gram = gram * scale
     rows, pivots = eliminate([gram[i * SUB:(i + 1) * SUB] for i in range(count)], PANEL)
     shape = rows[0].shape
     sub = lax.broadcasted_iota(jnp.int32, shape, 0)
     lane = lax.broadcasted_iota(jnp.int32, shape, 1)
+    pick = jnp.where(lane < size, 2 * lane, 2 * (lane - size) + 1)
     for i in range(count):
+        own_rows = slice(i * SUB, (i + 1) * SUB)
         root = lax.rsqrt(pivots[i])
         diagonal = 2 * (i * SUB + sub)
-        right = jnp.where(lane > diagonal + 1, rows[i], jnp.where(lane == diagonal, pivots[i], 0.0))
-        left = jnp.where(lane < diagonal, rows[i], jnp.where(lane == diagonal, 1.0, 0.0))
-        upper_ref[i * SUB:(i + 1) * SUB, :] = right * root
-        left = left * root
+        left = jnp.where(lane < diagonal, rows[i], jnp.where(lane == diagonal, 1.0, 0.0)) * root
         basis_ref[pl.ds(2 * i * SUB, SUB, stride=2), :] = left
         basis_ref[pl.ds(2 * i * SUB + 1, SUB, stride=2), :] = rotated(left, lane)
-    points = jnp.transpose(mine)
+        right = jnp.where(lane > diagonal + 1, rows[i], jnp.where(lane == diagonal, pivots[i], 0.0))
+        parts = jnp.take_along_axis(right * root, pick, axis=1)
+        factor_ref[0, own_rows, :] = parts[:, :size]
+        factor_ref[1, own_rows, :] = parts[:, size:]
     basis = basis_ref[...]
     high = basis.astype(jnp.bfloat16)
     low = (basis - high.astype(jnp.float32)).astype(jnp.bfloat16)
-    contract = (((1,), (1,)), ((), ()))
     modes_ref[...] = lax.dot_general(
-        points, high, contract, preferred_element_type=jnp.float32
-    ) + lax.dot_general(points, low, contract, preferred_element_type=jnp.float32)
-    lane_in = lax.broadcasted_iota(jnp.int32, (2 * size, size), 0)
-    lane_out = lax.broadcasted_iota(jnp.int32, (2 * size, size), 1)
-    for part in range(2):
-        pick = (lane_in == 2 * lane_out + part).astype(jnp.float32)
-        factor_ref[part] = jnp.dot(
-            upper_ref[...], pick,
-            precision=lax.Precision.HIGHEST, preferred_element_type=jnp.float32,
-        )
+        points_ref[...], jnp.concatenate([high, low], 1), (((1,), (1,)), ((), ())),
+        preferred_element_type=jnp.float32,
+    )
 
 
 def modes_and_factor(x, grams, width, slabs, scale):
@@ -269,7 +265,7 @@
         out_specs=(pl.BlockSpec(memory_space=pltpu.VMEM),) * 2,
         scratch_shapes=[
             pltpu.VMEM((width, width), jnp.float32),
-            pltpu.VMEM((size, width), jnp.float32),
+            pltpu.VMEM((points, 2 * width), jnp.bfloat16),
         ],
         compiler_params=pltpu.CompilerParams(vmem_limit_bytes=8 * 2**20),
         name="factor_and_modes",

time: 25.5 us -> 25.5 us (level)
  no operation moved by 1% of the time
where the time goes in v5:
time: 25.5 us; the launch traced here: 25.3 us
  blocking collectives  17.6 us (69%)
  Pallas kernels  7.06 us (28%)
  between operations  0.64 us (3%)
    all_to_all x1, blocking collectives, local(): x = swap(chunks, ('space', 'blk')).reshape(-1, points)  17.6 us
    pallas_call x1, Pallas kernels, modes_and_factor(): pl.pallas_call(functools.partial(modes_kernel, scale, slabs), out_shape=(...  4.53 us
    pallas_call x1, Pallas kernels, block_spectra(): pl.pallas_call(spectra_kernel, out_shape=jax.ShapeDtypeStruct((copies, ro...  2.53 us

profile of v5, /device:TPU:0, one launch (start us, length us, event | category | flops | bytes accessed | tf_op | source)
XLA Modules:
  0.0 25.3 jit_solution(15938729708610626413)
XLA Ops:
  0.6 2.5 %spectra.1 = bf16[2,128,512]{2,1,0:T(8,128)(2,1)} custom-call(bf16[1280,512]{1,0:T(8,128)(2,1)} %snap_hbm.1, f32[1280]{0:T(1024)} %scales_hbm.1, s32[4]{0:T(128)} %offsets_hbm.1, s32[16]{0:T(128)} %freq_hbm.1), custom_call_target="tpu_custom_call" | custom-call | tf_op jit(solution)/shard_map/spectra/pallas_call | solution.py:95
  3.2 17.6 %all_to_all.5 = bf16[32,8,512]{2,1,0:T(8,128)(2,1)S(1)} all-to-all(bf16[32,8,512]{2,1,0:T(8,128)(2,1)} %bitcast.5), channel_id=1, replica_groups=mesh['space'=2,'blk'=16] {'space','blk'}, dimensions={0} | all-to-all | bytes 524288 | tf_op jit(solution)/shard_map/all_to_all | solution.py:284
  20.8 4.5 %factor_and_modes.1 = (f32[512,128]{1,0:T(8,128)}, f32[2,64,64]{2,1,0:T(8,128)}) custom-call(bf16[256,512]{1,0:T(8,128)(2,1)S(1)} %bitcast.4), custom_call_target="tpu_custom_call" | custom-call | tf_op jit(solution)/shard_map/factor_and_modes/pallas_call | solution.py:258

commit v6 on v5

--- a/solution.py
+++ b/solution.py
@@ -9,7 +9,7 @@
 from jax.sharding import PartitionSpec as P
 
 NFFT = 512
-PANEL = 4
+PANEL = 8
 SUB = 8
 PIECE = 256
 FEW_SLABS = 2
@@ -148,6 +148,12 @@
     )(x)
 
 
+def tree_sum(terms):
+    while len(terms) > 1:
+        terms = [sum(terms[i:i + 2]) for i in range(0, len(terms), 2)]
+    return terms[0]
+
+
 def eliminate(rows, panel):
     count = len(rows)
     shape = rows[0].shape
@@ -161,55 +167,55 @@
         return jnp.broadcast_to(x[at:at + 1, :], shape)
 
     rows = list(rows)
-    pivots = [jnp.ones(shape, jnp.float32) for _ in range(count)]
+    final = [None] * count
+    pivots = [None] * count
     for first in range(0, count * SUB, panel):
         own = first // SUB
-        live = range(own, count)
-        re = [{i: over_lanes(rows[i], 2 * (first + c)) for i in live} for c in range(panel)]
-        im = [{i: over_lanes(rows[i], 2 * (first + c) + 1) for i in live} for c in range(panel)]
         head, turned = rows[own], rotated(rows[own], lane)
+        if first % SUB == 0:
+            final[own], pivots[own] = head, jnp.ones(shape, jnp.float32)
+        columns = [2 * (first + c) for c in range(panel)]
+        raw = {
+            i: [(over_lanes(rows[i], at), over_lanes(rows[i], at + 1)) for at in columns]
+            for i in range(own, count)
+        }
+        here = raw[own]
         for c in range(panel):
             at = (first + c) % SUB
-            k = first + c
-            pivot = over_rows(re[c][own], at)
-            pivots[own] = jnp.where(sub == at, pivot, pivots[own])
+            here_row = sub == at
+            pivot = over_rows(here[c][0], at)
             inverse = pl.reciprocal(pivot, approx=True)
-            upper = {
-                later: (over_rows(re[later][own], at), over_rows(im[later][own], at))
-                for later in range(c + 1, panel)
-            }
-            for i in live:
-                re[c][i] = re[c][i] * inverse
-                im[c][i] = im[c][i] * inverse
-                for later, (u_re, u_im) in upper.items():
-                    re[later][i] = re[later][i] - (re[c][i] * u_re - im[c][i] * u_im)
-                    im[later][i] = im[later][i] - (re[c][i] * u_im + im[c][i] * u_re)
-            below = sub > at
-            m_re = jnp.where(below, re[c][own], 0.0)
-            m_im = jnp.where(below, im[c][own], 0.0)
-            on_re, on_im = lane == 2 * k, lane == 2 * k + 1
+            m_re = jnp.where(here_row, -inverse, here[c][0] * inverse)
+            m_im = jnp.where(here_row, 0.0, here[c][1] * inverse)
+            if first % SUB:
+                m_re = jnp.where(sub < first % SUB, 0.0, m_re)
+                m_im = jnp.where(sub < first % SUB, 0.0, m_im)
+            final[own] = jnp.where(here_row, head, final[own])
+            pivots[own] = jnp.where(here_row, pivot, pivots[own])
+            for later in range(c + 1, panel):
+                re, im = here[later]
+                u_re, u_im = over_rows(re, at), over_rows(im, at)
+                here[later] = (
+                    jnp.where(here_row, 0.0, re) - (m_re * u_re - m_im * u_im),
+                    jnp.where(here_row, 0.0, im) - (m_re * u_im + m_im * u_re),
+                )
+            on_re, on_im = lane == columns[c], lane == columns[c] + 1
             p = jnp.where(on_re, 1.0, jnp.where(on_im, 0.0, over_rows(head, at)))
             q = jnp.where(on_im, 1.0, jnp.where(on_re, 0.0, over_rows(turned, at)))
-            cleared = below & (on_re | on_im)
+            cleared = here_row | ((on_re | on_im) & (sub >= first % SUB))
             head = jnp.where(cleared, 0.0, head) - (m_re * p + m_im * q)
             turned = jnp.where(cleared, 0.0, turned) - (m_re * q - m_im * p)
         rows[own] = head
-        if own + 1 == count:
-            continue
-        inside = (lane >= 2 * first) & (lane < 2 * (first + panel))
-        rest = {i: jnp.where(inside, 0.0, rows[i]) for i in range(own + 1, count)}
-        for c in range(panel):
-            at = (first + c) % SUB
-            k = first + c
-            on_re, on_im = lane == 2 * k, lane == 2 * k + 1
-            drop = (lane >= 2 * k) & (lane < 2 * (first + panel))
-            p = jnp.where(on_re, 1.0, jnp.where(drop, 0.0, over_rows(head, at)))
-            q = jnp.where(on_im, 1.0, jnp.where(drop, 0.0, over_rows(turned, at)))
-            for i in rest:
-                rest[i] = rest[i] - (re[c][i] * p + im[c][i] * q)
-        for i in rest:
-            rows[i] = rest[i]
-    return rows, pivots
+        inside = (lane >= columns[0]) & (lane < columns[0] + 2 * panel)
+        solved = [
+            (over_rows(head, (first + c) % SUB), over_rows(turned, (first + c) % SUB))
+            for c in range(panel)
+        ]
+        for i in range(own + 1, count):
+            rows[i] = jnp.where(inside, 0.0, rows[i]) - tree_sum(
+                [re * p + im * q for (re, im), (p, q) in zip(raw[i], solved)]
+            )
+    return final, pivots
 
 
 def modes_kernel(scale, slabs, x_ref, *refs):

time: 25.5 us -> 25 us (0.980)
  Pallas kernels: 7.06 us -> 6.53 us
    pallas_call x1, Pallas kernels: 4.53 us -> 4 us  [modes_and_factor(): pl.pallas_call(functools.partial(modes_kernel, scale, slabs), out_shape=(...]
where the time goes in v6:
time: 25 us; the launch traced here: 24.8 us
  blocking collectives  17.6 us (70%)
  Pallas kernels  6.53 us (26%)
  between operations  0.64 us (3%)
    all_to_all x1, blocking collectives, local(): x = swap(chunks, ('space', 'blk')).reshape(-1, points)  17.6 us
    pallas_call x1, Pallas kernels, modes_and_factor(): pl.pallas_call(functools.partial(modes_kernel, scale, slabs), out_shape=(...  4 us
    pallas_call x1, Pallas kernels, block_spectra(): pl.pallas_call(spectra_kernel, out_shape=jax.ShapeDtypeStruct((copies, ro...  2.53 us

profile of v6, /device:TPU:0, one launch (start us, length us, event | category | flops | bytes accessed | tf_op | source)
XLA Modules:
  0.0 24.8 jit_solution(14928681835666335463)
XLA Ops:
  0.6 2.5 %spectra.1 = bf16[2,128,512]{2,1,0:T(8,128)(2,1)} custom-call(bf16[1280,512]{1,0:T(8,128)(2,1)} %snap_hbm.1, f32[1280]{0:T(1024)} %scales_hbm.1, s32[4]{0:T(128)} %offsets_hbm.1, s32[16]{0:T(128)} %freq_hbm.1), custom_call_target="tpu_custom_call" | custom-call | tf_op jit(solution)/shard_map/spectra/pallas_call | solution.py:95
  3.2 17.6 %all_to_all.5 = bf16[32,8,512]{2,1,0:T(8,128)(2,1)S(1)} all-to-all(bf16[32,8,512]{2,1,0:T(8,128)(2,1)} %bitcast.5), channel_id=1, replica_groups=mesh['space'=2,'blk'=16] {'space','blk'}, dimensions={0} | all-to-all | bytes 524288 | tf_op jit(solution)/shard_map/all_to_all | solution.py:290
  20.8 4.0 %factor_and_modes.1 = (f32[512,128]{1,0:T(8,128)}, f32[2,64,64]{2,1,0:T(8,128)}) custom-call(bf16[256,512]{1,0:T(8,128)(2,1)S(1)} %bitcast.4), custom_call_target="tpu_custom_call" | custom-call | tf_op jit(solution)/shard_map/factor_and_modes/pallas_call | solution.py:264

commit v7 on v6

--- a/solution.py
+++ b/solution.py
@@ -12,7 +12,7 @@
 PANEL = 8
 SUB = 8
 PIECE = 256
-FEW_SLABS = 2
+INNER = 4
 SIN_COEFS = (
     0.9999999765895043,
     -0.1666664763439475,
@@ -32,10 +32,8 @@
     return total * x
 
 
-def spectra_kernel(
-    snap_hbm, scales_hbm, offsets_hbm, freq_hbm, out_ref,
-    snap_ref, scales_ref, offsets_ref, freq_ref, coef_ref, small_sems, snap_sems,
-):
+def spectra_kernel(inner, snap_hbm, scales_hbm, offsets_hbm, freq_hbm, *refs):
+    *out_refs, snap_ref, scales_ref, offsets_ref, freq_ref, coef_ref, small_sems, snap_sems = refs
     snaps = snap_ref.shape[0]
     blocks = offsets_ref.shape[0]
     rows = 2 * blocks
@@ -69,7 +67,10 @@
     quarter = (row[:, :NFFT] % 2) * (NFFT // 4)
     repeats = -(-snaps // NFFT)
 
-    def rows_of(f):
+    def rows_of(g):
+        f = g
+        if len(out_refs) > 1:
+            f = ((lax.axis_index("blk") // inner) ^ (g // inner)) * inner + g % inner
         freq = freq_ref[f].astype(jnp.float32)
         table = cos_of_phase((base * freq).astype(jnp.int32) + quarter)
         return jnp.concatenate([table] * repeats, 1)[:, :snaps] * weight
@@ -77,26 +78,27 @@
     for f in range(0, freqs, 2):
         pair = jnp.concatenate([rows_of(f), rows_of(f + 1)], 0)
         coef_ref[f * rows:(f + 2) * rows, :] = pair.astype(jnp.bfloat16)
-    total = jnp.zeros(out_ref.shape[1:], jnp.float32)
+    total = jnp.zeros(coef_ref.shape[:1] + snap_ref.shape[1:], jnp.float32)
     for copy, piece in zip(large, pieces):
         copy.wait()
         total += jnp.dot(
             coef_ref[:, piece], snap_ref[piece], preferred_element_type=jnp.float32
         )
     result = total.astype(jnp.bfloat16)
-    for copy in range(out_ref.shape[0]):
-        out_ref[copy] = result
-
-
-def block_spectra(copies, snapshots, row_scales, block_offsets, freq_index):
+    each = result.shape[0] // len(out_refs)
+    for i, out_ref in enumerate(out_refs):
+        out_ref[...] = result[i * each:(i + 1) * each]
+
+
+def block_spectra(parts, inner, snapshots, row_scales, block_offsets, freq_index):
     snaps, points = snapshots.shape
     rows = 2 * block_offsets.shape[0] * freq_index.shape[0]
     pieces = -(-snaps // PIECE)
     return pl.pallas_call(
-        spectra_kernel,
-        out_shape=jax.ShapeDtypeStruct((copies, rows, points), jnp.bfloat16),
+        functools.partial(spectra_kernel, inner),
+        out_shape=[jax.ShapeDtypeStruct((rows // parts, points), jnp.bfloat16)] * parts,
         in_specs=[pl.BlockSpec(memory_space=pltpu.HBM)] * 4,
-        out_specs=pl.BlockSpec(memory_space=pltpu.VMEM),
+        out_specs=[pl.BlockSpec(memory_space=pltpu.VMEM)] * parts,
         scratch_shapes=[
             pltpu.VMEM((snaps, points), jnp.bfloat16),
             pltpu.VMEM((snaps,), jnp.float32),
@@ -109,6 +111,30 @@
         compiler_params=pltpu.CompilerParams(vmem_limit_bytes=60 * 2**20),
         name="spectra",
     )(snapshots, row_scales, block_offsets, freq_index)
+
+
+def regroup_kernel(*refs):
+    outer = refs[-1].shape[0]
+    in_refs, out_refs = refs[:outer], refs[outer:]
+    inner = len(out_refs)
+    place = lax.axis_index("blk")
+    group, member = place // inner, place % inner
+    for e, out_ref in enumerate(out_refs):
+        for d, in_ref in enumerate(in_refs):
+            out_ref[group ^ d] = in_ref[member ^ e]
+
+
+def regroup(arrays):
+    outer, inner = len(arrays), arrays[0].shape[0]
+    shape = (outer,) + arrays[0].shape[1:]
+    return pl.pallas_call(
+        regroup_kernel,
+        out_shape=[jax.ShapeDtypeStruct(shape, arrays[0].dtype)] * inner,
+        in_specs=[pl.BlockSpec(memory_space=pltpu.VMEM)] * outer,
+        out_specs=[pl.BlockSpec(memory_space=pltpu.VMEM)] * inner,
+        compiler_params=pltpu.CompilerParams(vmem_limit_bytes=4 * 2**20),
+        name="regroup",
+    )(*arrays)
 
 
 def rotated(x, lane):
@@ -218,18 +244,32 @@
     return final, pivots
 
 
-def modes_kernel(scale, slabs, x_ref, *refs):
-    *given, modes_ref, factor_ref, basis_ref, points_ref = refs
+def gathered(refs, rows_ref):
+    inner = len(refs)
+    member = lax.axis_index("blk") % inner
+    rows = refs[0].shape[1]
+    for e, ref in enumerate(refs):
+        for group in range(ref.shape[0]):
+            at = pl.multiple_of((group * inner + (member ^ e)) * rows, rows)
+            rows_ref[pl.ds(at, rows), :] = ref[group].astype(jnp.float32)
+    return rows_ref[...].astype(jnp.bfloat16)
+
+
+def modes_kernel(scale, slabs, *refs):
+    *given, modes_ref, factor_ref, basis_ref, points_ref, rows_ref = refs
     width = basis_ref.shape[0]
     size = width // 2
     count = size // SUB
-    if given:
-        gram = given[0][...]
-        mine = x_ref[...]
+    if slabs:
+        each = len(given) // slabs
+        all_points = [
+            gathered(given[i * each:(i + 1) * each], rows_ref.at[i]) for i in range(slabs)
+        ]
+        mine = all_points[0]
+        gram = gram_rows(all_points, basis_ref)
     else:
-        gram = gram_rows([x_ref[i * width:(i + 1) * width] for i in range(slabs)], basis_ref)
-        own = lax.axis_index("space")
-        mine = x_ref[pl.ds(pl.multiple_of(own * width, width), width)]
+        mine = given[0][...]
+        gram = given[1][...]
     points = jnp.transpose(mine)
     points_ref[...] = jnp.concatenate([points, points], 1)
     gram = gram * scale
@@ -258,8 +298,7 @@
     )
 
 
-def modes_and_factor(x, grams, width, slabs, scale):
-    points = x.shape[1]
+def modes_and_factor(operands, width, points, slabs, scale):
     size = width // 2
     return pl.pallas_call(
         functools.partial(modes_kernel, scale, slabs),
@@ -267,38 +306,56 @@
             jax.ShapeDtypeStruct((points, width), jnp.float32),
             jax.ShapeDtypeStruct((2, size, size), jnp.float32),
         ),
-        in_specs=[pl.BlockSpec(memory_space=pltpu.VMEM)] * (1 + len(grams)),
+        in_specs=[pl.BlockSpec(memory_space=pltpu.VMEM)] * len(operands),
         out_specs=(pl.BlockSpec(memory_space=pltpu.VMEM),) * 2,
         scratch_shapes=[
             pltpu.VMEM((width, width), jnp.float32),
             pltpu.VMEM((points, 2 * width), jnp.bfloat16),
+            pltpu.VMEM((max(slabs, 1), width, points), jnp.float32),
         ],
         compiler_params=pltpu.CompilerParams(vmem_limit_bytes=8 * 2**20),
         name="factor_and_modes",
-    )(x, *grams)
-
-
-def local(slabs, snapshots, row_scales, block_offsets, freq_index):
+    )(*operands)
+
+
+def local(slabs, owners, snapshots, row_scales, block_offsets, freq_index):
     freqs = freq_index.shape[0]
     points = snapshots.shape[1]
-    width = 2 * block_offsets.shape[0] * lax.axis_size("blk")
-    copies = slabs if slabs <= FEW_SLABS else 1
-    spectra = block_spectra(copies, snapshots, row_scales, block_offsets, freq_index)
-    chunks = spectra.reshape(copies * freqs, -1, points)
-    swap = functools.partial(lax.all_to_all, split_axis=0, concat_axis=0, tiled=True)
-    if copies == slabs:
-        x = swap(chunks, ("space", "blk")).reshape(-1, points)
-        grams = []
+    rows = 2 * block_offsets.shape[0] * (freqs // owners)
+    width = 2 * block_offsets.shape[0] * owners
+    scale = 1.0 / (points * slabs)
+    inputs = (snapshots, row_scales, block_offsets, freq_index)
+    if slabs == 2 and freqs == owners and owners % INNER == 0:
+        outer = owners // INNER
+        spectra = block_spectra(outer, INNER, *inputs)
+        near = [part.reshape(INNER, rows, points) for part in spectra]
+        arrived = near[:1] + [
+            lax.ppermute(near[d], "blk", [(i, i ^ (d * INNER)) for i in range(owners)])
+            for d in range(1, outer)
+        ]
+        parts = list(regroup(arrived))
+        both = ("space", "blk")
+        other = [
+            lax.ppermute(parts[e], both, [(i, (i + owners) % (2 * owners) ^ e) for i in range(2 * owners)])
+            for e in range(INNER)
+        ]
+        own = parts[:1] + [
+            lax.ppermute(parts[e], "blk", [(i, i ^ e) for i in range(owners)])
+            for e in range(1, INNER)
+        ]
+        operands, slabs_here = own + other, 2
     else:
-        x = swap(chunks, "blk").reshape(-1, points)
-        grams = [lax.psum(complex_gram(x), "space")]
-    modes, factor = modes_and_factor(x, grams, width, slabs, 1.0 / (points * slabs))
+        chunks = block_spectra(1, 1, *inputs)[0].reshape(freqs, -1, points)
+        x = lax.all_to_all(chunks, "blk", split_axis=0, concat_axis=0, tiled=True)
+        x = x.reshape(-1, points)
+        operands, slabs_here = [x, lax.psum(complex_gram(x), "space")], 0
+    modes, factor = modes_and_factor(operands, width, points, slabs_here, scale)
     return modes[None], factor[None]
 
 
 def solution(mesh):
     return jax.shard_map(
-        functools.partial(local, mesh.shape["space"]),
+        functools.partial(local, mesh.shape["space"], mesh.shape["blk"]),
         mesh=mesh,
         in_specs=(P("blk", "space"), P("blk"), P("blk"), P()),
         out_specs=(P("blk", "space", None), P("blk", None, None, None)),

time: 25 us -> 29.4 us (1.18)
  blocking collectives: 17.6 us -> 0 us
  starting transfers between devices: 0 us -> 12.6 us
  waiting for transfers between devices: 0 us -> 8.68 us
  local copies, waits for them, and re-layouts: 0 us -> 0.76 us
    all_to_all x1 -> x0, blocking collectives: 17.6 us -> none  [local(): x = swap(chunks, ('space', 'blk')).reshape(-1, points)]
    ppermute x0 -> x10, starting transfers between devices: none -> 12.6 us  [the longest x3 5.68 us: local(): lax.ppermute(near[d], 'blk', [(i, i ^ d * INNER) for i in range(owners)])]
    ppermute x0 -> x10, waiting for transfers between devices: none -> 8.68 us  [the longest x3 5.92 us: local(): lax.ppermute(near[d], 'blk', [(i, i ^ d * INNER) for i in range(owners)])]
    unnamed x0 -> x2, local copies, waits for them, and re-layouts: none -> 0.76 us
    pallas_call x1 -> x2, Pallas kernels: 2.53 us -> 2.43 us  [the longest x1 2.42 us: block_spectra(): pl.pallas_call(functools.partial(spectra_kernel, inner), out_shape=[jax.S...]
  transfers between devices with their start and end apart: 0 -> 10, of which waited for: 0 -> 5; matrix products, arithmetic and copies ran while one was open for 0% -> 0% of each run, Pallas kernels for 0% -> 0%
where the time goes in v7:
time: 29.4 us; the launch traced here: 29.2 us
  starting transfers between devices  12.6 us (43%)
  waiting for transfers between devices  8.68 us (30%)
  Pallas kernels  6.49 us (22%)
  local copies, waits for them, and re-layouts  0.76 us (3%)
  between operations  0.65 us (2%)
    ppermute x3, waiting for transfers between devices, local(): lax.ppermute(near[d], 'blk', [(i, i ^ d * INNER) for i in range(owners)])  5.92 us
    ppermute x3, starting transfers between devices, local(): lax.ppermute(near[d], 'blk', [(i, i ^ d * INNER) for i in range(owners)])  5.68 us
    ppermute x4, starting transfers between devices, local(): lax.ppermute(parts[e], both, [(i, (i + owners) % (2 * owners) ^ e) for i...  4.55 us
    pallas_call x1, Pallas kernels, modes_and_factor(): pl.pallas_call(functools.partial(modes_kernel, scale, slabs), out_shape=(...  4.06 us
    pallas_call x1, Pallas kernels, block_spectra(): pl.pallas_call(functools.partial(spectra_kernel, inner), out_shape=[jax.S...  2.42 us
    ppermute x3, starting transfers between devices, local(): lax.ppermute(parts[e], 'blk', [(i, i ^ e) for i in range(owners)])  2.41 us
    ppermute x3, waiting for transfers between devices, local(): lax.ppermute(parts[e], 'blk', [(i, i ^ e) for i in range(owners)])  1.84 us
    ppermute x4, waiting for transfers between devices, local(): lax.ppermute(parts[e], both, [(i, (i + owners) % (2 * owners) ^ e) for i...  0.93 us
  transfers between devices with their start and end apart: 10, of which 5 were waited for; matrix products, arithmetic and copies ran while one was open for 0% of the time, Pallas kernels for 0%

profile of v7, /device:TPU:0, one launch (start us, length us, event | category | flops | bytes accessed | tf_op | source)
XLA Modules:
  0.0 29.2 jit_solution(1868363125170464079)
XLA Ops:
  0.6 2.4 %spectra.1 = (bf16[32,512]{1,0:T(8,128)(2,1)}, bf16[32,512]{1,0:T(8,128)(2,1)}, bf16[32,512]{1,0:T(8,128)(2,1)}, bf16[32,512]{1,0:T(8,128)(2,1)}) custom-call(bf16[1280,512]{1,0:T(8,128)(2,1)} %snap_hbm.1, f32[1280]{0:T(1024)} %scales_hbm.1, s32[4]{0:T(128)} %offsets_hbm.1, s32[16]{0:T(128)} %freq_hbm.1), custom_call_target="tpu_custom_call" | custom-call | tf_op jit(solution)/shard_map/spectra/pallas_call | solution.py:97
  3.1 3.1 %collective-permute-start = (bf16[4,8,512]{2,1,0:T(8,128)(2,1)}, bf16[4,8,512]{2,1,0:T(8,128)(2,1)S(1)}, u32[]{:S(2)}, u32[]{:S(2)}) collective-permute-start(bf16[4,8,512]{2,1,0:T(8,128)(2,1)} %bitcast.11), channel_id=1, source_target_pairs={{0,4},{1,5},{2,6},{3,7},{4,0},{5,1},{6,2},{7,3},{8,12},{9,13},{10,... | collective-permute-start | bytes 98312 | tf_op jit(solution)/shard_map/ppermute | solution.py:333
  6.1 2.6 %collective-permute-start.1 = (bf16[4,8,512]{2,1,0:T(8,128)(2,1)}, bf16[4,8,512]{2,1,0:T(8,128)(2,1)S(1)}, u32[]{:S(2)}, u32[]{:S(2)}) collective-permute-start(bf16[4,8,512]{2,1,0:T(8,128)(2,1)} %bitcast.10), channel_id=1, source_target_pairs={{0,8},{1,9},{2,10},{3,11},{4,12},{5,13},{6,14},{7,15},{8,0},{9,1},... | collective-permute-start | bytes 98312 | tf_op jit(solution)/shard_map/ppermute | solution.py:333
  8.7 0.0 collective-permute-start.2
  8.7 0.0 collective-permute-done.refs_1_
  8.7 3.0 %collective-permute-done.1.refs_2_ = bf16[4,8,512]{2,1,0:T(8,128)(2,1)S(1)} collective-permute-done((bf16[4,8,512]{2,1,0:T(8,128)(2,1)}, bf16[4,8,512]{2,1,0:T(8,128)(2,1)S(1)}, u32[]{:S(2)}, u32[]{:S(2)}) %collective-permute-start.1) | collective-permute-done | bytes 32800 | tf_op jit(solution)/shard_map/ppermute | solution.py:333
  11.8 2.9 %collective-permute-done.2.refs_3_ = bf16[4,8,512]{2,1,0:T(8,128)(2,1)S(1)} collective-permute-done((bf16[4,8,512]{2,1,0:T(8,128)(2,1)}, bf16[4,8,512]{2,1,0:T(8,128)(2,1)S(1)}, u32[]{:S(2)}, u32[]{:S(2)}) %collective-permute-start.2) | collective-permute-done | bytes 32800 | tf_op jit(solution)/shard_map/ppermute | solution.py:333
  14.7 0.0 copy-start
  14.7 0.8 %copy-done = bf16[32,512]{1,0:T(8,128)(2,1)S(1)} copy-done((bf16[32,512]{1,0:T(8,128)(2,1)S(1)}, bf16[32,512]{1,0:T(8,128)(2,1)}, u32[]{:S(2)}) %copy-start) | copy-done | bytes 32792
  15.4 1.6 %collective-permute-start.6 = (bf16[4,8,512]{2,1,0:T(8,128)(2,1)S(1)}, bf16[4,8,512]{2,1,0:T(8,128)(2,1)S(1)}, u32[]{:S(2)}, u32[]{:S(2)}) collective-permute-start(bf16[4,8,512]{2,1,0:T(8,128)(2,1)S(1)} %get-tuple-element.16.refs_0_), channel_id=1, source_target_pairs={{0,16},{1,17},{2,18},{3,19},{4,20},{5,21},{6,22},{7,23},{8,24},{9,... | collective-permute-start | bytes 98312 | tf_op jit(solution)/shard_map/ppermute | solution.py:339
  17.0 0.0 collective-permute-start.7
  17.0 0.6 %collective-permute-start.3 = (bf16[4,8,512]{2,1,0:T(8,128)(2,1)S(1)}, bf16[4,8,512]{2,1,0:T(8,128)(2,1)S(1)}, u32[]{:S(2)}, u32[]{:S(2)}) collective-permute-start(bf16[4,8,512]{2,1,0:T(8,128)(2,1)S(1)} %get-tuple-element.17), channel_id=1, source_target_pairs={{0,1},{1,0},{2,3},{3,2},{4,5},{5,4},{6,7},{7,6},{8,9},{9,8},{10,11... | collective-permute-start | bytes 98312 | tf_op jit(solution)/shard_map/ppermute | solution.py:343
  17.6 2.5 %collective-permute-start.8 = (bf16[4,8,512]{2,1,0:T(8,128)(2,1)S(1)}, bf16[4,8,512]{2,1,0:T(8,128)(2,1)S(1)}, u32[]{:S(2)}, u32[]{:S(2)}) collective-permute-start(bf16[4,8,512]{2,1,0:T(8,128)(2,1)S(1)} %get-tuple-element.18), channel_id=1, source_target_pairs={{0,18},{1,19},{2,16},{3,17},{4,22},{5,23},{6,20},{7,21},{8,26},{9,... | collective-permute-start | bytes 98312 | tf_op jit(solution)/shard_map/ppermute | solution.py:339
  20.1 0.5 %collective-permute-start.4 = (bf16[4,8,512]{2,1,0:T(8,128)(2,1)S(1)}, bf16[4,8,512]{2,1,0:T(8,128)(2,1)S(1)}, u32[]{:S(2)}, u32[]{:S(2)}) collective-permute-start(bf16[4,8,512]{2,1,0:T(8,128)(2,1)S(1)} %get-tuple-element.18), channel_id=1, source_target_pairs={{0,2},{1,3},{2,0},{3,1},{4,6},{5,7},{6,4},{7,5},{8,10},{9,11},{10,... | collective-permute-start | bytes 98312 | tf_op jit(solution)/shard_map/ppermute | solution.py:343
  20.6 0.0 collective-permute-done.6.refs_4_
  20.6 0.5 %collective-permute-start.9 = (bf16[4,8,512]{2,1,0:T(8,128)(2,1)S(1)}, bf16[4,8,512]{2,1,0:T(8,128)(2,1)S(1)}, u32[]{:S(2)}, u32[]{:S(2)}) collective-permute-start(bf16[4,8,512]{2,1,0:T(8,128)(2,1)S(1)} %get-tuple-element.19), channel_id=1, source_target_pairs={{0,19},{1,18},{2,17},{3,16},{4,23},{5,22},{6,21},{7,20},{8,27},{9,... | collective-permute-start | bytes 98312 | tf_op jit(solution)/shard_map/ppermute | solution.py:339
  21.1 0.0 collective-permute-done.7.refs_5_
  21.1 1.3 %collective-permute-start.5 = (bf16[4,8,512]{2,1,0:T(8,128)(2,1)S(1)}, bf16[4,8,512]{2,1,0:T(8,128)(2,1)S(1)}, u32[]{:S(2)}, u32[]{:S(2)}) collective-permute-start(bf16[4,8,512]{2,1,0:T(8,128)(2,1)S(1)} %get-tuple-element.19), channel_id=1, source_target_pairs={{0,3},{1,2},{2,1},{3,0},{4,7},{5,6},{6,5},{7,4},{8,11},{9,10},{10,... | collective-permute-start | bytes 98312 | tf_op jit(solution)/shard_map/ppermute | solution.py:343
  22.4 0.0 collective-permute-done.3.refs_1_
  22.4 0.0 collective-permute-done.8.refs_6_
  22.5 1.6 %collective-permute-done.4.refs_2_ = bf16[4,8,512]{2,1,0:T(8,128)(2,1)S(1)} collective-permute-done((bf16[4,8,512]{2,1,0:T(8,128)(2,1)S(1)}, bf16[4,8,512]{2,1,0:T(8,128)(2,1)S(1)}, u32[]{:S(2)}, u32[]{:S(2)}) %collective-permute-start.4) | collective-permute-done | bytes 32800 | tf_op jit(solution)/shard_map/ppermute | solution.py:343
  24.0 0.9 %collective-permute-done.9.refs_7_ = bf16[4,8,512]{2,1,0:T(8,128)(2,1)S(1)} collective-permute-done((bf16[4,8,512]{2,1,0:T(8,128)(2,1)S(1)}, bf16[4,8,512]{2,1,0:T(8,128)(2,1)S(1)}, u32[]{:S(2)}, u32[]{:S(2)}) %collective-permute-start.9) | collective-permute-done | bytes 32800 | tf_op jit(solution)/shard_map/ppermute | solution.py:339
  24.9 0.3 collective-permute-done.5.refs_3_
  25.2 4.1 %factor_and_modes.1 = (f32[512,128]{1,0:T(8,128)}, f32[2,64,64]{2,1,0:T(8,128)}) custom-call(bf16[4,8,512]{2,1,0:T(8,128)(2,1)S(1)} %get-tuple-element.16.refs_0_, bf16[4,8,512]{2,1,0:T(8,128)(2,1)S(1)} %collective-permute-done.3.refs_1_, bf16[4,8,512]{2,1,0:T(8,128)(2,1)S(1)} %collective-permute-done.4.refs_2_, ...), custom_call_target="tpu_custom_call" | custom-call | tf_op jit(solution)/shard_map/factor_and_modes/pallas_call | solution.py:303
  (1 shorter events, 0.0 us)
Async XLA Ops:
  3.1 5.7 %collective-permute-start = (bf16[4,8,512]{2,1,0:T(8,128)(2,1)}, bf16[4,8,512]{2,1,0:T(8,128)(2,1)S(1)}, u32[]{:S(2)}, u32[]{:S(2)}) collective-permute-start(bf16[4,8,512]{2,1,0:T(8,128)(2,1)} %bitcast.11), channel_id=1, source_target_pairs={{0,4},{1,5},{2,6},{3,7},{4,0},{5,1},{6,2},{7,3},{8,12},{9,13},{10,... | collective-permute-start | bytes 98312 | tf_op jit(solution)/shard_map/ppermute | solution.py:333
  6.1 5.6 %collective-permute-start.1 = (bf16[4,8,512]{2,1,0:T(8,128)(2,1)}, bf16[4,8,512]{2,1,0:T(8,128)(2,1)S(1)}, u32[]{:S(2)}, u32[]{:S(2)}) collective-permute-start(bf16[4,8,512]{2,1,0:T(8,128)(2,1)} %bitcast.10), channel_id=1, source_target_pairs={{0,8},{1,9},{2,10},{3,11},{4,12},{5,13},{6,14},{7,15},{8,0},{9,1},... | collective-permute-start | bytes 98312 | tf_op jit(solution)/shard_map/ppermute | solution.py:333
  8.7 5.9 %collective-permute-start.2 = (bf16[4,8,512]{2,1,0:T(8,128)(2,1)}, bf16[4,8,512]{2,1,0:T(8,128)(2,1)S(1)}, u32[]{:S(2)}, u32[]{:S(2)}) collective-permute-start(bf16[4,8,512]{2,1,0:T(8,128)(2,1)} %bitcast.9), channel_id=1, source_target_pairs={{0,12},{1,13},{2,14},{3,15},{4,8},{5,9},{6,10},{7,11},{8,4},{9,5},... | collective-permute-start | bytes 98312 | tf_op jit(solution)/shard_map/ppermute | solution.py:333
  14.7 0.8 %copy-start = (bf16[32,512]{1,0:T(8,128)(2,1)S(1)}, bf16[32,512]{1,0:T(8,128)(2,1)}, u32[]{:S(2)}) copy-start(bf16[32,512]{1,0:T(8,128)(2,1)} %get-tuple-element.12) | copy-start | bytes 98308
  15.4 5.2 %collective-permute-start.6 = (bf16[4,8,512]{2,1,0:T(8,128)(2,1)S(1)}, bf16[4,8,512]{2,1,0:T(8,128)(2,1)S(1)}, u32[]{:S(2)}, u32[]{:S(2)}) collective-permute-start(bf16[4,8,512]{2,1,0:T(8,128)(2,1)S(1)} %get-tuple-element.16.refs_0_), channel_id=1, source_target_pairs={{0,16},{1,17},{2,18},{3,19},{4,20},{5,21},{6,22},{7,23},{8,24},{9,... | collective-permute-start | bytes 98312 | tf_op jit(solution)/shard_map/ppermute | solution.py:339
  17.0 4.2 %collective-permute-start.7 = (bf16[4,8,512]{2,1,0:T(8,128)(2,1)S(1)}, bf16[4,8,512]{2,1,0:T(8,128)(2,1)S(1)}, u32[]{:S(2)}, u32[]{:S(2)}) collective-permute-start(bf16[4,8,512]{2,1,0:T(8,128)(2,1)S(1)} %get-tuple-element.17), channel_id=1, source_target_pairs={{0,17},{1,16},{2,19},{3,18},{4,21},{5,20},{6,23},{7,22},{8,25},{9,... | collective-permute-start | bytes 98312 | tf_op jit(solution)/shard_map/ppermute | solution.py:339
  17.0 5.4 %collective-permute-start.3 = (bf16[4,8,512]{2,1,0:T(8,128)(2,1)S(1)}, bf16[4,8,512]{2,1,0:T(8,128)(2,1)S(1)}, u32[]{:S(2)}, u32[]{:S(2)}) collective-permute-start(bf16[4,8,512]{2,1,0:T(8,128)(2,1)S(1)} %get-tuple-element.17), channel_id=1, source_target_pairs={{0,1},{1,0},{2,3},{3,2},{4,5},{5,4},{6,7},{7,6},{8,9},{9,8},{10,11... | collective-permute-start | bytes 98312 | tf_op jit(solution)/shard_map/ppermute | solution.py:343
  17.6 4.8 %collective-permute-start.8 = (bf16[4,8,512]{2,1,0:T(8,128)(2,1)S(1)}, bf16[4,8,512]{2,1,0:T(8,128)(2,1)S(1)}, u32[]{:S(2)}, u32[]{:S(2)}) collective-permute-start(bf16[4,8,512]{2,1,0:T(8,128)(2,1)S(1)} %get-tuple-element.18), channel_id=1, source_target_pairs={{0,18},{1,19},{2,16},{3,17},{4,22},{5,23},{6,20},{7,21},{8,26},{9,... | collective-permute-start | bytes 98312 | tf_op jit(solution)/shard_map/ppermute | solution.py:339
  20.1 3.9 %collective-permute-start.4 = (bf16[4,8,512]{2,1,0:T(8,128)(2,1)S(1)}, bf16[4,8,512]{2,1,0:T(8,128)(2,1)S(1)}, u32[]{:S(2)}, u32[]{:S(2)}) collective-permute-start(bf16[4,8,512]{2,1,0:T(8,128)(2,1)S(1)} %get-tuple-element.18), channel_id=1, source_target_pairs={{0,2},{1,3},{2,0},{3,1},{4,6},{5,7},{6,4},{7,5},{8,10},{9,11},{10,... | collective-permute-start | bytes 98312 | tf_op jit(solution)/shard_map/ppermute | solution.py:343
  20.6 4.3 %collective-permute-start.9 = (bf16[4,8,512]{2,1,0:T(8,128)(2,1)S(1)}, bf16[4,8,512]{2,1,0:T(8,128)(2,1)S(1)}, u32[]{:S(2)}, u32[]{:S(2)}) collective-permute-start(bf16[4,8,512]{2,1,0:T(8,128)(2,1)S(1)} %get-tuple-element.19), channel_id=1, source_target_pairs={{0,19},{1,18},{2,17},{3,16},{4,23},{5,22},{6,21},{7,20},{8,27},{9,... | collective-permute-start | bytes 98312 | tf_op jit(solution)/shard_map/ppermute | solution.py:339
  21.1 4.0 %collective-permute-start.5 = (bf16[4,8,512]{2,1,0:T(8,128)(2,1)S(1)}, bf16[4,8,512]{2,1,0:T(8,128)(2,1)S(1)}, u32[]{:S(2)}, u32[]{:S(2)}) collective-permute-start(bf16[4,8,512]{2,1,0:T(8,128)(2,1)S(1)} %get-tuple-element.19), channel_id=1, source_target_pairs={{0,3},{1,2},{2,1},{3,0},{4,7},{5,6},{6,5},{7,4},{8,11},{9,10},{10,... | collective-permute-start | bytes 98312 | tf_op jit(solution)/shard_map/ppermute | solution.py:343

commit v8 on v6

--- a/solution.py
+++ b/solution.py
@@ -106,9 +106,12 @@
             pltpu.SemaphoreType.DMA((3,)),
             pltpu.SemaphoreType.DMA((pieces,)),
         ],
-        compiler_params=pltpu.CompilerParams(vmem_limit_bytes=60 * 2**20),
+        compiler_params=pltpu.CompilerParams(vmem_limit_bytes=8 * 2**20),
         name="spectra",
-    )(snapshots, row_scales, block_offsets, freq_index)
+    )(*(
+        pltpu.with_memory_space_constraint(x, pltpu.HBM)
+        for x in (snapshots, row_scales, block_offsets, freq_index)
+    ))
 
 
 def rotated(x, lane):

time: 25 us -> 24 us (0.960)
  Pallas kernels: 6.53 us -> 5.83 us
    pallas_call x1, Pallas kernels: 2.53 us -> 1.83 us  [block_spectra(): pl.pallas_call(spectra_kernel, out_shape=jax.ShapeDtypeStruct((copies, ro...]
where the time goes in v8:
time: 24 us; the launch traced here: 23.9 us
  blocking collectives  17.4 us (72%)
  Pallas kernels  5.83 us (24%)
  between operations  0.64 us (3%)
    all_to_all x1, blocking collectives, local(): x = swap(chunks, ('space', 'blk')).reshape(-1, points)  17.4 us
    pallas_call x1, Pallas kernels, modes_and_factor(): pl.pallas_call(functools.partial(modes_kernel, scale, slabs), out_shape=(...  4 us
    pallas_call x1, Pallas kernels, block_spectra(): pl.pallas_call(spectra_kernel, out_shape=jax.ShapeDtypeStruct((copies, ro...  1.83 us

profile of v8, /device:TPU:0, one launch (start us, length us, event | category | flops | bytes accessed | tf_op | source)
XLA Modules:
  0.0 23.9 jit_solution(12381248686807624841)
XLA Ops:
  0.6 1.8 %spectra.1 = bf16[2,128,512]{2,1,0:T(8,128)(2,1)S(1)} custom-call(bf16[1280,512]{1,0:T(8,128)(2,1)} %snap_hbm.1, f32[1280]{0:T(1024)} %scales_hbm.1, s32[4]{0:T(128)} %offsets_hbm.1, s32[16]{0:T(128)} %freq_hbm.1), custom_call_target="tpu_custom_call" | custom-call | tf_op jit(solution)/shard_map/spectra/pallas_call | solution.py:95
  2.5 17.4 %all_to_all.5 = bf16[32,8,512]{2,1,0:T(8,128)(2,1)S(1)} all-to-all(bf16[32,8,512]{2,1,0:T(8,128)(2,1)S(1)} %bitcast.5), channel_id=1, replica_groups=mesh['space'=2,'blk'=16] {'space','blk'}, dimensions={0} | all-to-all | bytes 524288 | tf_op jit(solution)/shard_map/all_to_all | solution.py:293
  19.9 4.0 %factor_and_modes.1 = (f32[512,128]{1,0:T(8,128)}, f32[2,64,64]{2,1,0:T(8,128)}) custom-call(bf16[256,512]{1,0:T(8,128)(2,1)S(1)} %bitcast.4), custom_call_target="tpu_custom_call" | custom-call | tf_op jit(solution)/shard_map/factor_and_modes/pallas_call | solution.py:267

commit v9 on v8

--- a/solution.py
+++ b/solution.py
@@ -9,7 +9,7 @@
 from jax.sharding import PartitionSpec as P
 
 NFFT = 512
-PANEL = 8
+PANEL = 4
 SUB = 8
 PIECE = 256
 FEW_SLABS = 2
@@ -77,24 +77,25 @@
     for f in range(0, freqs, 2):
         pair = jnp.concatenate([rows_of(f), rows_of(f + 1)], 0)
         coef_ref[f * rows:(f + 2) * rows, :] = pair.astype(jnp.bfloat16)
-    total = jnp.zeros(out_ref.shape[1:], jnp.float32)
+    total = jnp.zeros(coef_ref.shape[:1] + snap_ref.shape[1:], jnp.float32)
     for copy, piece in zip(large, pieces):
         copy.wait()
         total += jnp.dot(
             coef_ref[:, piece], snap_ref[piece], preferred_element_type=jnp.float32
         )
-    result = total.astype(jnp.bfloat16)
-    for copy in range(out_ref.shape[0]):
-        out_ref[copy] = result
+    for f in range(freqs):
+        one = total[f * rows:(f + 1) * rows]
+        out_ref[f] = jnp.concatenate([one] * (out_ref.shape[1] // rows), 0).astype(jnp.bfloat16)
 
 
 def block_spectra(copies, snapshots, row_scales, block_offsets, freq_index):
     snaps, points = snapshots.shape
-    rows = 2 * block_offsets.shape[0] * freq_index.shape[0]
+    freqs = freq_index.shape[0]
+    rows = 2 * block_offsets.shape[0]
     pieces = -(-snaps // PIECE)
     return pl.pallas_call(
         spectra_kernel,
-        out_shape=jax.ShapeDtypeStruct((copies, rows, points), jnp.bfloat16),
+        out_shape=jax.ShapeDtypeStruct((freqs, copies * rows, points), jnp.bfloat16),
         in_specs=[pl.BlockSpec(memory_space=pltpu.HBM)] * 4,
         out_specs=pl.BlockSpec(memory_space=pltpu.VMEM),
         scratch_shapes=[
@@ -102,7 +103,7 @@
             pltpu.VMEM((snaps,), jnp.float32),
             pltpu.SMEM(block_offsets.shape, jnp.int32),
             pltpu.SMEM(freq_index.shape, jnp.int32),
-            pltpu.VMEM((rows, snaps), jnp.bfloat16),
+            pltpu.VMEM((freqs * rows, snaps), jnp.bfloat16),
             pltpu.SemaphoreType.DMA((3,)),
             pltpu.SemaphoreType.DMA((pieces,)),
         ],
@@ -221,7 +222,7 @@
     return final, pivots
 
 
-def modes_kernel(scale, slabs, x_ref, *refs):
+def modes_kernel(scale, slabs, rows, x_ref, *refs):
     *given, modes_ref, factor_ref, basis_ref, points_ref = refs
     width = basis_ref.shape[0]
     size = width // 2
@@ -230,14 +231,19 @@
         gram = given[0][...]
         mine = x_ref[...]
     else:
-        gram = gram_rows([x_ref[i * width:(i + 1) * width] for i in range(slabs)], basis_ref)
+        points = x_ref.shape[1]
+        both = x_ref[...].astype(jnp.float32).reshape(-1, slabs, rows, points)
+        split = [both[:, i].reshape(width, points).astype(jnp.bfloat16) for i in range(slabs)]
+        gram = gram_rows(split, basis_ref)
         own = lax.axis_index("space")
-        mine = x_ref[pl.ds(pl.multiple_of(own * width, width), width)]
+        mine = split[0]
+        for i in range(1, slabs):
+            mine = jnp.where(own == i, split[i], mine)
     points = jnp.transpose(mine)
     points_ref[...] = jnp.concatenate([points, points], 1)
     gram = gram * scale
-    rows, pivots = eliminate([gram[i * SUB:(i + 1) * SUB] for i in range(count)], PANEL)
-    shape = rows[0].shape
+    factored, pivots = eliminate([gram[i * SUB:(i + 1) * SUB] for i in range(count)], PANEL)
+    shape = factored[0].shape
     sub = lax.broadcasted_iota(jnp.int32, shape, 0)
     lane = lax.broadcasted_iota(jnp.int32, shape, 1)
     pick = jnp.where(lane < size, 2 * lane, 2 * (lane - size) + 1)
@@ -245,10 +251,10 @@
         own_rows = slice(i * SUB, (i + 1) * SUB)
         root = lax.rsqrt(pivots[i])
         diagonal = 2 * (i * SUB + sub)
-        left = jnp.where(lane < diagonal, rows[i], jnp.where(lane == diagonal, 1.0, 0.0)) * root
+        left = jnp.where(lane < diagonal, factored[i], jnp.where(lane == diagonal, 1.0, 0.0)) * root
         basis_ref[pl.ds(2 * i * SUB, SUB, stride=2), :] = left
         basis_ref[pl.ds(2 * i * SUB + 1, SUB, stride=2), :] = rotated(left, lane)
-        right = jnp.where(lane > diagonal + 1, rows[i], jnp.where(lane == diagonal, pivots[i], 0.0))
+        right = jnp.where(lane > diagonal + 1, factored[i], jnp.where(lane == diagonal, pivots[i], 0.0))
         parts = jnp.take_along_axis(right * root, pick, axis=1)
         factor_ref[0, own_rows, :] = parts[:, :size]
         factor_ref[1, own_rows, :] = parts[:, size:]
@@ -261,11 +267,11 @@
     )
 
 
-def modes_and_factor(x, grams, width, slabs, scale):
+def modes_and_factor(x, grams, width, slabs, rows, scale):
     points = x.shape[1]
     size = width // 2
     return pl.pallas_call(
-        functools.partial(modes_kernel, scale, slabs),
+        functools.partial(modes_kernel, scale, slabs, rows),
         out_shape=(
             jax.ShapeDtypeStruct((points, width), jnp.float32),
             jax.ShapeDtypeStruct((2, size, size), jnp.float32),
@@ -285,17 +291,18 @@
     freqs = freq_index.shape[0]
     points = snapshots.shape[1]
     width = 2 * block_offsets.shape[0] * lax.axis_size("blk")
+    rows = 2 * block_offsets.shape[0]
     copies = slabs if slabs <= FEW_SLABS else 1
     spectra = block_spectra(copies, snapshots, row_scales, block_offsets, freq_index)
-    chunks = spectra.reshape(copies * freqs, -1, points)
+    chunks = spectra.reshape(copies * freqs, rows, points)
     swap = functools.partial(lax.all_to_all, split_axis=0, concat_axis=0, tiled=True)
     if copies == slabs:
-        x = swap(chunks, ("space", "blk")).reshape(-1, points)
+        x = swap(chunks, ("blk", "space")).reshape(-1, points)
         grams = []
     else:
         x = swap(chunks, "blk").reshape(-1, points)
         grams = [lax.psum(complex_gram(x), "space")]
-    modes, factor = modes_and_factor(x, grams, width, slabs, 1.0 / (points * slabs))
+    modes, factor = modes_and_factor(x, grams, width, slabs, rows, 1.0 / (points * slabs))
     return modes[None], factor[None]
 
 

time: 24 us -> 25.3 us (1.054)
  Pallas kernels: 5.83 us -> 6.7 us
  blocking collectives: 17.4 us -> 17.8 us
    pallas_call x2, Pallas kernels: 5.83 us -> 6.7 us  [the longest x1 4.88 us: modes_and_factor(): pl.pallas_call(functools.partial(modes_kernel, scale, slabs, rows), out_s...]
    all_to_all x1, blocking collectives: 17.4 us -> 17.8 us  [local(): x = swap(chunks, ('blk', 'space')).reshape(-1, points)]
where the time goes in v9:
time: 25.3 us; the launch traced here: 25.1 us
  blocking collectives  17.8 us (70%)
  Pallas kernels  6.7 us (26%)
  between operations  0.64 us (3%)
    all_to_all x1, blocking collectives, local(): x = swap(chunks, ('blk', 'space')).reshape(-1, points)  17.8 us
    pallas_call x1, Pallas kernels, modes_and_factor(): pl.pallas_call(functools.partial(modes_kernel, scale, slabs, rows), out_s...  4.88 us
    pallas_call x1, Pallas kernels, block_spectra(): pl.pallas_call(spectra_kernel, out_shape=jax.ShapeDtypeStruct((freqs, cop...  1.83 us

profile of v9, /device:TPU:0, one launch (start us, length us, event | category | flops | bytes accessed | tf_op | source)
XLA Modules:
  0.0 25.1 jit_solution(10016508347185949973)
XLA Ops:
  0.6 1.8 %spectra.1 = bf16[16,16,512]{2,1,0:T(8,128)(2,1)S(1)} custom-call(bf16[1280,512]{1,0:T(8,128)(2,1)} %snap_hbm.1, f32[1280]{0:T(1024)} %scales_hbm.1, s32[4]{0:T(128)} %offsets_hbm.1, s32[16]{0:T(128)} %freq_hbm.1), custom_call_target="tpu_custom_call" | custom-call | tf_op jit(solution)/shard_map/spectra/pallas_call | solution.py:96
  2.5 17.8 %all_to_all.5 = bf16[32,8,512]{2,1,0:T(8,128)(2,1)S(1)} all-to-all(bf16[32,8,512]{2,1,0:T(8,128)(2,1)S(1)} %bitcast.5), channel_id=1, replica_groups=mesh['space'=2,'blk'=16] {'blk','space'}, dimensions={0} | all-to-all | bytes 524288 | tf_op jit(solution)/shard_map/all_to_all | solution.py:300
  20.3 4.9 %factor_and_modes.1 = (f32[512,128]{1,0:T(8,128)}, f32[2,64,64]{2,1,0:T(8,128)}) custom-call(bf16[256,512]{1,0:T(8,128)(2,1)S(1)} %bitcast.4), custom_call_target="tpu_custom_call" | custom-call | tf_op jit(solution)/shard_map/factor_and_modes/pallas_call | solution.py:273

commit v10 on v8

--- a/solution.py
+++ b/solution.py
@@ -77,12 +77,9 @@
     for f in range(0, freqs, 2):
         pair = jnp.concatenate([rows_of(f), rows_of(f + 1)], 0)
         coef_ref[f * rows:(f + 2) * rows, :] = pair.astype(jnp.bfloat16)
-    total = jnp.zeros(out_ref.shape[1:], jnp.float32)
-    for copy, piece in zip(large, pieces):
+    for copy in large:
         copy.wait()
-        total += jnp.dot(
-            coef_ref[:, piece], snap_ref[piece], preferred_element_type=jnp.float32
-        )
+    total = jnp.dot(coef_ref[...], snap_ref[...], preferred_element_type=jnp.float32)
     result = total.astype(jnp.bfloat16)
     for copy in range(out_ref.shape[0]):
         out_ref[copy] = result
@@ -183,29 +180,34 @@
             for i in range(own, count)
         }
         here = raw[own]
+        pivot = over_rows(here[0][0], first % SUB)
         for c in range(panel):
             at = (first + c) % SUB
             here_row = sub == at
-            pivot = over_rows(here[c][0], at)
             inverse = pl.reciprocal(pivot, approx=True)
-            m_re = jnp.where(here_row, -inverse, here[c][0] * inverse)
-            m_im = jnp.where(here_row, 0.0, here[c][1] * inverse)
+            m_re = jnp.where(here_row, -1.0, here[c][0])
+            m_im = jnp.where(here_row, 0.0, here[c][1])
             if first % SUB:
                 m_re = jnp.where(sub < first % SUB, 0.0, m_re)
                 m_im = jnp.where(sub < first % SUB, 0.0, m_im)
+            m_re, m_im = m_re * inverse, m_im * inverse
             final[own] = jnp.where(here_row, head, final[own])
             pivots[own] = jnp.where(here_row, pivot, pivots[own])
             for later in range(c + 1, panel):
                 re, im = here[later]
                 u_re, u_im = over_rows(re, at), over_rows(im, at)
+                if later == c + 1:
+                    loss = (u_re * inverse) * u_re + (u_im * inverse) * u_im
+                    pivot = over_rows(re, at + 1) - loss
                 here[later] = (
-                    jnp.where(here_row, 0.0, re) - (m_re * u_re - m_im * u_im),
-                    jnp.where(here_row, 0.0, im) - (m_re * u_im + m_im * u_re),
+                    jnp.where(here_row, 0.0, re) - m_re * u_re + m_im * u_im,
+                    jnp.where(here_row, 0.0, im) - m_re * u_im - m_im * u_re,
                 )
             on_re, on_im = lane == columns[c], lane == columns[c] + 1
-            p = jnp.where(on_re, 1.0, jnp.where(on_im, 0.0, over_rows(head, at)))
-            q = jnp.where(on_im, 1.0, jnp.where(on_re, 0.0, over_rows(turned, at)))
-            cleared = here_row | ((on_re | on_im) & (sub >= first % SUB))
+            on_pair = on_re | on_im
+            p = jnp.where(on_pair, on_re.astype(jnp.float32), over_rows(head, at))
+            q = jnp.where(on_pair, on_im.astype(jnp.float32), over_rows(turned, at))
+            cleared = here_row | (on_pair & (sub >= first % SUB))
             head = jnp.where(cleared, 0.0, head) - (m_re * p + m_im * q)
             turned = jnp.where(cleared, 0.0, turned) - (m_re * q - m_im * p)
         rows[own] = head

time: 24 us -> 23.7 us (0.987)
  Pallas kernels: 5.83 us -> 5.49 us
where the time goes in v10:
time: 23.7 us; the launch traced here: 23.5 us
  blocking collectives  17.4 us (73%)
  Pallas kernels  5.49 us (23%)
  between operations  0.64 us (3%)
    all_to_all x1, blocking collectives, local(): x = swap(chunks, ('space', 'blk')).reshape(-1, points)  17.4 us
    pallas_call x1, Pallas kernels, modes_and_factor(): pl.pallas_call(functools.partial(modes_kernel, scale, slabs), out_shape=(...  3.78 us
    pallas_call x1, Pallas kernels, block_spectra(): pl.pallas_call(spectra_kernel, out_shape=jax.ShapeDtypeStruct((copies, ro...  1.71 us

profile of v10, /device:TPU:0, one launch (start us, length us, event | category | flops | bytes accessed | tf_op | source)
XLA Modules:
  0.0 23.5 jit_solution(18280646918642206057)
XLA Ops:
  0.6 1.7 %spectra.1 = bf16[2,128,512]{2,1,0:T(8,128)(2,1)S(1)} custom-call(bf16[1280,512]{1,0:T(8,128)(2,1)} %snap_hbm.1, f32[1280]{0:T(1024)} %scales_hbm.1, s32[4]{0:T(128)} %offsets_hbm.1, s32[16]{0:T(128)} %freq_hbm.1), custom_call_target="tpu_custom_call" | custom-call | tf_op jit(solution)/shard_map/spectra/pallas_call | solution.py:92
  2.4 17.4 %all_to_all.5 = bf16[32,8,512]{2,1,0:T(8,128)(2,1)S(1)} all-to-all(bf16[32,8,512]{2,1,0:T(8,128)(2,1)S(1)} %bitcast.5), channel_id=1, replica_groups=mesh['space'=2,'blk'=16] {'space','blk'}, dimensions={0} | all-to-all | bytes 524288 | tf_op jit(solution)/shard_map/all_to_all | solution.py:295
  19.7 3.8 %factor_and_modes.1 = (f32[512,128]{1,0:T(8,128)}, f32[2,64,64]{2,1,0:T(8,128)}) custom-call(bf16[256,512]{1,0:T(8,128)(2,1)S(1)} %bitcast.4), custom_call_target="tpu_custom_call" | custom-call | tf_op jit(solution)/shard_map/factor_and_modes/pallas_call | solution.py:269

commit v11 on v10

--- a/solution.py
+++ b/solution.py
@@ -12,6 +12,7 @@
 PANEL = 8
 SUB = 8
 PIECE = 256
+PARTS = 4
 FEW_SLABS = 2
 SIN_COEFS = (
     0.9999999765895043,
@@ -168,12 +169,14 @@
 
     rows = list(rows)
     final = [None] * count
+    final_turned = [None] * count
     pivots = [None] * count
     for first in range(0, count * SUB, panel):
         own = first // SUB
         head, turned = rows[own], rotated(rows[own], lane)
         if first % SUB == 0:
-            final[own], pivots[own] = head, jnp.ones(shape, jnp.float32)
+            final[own], final_turned[own] = head, turned
+            pivots[own] = jnp.ones(shape, jnp.float32)
         columns = [2 * (first + c) for c in range(panel)]
         raw = {
             i: [(over_lanes(rows[i], at), over_lanes(rows[i], at + 1)) for at in columns]
@@ -192,6 +195,7 @@
                 m_im = jnp.where(sub < first % SUB, 0.0, m_im)
             m_re, m_im = m_re * inverse, m_im * inverse
             final[own] = jnp.where(here_row, head, final[own])
+            final_turned[own] = jnp.where(here_row, turned, final_turned[own])
             pivots[own] = jnp.where(here_row, pivot, pivots[own])
             for later in range(c + 1, panel):
                 re, im = here[later]
@@ -220,11 +224,11 @@
             rows[i] = jnp.where(inside, 0.0, rows[i]) - tree_sum(
                 [re * p + im * q for (re, im), (p, q) in zip(raw[i], solved)]
             )
-    return final, pivots
+    return final, final_turned, pivots
 
 
 def modes_kernel(scale, slabs, x_ref, *refs):
-    *given, modes_ref, factor_ref, basis_ref, points_ref = refs
+    *given, modes_hbm, factor_hbm, basis_ref, points_ref, modes_ref, factor_ref, sems = refs
     width = basis_ref.shape[0]
     size = width // 2
     count = size // SUB
@@ -238,7 +242,7 @@
     points = jnp.transpose(mine)
     points_ref[...] = jnp.concatenate([points, points], 1)
     gram = gram * scale
-    rows, pivots = eliminate([gram[i * SUB:(i + 1) * SUB] for i in range(count)], PANEL)
+    rows, turned, pivots = eliminate([gram[i * SUB:(i + 1) * SUB] for i in range(count)], PANEL)
     shape = rows[0].shape
     sub = lax.broadcasted_iota(jnp.int32, shape, 0)
     lane = lax.broadcasted_iota(jnp.int32, shape, 1)
@@ -247,20 +251,31 @@
         own_rows = slice(i * SUB, (i + 1) * SUB)
         root = lax.rsqrt(pivots[i])
         diagonal = 2 * (i * SUB + sub)
-        left = jnp.where(lane < diagonal, rows[i], jnp.where(lane == diagonal, 1.0, 0.0)) * root
-        basis_ref[pl.ds(2 * i * SUB, SUB, stride=2), :] = left
-        basis_ref[pl.ds(2 * i * SUB + 1, SUB, stride=2), :] = rotated(left, lane)
+        left = jnp.where(lane < diagonal, rows[i], (lane == diagonal).astype(jnp.float32))
+        aside = jnp.where(lane < diagonal, turned[i], (lane == diagonal + 1).astype(jnp.float32))
+        basis_ref[pl.ds(2 * i * SUB, SUB, stride=2), :] = left * root
+        basis_ref[pl.ds(2 * i * SUB + 1, SUB, stride=2), :] = aside * root
         right = jnp.where(lane > diagonal + 1, rows[i], jnp.where(lane == diagonal, pivots[i], 0.0))
         parts = jnp.take_along_axis(right * root, pick, axis=1)
         factor_ref[0, own_rows, :] = parts[:, :size]
         factor_ref[1, own_rows, :] = parts[:, size:]
+    copies = [pltpu.make_async_copy(factor_ref, factor_hbm, sems.at[0])]
+    copies[0].start()
     basis = basis_ref[...]
     high = basis.astype(jnp.bfloat16)
     low = (basis - high.astype(jnp.float32)).astype(jnp.bfloat16)
-    modes_ref[...] = lax.dot_general(
-        points_ref[...], jnp.concatenate([high, low], 1), (((1,), (1,)), ((), ())),
-        preferred_element_type=jnp.float32,
-    )
+    terms = jnp.concatenate([high, low], 1)
+    each = modes_ref.shape[0] // PARTS
+    for i in range(PARTS):
+        part = slice(i * each, (i + 1) * each)
+        modes_ref[part] = lax.dot_general(
+            points_ref[part], terms, (((1,), (1,)), ((), ())),
+            preferred_element_type=jnp.float32,
+        )
+        copies.append(pltpu.make_async_copy(modes_ref.at[part], modes_hbm.at[part], sems.at[1 + i]))
+        copies[-1].start()
+    for copy in copies:
+        copy.wait()
 
 
 def modes_and_factor(x, grams, width, slabs, scale):
@@ -273,10 +288,13 @@
             jax.ShapeDtypeStruct((2, size, size), jnp.float32),
         ),
         in_specs=[pl.BlockSpec(memory_space=pltpu.VMEM)] * (1 + len(grams)),
-        out_specs=(pl.BlockSpec(memory_space=pltpu.VMEM),) * 2,
+        out_specs=(pl.BlockSpec(memory_space=pltpu.HBM),) * 2,
         scratch_shapes=[
             pltpu.VMEM((width, width), jnp.float32),
             pltpu.VMEM((points, 2 * width), jnp.bfloat16),
+            pltpu.VMEM((points, width), jnp.float32),
+            pltpu.VMEM((2, size, size), jnp.float32),
+            pltpu.SemaphoreType.DMA((1 + PARTS,)),
         ],
         compiler_params=pltpu.CompilerParams(vmem_limit_bytes=8 * 2**20),
         name="factor_and_modes",

time: 23.7 us -> 23.6 us (level)
  no operation moved by 1% of the time
where the time goes in v11:
time: 23.6 us; the launch traced here: 23.5 us
  blocking collectives  17.4 us (74%)
  Pallas kernels  5.43 us (23%)
  between operations  0.64 us (3%)
    all_to_all x1, blocking collectives, local(): x = swap(chunks, ('space', 'blk')).reshape(-1, points)  17.4 us
    pallas_call x1, Pallas kernels, modes_and_factor(): pl.pallas_call(functools.partial(modes_kernel, scale, slabs), out_shape=(...  3.72 us
    pallas_call x1, Pallas kernels, block_spectra(): pl.pallas_call(spectra_kernel, out_shape=jax.ShapeDtypeStruct((copies, ro...  1.71 us

profile of v11, /device:TPU:0, one launch (start us, length us, event | category | flops | bytes accessed | tf_op | source)
XLA Modules:
  0.0 23.5 jit_solution(6423331577908105515)
XLA Ops:
  0.6 1.7 %spectra.1 = bf16[2,128,512]{2,1,0:T(8,128)(2,1)S(1)} custom-call(bf16[1280,512]{1,0:T(8,128)(2,1)} %snap_hbm.1, f32[1280]{0:T(1024)} %scales_hbm.1, s32[4]{0:T(128)} %offsets_hbm.1, s32[16]{0:T(128)} %freq_hbm.1), custom_call_target="tpu_custom_call" | custom-call | tf_op jit(solution)/shard_map/spectra/pallas_call | solution.py:93
  2.4 17.4 %all_to_all.5 = bf16[32,8,512]{2,1,0:T(8,128)(2,1)S(1)} all-to-all(bf16[32,8,512]{2,1,0:T(8,128)(2,1)S(1)} %bitcast.5), channel_id=1, replica_groups=mesh['space'=2,'blk'=16] {'space','blk'}, dimensions={0} | all-to-all | bytes 524288 | tf_op jit(solution)/shard_map/all_to_all | solution.py:313
  19.7 3.7 %factor_and_modes.1 = (f32[512,128]{1,0:T(8,128)}, f32[2,64,64]{2,1,0:T(8,128)}) custom-call(bf16[256,512]{1,0:T(8,128)(2,1)S(1)} %bitcast.4), custom_call_target="tpu_custom_call" | custom-call | tf_op jit(solution)/shard_map/factor_and_modes/pallas_call | solution.py:284

commit v12 on v11

--- a/solution.py
+++ b/solution.py
@@ -9,7 +9,6 @@
 from jax.sharding import PartitionSpec as P
 
 NFFT = 512
-PANEL = 8
 SUB = 8
 PIECE = 256
 PARTS = 4
@@ -155,7 +154,15 @@
     return terms[0]
 
 
-def eliminate(rows, panel):
+def times(a, b):
+    return a[0] * b[0] - a[1] * b[1], a[0] * b[1] + a[1] * b[0]
+
+
+def conj_times(a, b):
+    return a[0] * b[0] + a[1] * b[1], a[0] * b[1] - a[1] * b[0]
+
+
+def eliminate(rows):
     count = len(rows)
     shape = rows[0].shape
     sub = lax.broadcasted_iota(jnp.int32, shape, 0)
@@ -167,64 +174,92 @@
     def over_rows(x, at):
         return jnp.broadcast_to(x[at:at + 1, :], shape)
 
+    def entry(column, at):
+        return over_rows(column[0], at), over_rows(column[1], at)
+
     rows = list(rows)
-    final = [None] * count
-    final_turned = [None] * count
-    pivots = [None] * count
-    for first in range(0, count * SUB, panel):
-        own = first // SUB
+    final, final_turned, pivots = [], [], []
+    for own in range(count):
         head, turned = rows[own], rotated(rows[own], lane)
-        if first % SUB == 0:
-            final[own], final_turned[own] = head, turned
-            pivots[own] = jnp.ones(shape, jnp.float32)
-        columns = [2 * (first + c) for c in range(panel)]
+        keep, keep_turned, keep_pivot = head, turned, jnp.ones(shape, jnp.float32)
+        columns = [2 * (own * SUB + c) for c in range(SUB)]
         raw = {
             i: [(over_lanes(rows[i], at), over_lanes(rows[i], at + 1)) for at in columns]
             for i in range(own, count)
         }
         here = raw[own]
-        pivot = over_rows(here[0][0], first % SUB)
-        for c in range(panel):
-            at = (first + c) % SUB
-            here_row = sub == at
-            inverse = pl.reciprocal(pivot, approx=True)
-            m_re = jnp.where(here_row, -1.0, here[c][0])
-            m_im = jnp.where(here_row, 0.0, here[c][1])
-            if first % SUB:
-                m_re = jnp.where(sub < first % SUB, 0.0, m_re)
-                m_im = jnp.where(sub < first % SUB, 0.0, m_im)
-            m_re, m_im = m_re * inverse, m_im * inverse
-            final[own] = jnp.where(here_row, head, final[own])
-            final_turned[own] = jnp.where(here_row, turned, final_turned[own])
-            pivots[own] = jnp.where(here_row, pivot, pivots[own])
-            for later in range(c + 1, panel):
-                re, im = here[later]
-                u_re, u_im = over_rows(re, at), over_rows(im, at)
-                if later == c + 1:
-                    loss = (u_re * inverse) * u_re + (u_im * inverse) * u_im
-                    pivot = over_rows(re, at + 1) - loss
-                here[later] = (
-                    jnp.where(here_row, 0.0, re) - m_re * u_re + m_im * u_im,
-                    jnp.where(here_row, 0.0, im) - m_re * u_im - m_im * u_re,
+        ahead = over_rows(here[0][0], 0), over_rows(here[1][0], 1), entry(here[1], 0)
+        for pair in range(0, SUB, 2):
+            first, second, u = ahead
+            square = u[0] * u[0] + u[1] * u[1]
+            inverse = pl.reciprocal(first, approx=True)
+            inverses = inverse, first * pl.reciprocal(first * second - square, approx=True)
+            values = first, second - square * inverse
+            uppers = [{c: entry(here[c], pair) for c in range(pair + 1, SUB)}, {}]
+            for c in range(pair + 2, SUB):
+                old, loss = entry(here[c], pair + 1), conj_times(u, uppers[0][c])
+                uppers[1][c] = old[0] - loss[0] * inverse, old[1] - loss[1] * inverse
+            if pair + 2 < SUB:
+                one, two = pair + 2, pair + 3
+                parts = [
+                    (conj_times(up[one], up[one])[0], conj_times(up[two], up[two])[0], conj_times(up[one], up[two]))
+                    for up in uppers
+                ]
+                next_u = entry(here[two], one)
+                (a1, a2, au), (b1, b2, bu) = parts
+                ahead = (
+                    (over_rows(here[one][0], one) - a1 * inverse) - b1 * inverses[1],
+                    (over_rows(here[two][0], two) - a2 * inverse) - b2 * inverses[1],
+                    tuple(
+                        (next_u[k] - au[k] * inverse) - bu[k] * inverses[1] for k in range(2)
+                    ),
                 )
-            on_re, on_im = lane == columns[c], lane == columns[c] + 1
-            on_pair = on_re | on_im
-            p = jnp.where(on_pair, on_re.astype(jnp.float32), over_rows(head, at))
-            q = jnp.where(on_pair, on_im.astype(jnp.float32), over_rows(turned, at))
-            cleared = here_row | (on_pair & (sub >= first % SUB))
-            head = jnp.where(cleared, 0.0, head) - (m_re * p + m_im * q)
-            turned = jnp.where(cleared, 0.0, turned) - (m_re * q - m_im * p)
-        rows[own] = head
-        inside = (lane >= columns[0]) & (lane < columns[0] + 2 * panel)
-        solved = [
-            (over_rows(head, (first + c) % SUB), over_rows(turned, (first + c) % SUB))
-            for c in range(panel)
-        ]
+            for c in (pair, pair + 1):
+                here_row = sub == c
+                m_re = jnp.where(here_row, -1.0, here[c][0]) * inverses[c - pair]
+                m_im = jnp.where(here_row, 0.0, here[c][1]) * inverses[c - pair]
+                keep = jnp.where(here_row, head, keep)
+                keep_turned = jnp.where(here_row, turned, keep_turned)
+                keep_pivot = jnp.where(here_row, values[c - pair], keep_pivot)
+                for later, (u_re, u_im) in uppers[c - pair].items():
+                    re, im = here[later]
+                    here[later] = (
+                        jnp.where(here_row, 0.0, re) - m_re * u_re + m_im * u_im,
+                        jnp.where(here_row, 0.0, im) - m_re * u_im - m_im * u_re,
+                    )
+                on_re, on_im = lane == columns[c], lane == columns[c] + 1
+                on_pair = on_re | on_im
+                p = jnp.where(on_pair, on_re.astype(jnp.float32), over_rows(head, c))
+                q = jnp.where(on_pair, on_im.astype(jnp.float32), over_rows(turned, c))
+                cleared = here_row | on_pair
+                head = jnp.where(cleared, 0.0, head) - (m_re * p + m_im * q)
+                turned = jnp.where(cleared, 0.0, turned) - (m_re * q - m_im * p)
+        final.append(keep)
+        final_turned.append(keep_turned)
+        pivots.append(keep_pivot)
+        inside = (lane >= columns[0]) & (lane < columns[0] + 2 * SUB)
+        solved = [(over_rows(head, c), over_rows(turned, c)) for c in range(SUB)]
         for i in range(own + 1, count):
             rows[i] = jnp.where(inside, 0.0, rows[i]) - tree_sum(
                 [re * p + im * q for (re, im), (p, q) in zip(raw[i], solved)]
             )
     return final, final_turned, pivots
+
+
+def unit_diagonal(rows):
+    shape = rows[0].shape
+    sub = lax.broadcasted_iota(jnp.int32, shape, 0)
+    lane = lax.broadcasted_iota(jnp.int32, shape, 1)
+    diagonals = [jnp.where(lane == 2 * (i * SUB + sub), row, 0.0) for i, row in enumerate(rows)]
+    across = jnp.sum(tree_sum(diagonals), axis=0, keepdims=True)
+    across = jnp.broadcast_to(across, shape)
+    across = across + pltpu.roll(across, 1, 1)
+    root = lax.rsqrt(across)
+    scaled = [
+        row * lax.rsqrt(jnp.sum(diagonal, axis=1, keepdims=True)) * root
+        for row, diagonal in zip(rows, diagonals)
+    ]
+    return scaled, root, across * root
 
 
 def modes_kernel(scale, slabs, x_ref, *refs):
@@ -241,8 +276,9 @@
         mine = x_ref[pl.ds(pl.multiple_of(own * width, width), width)]
     points = jnp.transpose(mine)
     points_ref[...] = jnp.concatenate([points, points], 1)
-    gram = gram * scale
-    rows, turned, pivots = eliminate([gram[i * SUB:(i + 1) * SUB] for i in range(count)], PANEL)
+    rows, shrink, grow = unit_diagonal([gram[i * SUB:(i + 1) * SUB] for i in range(count)])
+    shrink, grow = shrink * (1.0 / math.sqrt(scale)), grow * math.sqrt(scale)
+    rows, turned, pivots = eliminate(rows)
     shape = rows[0].shape
     sub = lax.broadcasted_iota(jnp.int32, shape, 0)
     lane = lax.broadcasted_iota(jnp.int32, shape, 1)
@@ -253,10 +289,10 @@
         diagonal = 2 * (i * SUB + sub)
         left = jnp.where(lane < diagonal, rows[i], (lane == diagonal).astype(jnp.float32))
         aside = jnp.where(lane < diagonal, turned[i], (lane == diagonal + 1).astype(jnp.float32))
-        basis_ref[pl.ds(2 * i * SUB, SUB, stride=2), :] = left * root
-        basis_ref[pl.ds(2 * i * SUB + 1, SUB, stride=2), :] = aside * root
+        basis_ref[pl.ds(2 * i * SUB, SUB, stride=2), :] = left * (root * shrink)
+        basis_ref[pl.ds(2 * i * SUB + 1, SUB, stride=2), :] = aside * (root * shrink)
         right = jnp.where(lane > diagonal + 1, rows[i], jnp.where(lane == diagonal, pivots[i], 0.0))
-        parts = jnp.take_along_axis(right * root, pick, axis=1)
+        parts = jnp.take_along_axis(right * (root * grow), pick, axis=1)
         factor_ref[0, own_rows, :] = parts[:, :size]
         factor_ref[1, own_rows, :] = parts[:, size:]
     copies = [pltpu.make_async_copy(factor_ref, factor_hbm, sems.at[0])]

time: 23.6 us -> 24 us (1.017)
  Pallas kernels: 5.43 us -> 5.79 us
    pallas_call x1, Pallas kernels: 3.72 us -> 4.07 us  [modes_and_factor(): pl.pallas_call(functools.partial(modes_kernel, scale, slabs), out_shape=(...]
where the time goes in v12:
time: 24 us; the launch traced here: 23.8 us
  blocking collectives  17.4 us (72%)
  Pallas kernels  5.79 us (24%)
  between operations  0.64 us (3%)
    all_to_all x1, blocking collectives, local(): x = swap(chunks, ('space', 'blk')).reshape(-1, points)  17.4 us
    pallas_call x1, Pallas kernels, modes_and_factor(): pl.pallas_call(functools.partial(modes_kernel, scale, slabs), out_shape=(...  4.07 us
    pallas_call x1, Pallas kernels, block_spectra(): pl.pallas_call(spectra_kernel, out_shape=jax.ShapeDtypeStruct((copies, ro...  1.71 us

profile of v12, /device:TPU:0, one launch (start us, length us, event | category | flops | bytes accessed | tf_op | source)
XLA Modules:
  0.0 23.8 jit_solution(13822062373308581250)
XLA Ops:
  0.6 1.7 %spectra.1 = bf16[2,128,512]{2,1,0:T(8,128)(2,1)S(1)} custom-call(bf16[1280,512]{1,0:T(8,128)(2,1)} %snap_hbm.1, f32[1280]{0:T(1024)} %scales_hbm.1, s32[4]{0:T(128)} %offsets_hbm.1, s32[16]{0:T(128)} %freq_hbm.1), custom_call_target="tpu_custom_call" | custom-call | tf_op jit(solution)/shard_map/spectra/pallas_call | solution.py:92
  2.4 17.4 %all_to_all.5 = bf16[32,8,512]{2,1,0:T(8,128)(2,1)S(1)} all-to-all(bf16[32,8,512]{2,1,0:T(8,128)(2,1)S(1)} %bitcast.5), channel_id=1, replica_groups=mesh['space'=2,'blk'=16] {'space','blk'}, dimensions={0} | all-to-all | bytes 524288 | tf_op jit(solution)/shard_map/all_to_all | solution.py:349
  19.7 4.1 %factor_and_modes.1 = (f32[512,128]{1,0:T(8,128)}, f32[2,64,64]{2,1,0:T(8,128)}) custom-call(bf16[256,512]{1,0:T(8,128)(2,1)S(1)} %bitcast.4), custom_call_target="tpu_custom_call" | custom-call | tf_op jit(solution)/shard_map/factor_and_modes/pallas_call | solution.py:320

commit v13 on v11

--- a/solution.py
+++ b/solution.py
@@ -9,7 +9,6 @@
 from jax.sharding import PartitionSpec as P
 
 NFFT = 512
-PANEL = 8
 SUB = 8
 PIECE = 256
 PARTS = 4
@@ -155,7 +154,7 @@
     return terms[0]
 
 
-def eliminate(rows, panel):
+def eliminate(rows, solved_ref):
     count = len(rows)
     shape = rows[0].shape
     sub = lax.broadcasted_iota(jnp.int32, shape, 0)
@@ -168,67 +167,69 @@
         return jnp.broadcast_to(x[at:at + 1, :], shape)
 
     rows = list(rows)
-    final = [None] * count
-    final_turned = [None] * count
-    pivots = [None] * count
-    for first in range(0, count * SUB, panel):
-        own = first // SUB
+    final, final_turned, pivots = [], [], []
+    solved_ref[...] = jnp.zeros_like(solved_ref)
+    for own in range(count):
         head, turned = rows[own], rotated(rows[own], lane)
-        if first % SUB == 0:
-            final[own], final_turned[own] = head, turned
-            pivots[own] = jnp.ones(shape, jnp.float32)
-        columns = [2 * (first + c) for c in range(panel)]
+        keep, keep_turned, keep_pivot = head, turned, jnp.ones(shape, jnp.float32)
+        columns = [2 * (own * SUB + c) for c in range(SUB)]
         raw = {
             i: [(over_lanes(rows[i], at), over_lanes(rows[i], at + 1)) for at in columns]
-            for i in range(own, count)
+            for i in range(own, min(own + 2, count))
         }
         here = raw[own]
-        pivot = over_rows(here[0][0], first % SUB)
-        for c in range(panel):
-            at = (first + c) % SUB
-            here_row = sub == at
+        pivot = over_rows(here[0][0], 0)
+        for c in range(SUB):
+            here_row = sub == c
             inverse = pl.reciprocal(pivot, approx=True)
-            m_re = jnp.where(here_row, -1.0, here[c][0])
-            m_im = jnp.where(here_row, 0.0, here[c][1])
-            if first % SUB:
-                m_re = jnp.where(sub < first % SUB, 0.0, m_re)
-                m_im = jnp.where(sub < first % SUB, 0.0, m_im)
-            m_re, m_im = m_re * inverse, m_im * inverse
-            final[own] = jnp.where(here_row, head, final[own])
-            final_turned[own] = jnp.where(here_row, turned, final_turned[own])
-            pivots[own] = jnp.where(here_row, pivot, pivots[own])
-            for later in range(c + 1, panel):
+            m_re = jnp.where(here_row, -1.0, here[c][0]) * inverse
+            m_im = jnp.where(here_row, 0.0, here[c][1]) * inverse
+            keep = jnp.where(here_row, head, keep)
+            keep_turned = jnp.where(here_row, turned, keep_turned)
+            keep_pivot = jnp.where(here_row, pivot, keep_pivot)
+            for later in range(c + 1, SUB):
                 re, im = here[later]
-                u_re, u_im = over_rows(re, at), over_rows(im, at)
+                u_re, u_im = over_rows(re, c), over_rows(im, c)
                 if later == c + 1:
                     loss = (u_re * inverse) * u_re + (u_im * inverse) * u_im
-                    pivot = over_rows(re, at + 1) - loss
+                    pivot = over_rows(re, c + 1) - loss
                 here[later] = (
                     jnp.where(here_row, 0.0, re) - m_re * u_re + m_im * u_im,
                     jnp.where(here_row, 0.0, im) - m_re * u_im - m_im * u_re,
                 )
             on_re, on_im = lane == columns[c], lane == columns[c] + 1
             on_pair = on_re | on_im
-            p = jnp.where(on_pair, on_re.astype(jnp.float32), over_rows(head, at))
-            q = jnp.where(on_pair, on_im.astype(jnp.float32), over_rows(turned, at))
-            cleared = here_row | (on_pair & (sub >= first % SUB))
+            p = jnp.where(on_pair, on_re.astype(jnp.float32), over_rows(head, c))
+            q = jnp.where(on_pair, on_im.astype(jnp.float32), over_rows(turned, c))
+            cleared = here_row | on_pair
             head = jnp.where(cleared, 0.0, head) - (m_re * p + m_im * q)
             turned = jnp.where(cleared, 0.0, turned) - (m_re * q - m_im * p)
-        rows[own] = head
-        inside = (lane >= columns[0]) & (lane < columns[0] + 2 * panel)
-        solved = [
-            (over_rows(head, (first + c) % SUB), over_rows(turned, (first + c) % SUB))
-            for c in range(panel)
-        ]
-        for i in range(own + 1, count):
-            rows[i] = jnp.where(inside, 0.0, rows[i]) - tree_sum(
-                [re * p + im * q for (re, im), (p, q) in zip(raw[i], solved)]
+        final.append(keep)
+        final_turned.append(keep_turned)
+        pivots.append(keep_pivot)
+        if own + 1 == count:
+            break
+        inside = (lane >= columns[0]) & (lane < columns[0] + 2 * SUB)
+        solved = [(over_rows(head, c), over_rows(turned, c)) for c in range(SUB)]
+        rows[own + 1] = jnp.where(inside, 0.0, rows[own + 1]) - tree_sum(
+            [re * p + im * q for (re, im), (p, q) in zip(raw[own + 1], solved)]
+        )
+        far = range(own + 2, count)
+        if far:
+            solved_ref[pl.ds(columns[0], SUB, stride=2), :] = head
+            solved_ref[pl.ds(columns[0] + 1, SUB, stride=2), :] = turned
+            losses = jnp.dot(
+                jnp.concatenate([jnp.where(inside, rows[i], 0.0) for i in far], 0), solved_ref[...],
+                precision=lax.Precision.HIGHEST, preferred_element_type=jnp.float32,
             )
+            for at, i in enumerate(far):
+                loss = losses[at * SUB:(at + 1) * SUB]
+                rows[i] = jnp.where(inside, 0.0, rows[i]) - loss
     return final, final_turned, pivots
 
 
 def modes_kernel(scale, slabs, x_ref, *refs):
-    *given, modes_hbm, factor_hbm, basis_ref, points_ref, modes_ref, factor_ref, sems = refs
+    *given, modes_hbm, factor_hbm, basis_ref, solved_ref, points_ref, modes_ref, factor_ref, sems = refs
     width = basis_ref.shape[0]
     size = width // 2
     count = size // SUB
@@ -242,7 +243,7 @@
     points = jnp.transpose(mine)
     points_ref[...] = jnp.concatenate([points, points], 1)
     gram = gram * scale
-    rows, turned, pivots = eliminate([gram[i * SUB:(i + 1) * SUB] for i in range(count)], PANEL)
+    rows, turned, pivots = eliminate([gram[i * SUB:(i + 1) * SUB] for i in range(count)], solved_ref)
     shape = rows[0].shape
     sub = lax.broadcasted_iota(jnp.int32, shape, 0)
     lane = lax.broadcasted_iota(jnp.int32, shape, 1)
@@ -291,6 +292,7 @@
         out_specs=(pl.BlockSpec(memory_space=pltpu.HBM),) * 2,
         scratch_shapes=[
             pltpu.VMEM((width, width), jnp.float32),
+            pltpu.VMEM((width, width), jnp.float32),
             pltpu.VMEM((points, 2 * width), jnp.bfloat16),
             pltpu.VMEM((points, width), jnp.float32),
             pltpu.VMEM((2, size, size), jnp.float32),

time: 23.6 us -> 23.2 us (0.983)
  Pallas kernels: 5.43 us -> 4.99 us
    pallas_call x1, Pallas kernels: 3.72 us -> 3.28 us  [modes_and_factor(): pl.pallas_call(functools.partial(modes_kernel, scale, slabs), out_shape=(...]
where the time goes in v13:
time: 23.2 us; the launch traced here: 23 us
  blocking collectives  17.4 us (75%)
  Pallas kernels  4.99 us (22%)
  between operations  0.64 us (3%)
    all_to_all x1, blocking collectives, local(): x = swap(chunks, ('space', 'blk')).reshape(-1, points)  17.4 us
    pallas_call x1, Pallas kernels, modes_and_factor(): pl.pallas_call(functools.partial(modes_kernel, scale, slabs), out_shape=(...  3.28 us
    pallas_call x1, Pallas kernels, block_spectra(): pl.pallas_call(spectra_kernel, out_shape=jax.ShapeDtypeStruct((copies, ro...  1.71 us

profile of v13, /device:TPU:0, one launch (start us, length us, event | category | flops | bytes accessed | tf_op | source)
XLA Modules:
  0.0 23.0 jit_solution(5075185497125001092)
XLA Ops:
  0.6 1.7 %spectra.1 = bf16[2,128,512]{2,1,0:T(8,128)(2,1)S(1)} custom-call(bf16[1280,512]{1,0:T(8,128)(2,1)} %snap_hbm.1, f32[1280]{0:T(1024)} %scales_hbm.1, s32[4]{0:T(128)} %offsets_hbm.1, s32[16]{0:T(128)} %freq_hbm.1), custom_call_target="tpu_custom_call" | custom-call | tf_op jit(solution)/shard_map/spectra/pallas_call | solution.py:92
  2.4 17.4 %all_to_all.5 = bf16[32,8,512]{2,1,0:T(8,128)(2,1)S(1)} all-to-all(bf16[32,8,512]{2,1,0:T(8,128)(2,1)S(1)} %bitcast.5), channel_id=1, replica_groups=mesh['space'=2,'blk'=16] {'space','blk'}, dimensions={0} | all-to-all | bytes 524288 | tf_op jit(solution)/shard_map/all_to_all | solution.py:315
  19.7 3.3 %factor_and_modes.1 = (f32[512,128]{1,0:T(8,128)}, f32[2,64,64]{2,1,0:T(8,128)}) custom-call(bf16[256,512]{1,0:T(8,128)(2,1)S(1)} %bitcast.4), custom_call_target="tpu_custom_call" | custom-call | tf_op jit(solution)/shard_map/factor_and_modes/pallas_call | solution.py:285

commit v14 on v13

--- a/solution.py
+++ b/solution.py
@@ -154,7 +154,7 @@
     return terms[0]
 
 
-def eliminate(rows, solved_ref):
+def eliminate(rows, solved_ref, step_ref):
     count = len(rows)
     shape = rows[0].shape
     sub = lax.broadcasted_iota(jnp.int32, shape, 0)
@@ -166,9 +166,11 @@
     def over_rows(x, at):
         return jnp.broadcast_to(x[at:at + 1, :], shape)
 
+    def row_of(ref, *at):
+        return ref[(*at[:-1], pl.ds(at[-1], SUB, stride=0), slice(None))]
+
     rows = list(rows)
     final, final_turned, pivots = [], [], []
-    solved_ref[...] = jnp.zeros_like(solved_ref)
     for own in range(count):
         head, turned = rows[own], rotated(rows[own], lane)
         keep, keep_turned, keep_pivot = head, turned, jnp.ones(shape, jnp.float32)
@@ -199,8 +201,10 @@
                 )
             on_re, on_im = lane == columns[c], lane == columns[c] + 1
             on_pair = on_re | on_im
-            p = jnp.where(on_pair, on_re.astype(jnp.float32), over_rows(head, c))
-            q = jnp.where(on_pair, on_im.astype(jnp.float32), over_rows(turned, c))
+            step_ref[c, :SUB, :] = head
+            step_ref[c, SUB:, :] = turned
+            p = jnp.where(on_pair, on_re.astype(jnp.float32), row_of(step_ref, c, c))
+            q = jnp.where(on_pair, on_im.astype(jnp.float32), row_of(step_ref, c, SUB + c))
             cleared = here_row | on_pair
             head = jnp.where(cleared, 0.0, head) - (m_re * p + m_im * q)
             turned = jnp.where(cleared, 0.0, turned) - (m_re * q - m_im * p)
@@ -210,16 +214,17 @@
         if own + 1 == count:
             break
         inside = (lane >= columns[0]) & (lane < columns[0] + 2 * SUB)
+        solved_ref[own, pl.ds(0, SUB, stride=2), :] = head
+        solved_ref[own, pl.ds(1, SUB, stride=2), :] = turned
         solved = [(over_rows(head, c), over_rows(turned, c)) for c in range(SUB)]
         rows[own + 1] = jnp.where(inside, 0.0, rows[own + 1]) - tree_sum(
             [re * p + im * q for (re, im), (p, q) in zip(raw[own + 1], solved)]
         )
         far = range(own + 2, count)
         if far:
-            solved_ref[pl.ds(columns[0], SUB, stride=2), :] = head
-            solved_ref[pl.ds(columns[0] + 1, SUB, stride=2), :] = turned
+            below = jnp.concatenate([rows[i] for i in far], 0)
             losses = jnp.dot(
-                jnp.concatenate([jnp.where(inside, rows[i], 0.0) for i in far], 0), solved_ref[...],
+                below[:, columns[0]:columns[0] + 2 * SUB], solved_ref[own],
                 precision=lax.Precision.HIGHEST, preferred_element_type=jnp.float32,
             )
             for at, i in enumerate(far):
@@ -229,7 +234,7 @@
 
 
 def modes_kernel(scale, slabs, x_ref, *refs):
-    *given, modes_hbm, factor_hbm, basis_ref, solved_ref, points_ref, modes_ref, factor_ref, sems = refs
+    *given, modes_hbm, factor_hbm, basis_ref, solved_ref, step_ref, points_ref, modes_ref, factor_ref, sems = refs
     width = basis_ref.shape[0]
     size = width // 2
     count = size // SUB
@@ -243,7 +248,7 @@
     points = jnp.transpose(mine)
     points_ref[...] = jnp.concatenate([points, points], 1)
     gram = gram * scale
-    rows, turned, pivots = eliminate([gram[i * SUB:(i + 1) * SUB] for i in range(count)], solved_ref)
+    rows, turned, pivots = eliminate([gram[i * SUB:(i + 1) * SUB] for i in range(count)], solved_ref, step_ref)
     shape = rows[0].shape
     sub = lax.broadcasted_iota(jnp.int32, shape, 0)
     lane = lax.broadcasted_iota(jnp.int32, shape, 1)
@@ -292,7 +297,8 @@
         out_specs=(pl.BlockSpec(memory_space=pltpu.HBM),) * 2,
         scratch_shapes=[
             pltpu.VMEM((width, width), jnp.float32),
-            pltpu.VMEM((width, width), jnp.float32),
+            pltpu.VMEM((size // SUB, 2 * SUB, width), jnp.float32),
+            pltpu.VMEM((SUB, 2 * SUB, width), jnp.float32),
             pltpu.VMEM((points, 2 * width), jnp.bfloat16),
             pltpu.VMEM((points, width), jnp.float32),
             pltpu.VMEM((2, size, size), jnp.float32),

time: 23.2 us -> 23.2 us (level)
  no operation moved by 1% of the time
where the time goes in v14:
time: 23.2 us; the launch traced here: 23 us
  blocking collectives  17.4 us (75%)
  Pallas kernels  5.01 us (22%)
  between operations  0.64 us (3%)
    all_to_all x1, blocking collectives, local(): x = swap(chunks, ('space', 'blk')).reshape(-1, points)  17.4 us
    pallas_call x1, Pallas kernels, modes_and_factor(): pl.pallas_call(functools.partial(modes_kernel, scale, slabs), out_shape=(...  3.3 us
    pallas_call x1, Pallas kernels, block_spectra(): pl.pallas_call(spectra_kernel, out_shape=jax.ShapeDtypeStruct((copies, ro...  1.71 us

profile of v14, /device:TPU:0, one launch (start us, length us, event | category | flops | bytes accessed | tf_op | source)
XLA Modules:
  0.0 23.0 jit_solution(13314406489171725129)
XLA Ops:
  0.6 1.7 %spectra.1 = bf16[2,128,512]{2,1,0:T(8,128)(2,1)S(1)} custom-call(bf16[1280,512]{1,0:T(8,128)(2,1)} %snap_hbm.1, f32[1280]{0:T(1024)} %scales_hbm.1, s32[4]{0:T(128)} %offsets_hbm.1, s32[16]{0:T(128)} %freq_hbm.1), custom_call_target="tpu_custom_call" | custom-call | tf_op jit(solution)/shard_map/spectra/pallas_call | solution.py:92
  2.4 17.4 %all_to_all.5 = bf16[32,8,512]{2,1,0:T(8,128)(2,1)S(1)} all-to-all(bf16[32,8,512]{2,1,0:T(8,128)(2,1)S(1)} %bitcast.5), channel_id=1, replica_groups=mesh['space'=2,'blk'=16] {'space','blk'}, dimensions={0} | all-to-all | bytes 524288 | tf_op jit(solution)/shard_map/all_to_all | solution.py:321
  19.7 3.3 %factor_and_modes.1 = (f32[512,128]{1,0:T(8,128)}, f32[2,64,64]{2,1,0:T(8,128)}) custom-call(bf16[256,512]{1,0:T(8,128)(2,1)S(1)} %bitcast.4), custom_call_target="tpu_custom_call" | custom-call | tf_op jit(solution)/shard_map/factor_and_modes/pallas_call | solution.py:290

commit v15 on v14

--- a/solution.py
+++ b/solution.py
@@ -10,7 +10,7 @@
 
 NFFT = 512
 SUB = 8
-PIECE = 256
+PIECE = 640
 PARTS = 4
 FEW_SLABS = 2
 SIN_COEFS = (
@@ -65,14 +65,22 @@
     inside = (shifted >= 0) & (shifted < NFFT)
     scales = jnp.broadcast_to(scales_ref[...].reshape(1, snaps), (rows, snaps))
     weight = jnp.where(inside, hann * scales * (1.0 / math.sqrt(NFFT)), 0.0)
-    base = shifted[:, :NFFT].astype(jnp.float32)
-    quarter = (row[:, :NFFT] % 2) * (NFFT // 4)
+    quarter = NFFT // 4
+    base = shifted[:, :quarter].astype(jnp.float32)
+    turn = (row[:, :quarter] % 2) * quarter
     repeats = -(-snaps // NFFT)
 
     def rows_of(f):
-        freq = freq_ref[f].astype(jnp.float32)
-        table = cos_of_phase((base * freq).astype(jnp.int32) + quarter)
-        return jnp.concatenate([table] * repeats, 1)[:, :snaps] * weight
+        freq = freq_ref[f]
+        phase = (base * freq.astype(jnp.float32)).astype(jnp.int32) + turn
+        even, odd = cos_of_phase(phase), cos_of_phase(phase + quarter)
+        tiles = [even]
+        for j in range(1, 4):
+            turns = (freq * j) & 3
+            along = ((1 - (turns & 1)) * (1 - turns)).astype(jnp.float32)
+            across = ((turns & 1) * (2 - turns)).astype(jnp.float32)
+            tiles.append(even * along + odd * across)
+        return jnp.concatenate(tiles * repeats, 1)[:, :snaps] * weight
 
     for f in range(0, freqs, 2):
         pair = jnp.concatenate([rows_of(f), rows_of(f + 1)], 0)

time: 23.2 us -> 23.2 us (level)
  no operation moved by 1% of the time
where the time goes in v15:
time: 23.2 us; the launch traced here: 23 us
  blocking collectives  17.4 us (75%)
  Pallas kernels  4.99 us (22%)
  between operations  0.64 us (3%)
    all_to_all x1, blocking collectives, local(): x = swap(chunks, ('space', 'blk')).reshape(-1, points)  17.4 us
    pallas_call x1, Pallas kernels, modes_and_factor(): pl.pallas_call(functools.partial(modes_kernel, scale, slabs), out_shape=(...  3.3 us
    pallas_call x1, Pallas kernels, block_spectra(): pl.pallas_call(spectra_kernel, out_shape=jax.ShapeDtypeStruct((copies, ro...  1.69 us

profile of v15, /device:TPU:0, one launch (start us, length us, event | category | flops | bytes accessed | tf_op | source)
XLA Modules:
  0.0 23.0 jit_solution(15217974582928907375)
XLA Ops:
  0.6 1.7 %spectra.1 = bf16[2,128,512]{2,1,0:T(8,128)(2,1)S(1)} custom-call(bf16[1280,512]{1,0:T(8,128)(2,1)} %snap_hbm.1, f32[1280]{0:T(1024)} %scales_hbm.1, s32[4]{0:T(128)} %offsets_hbm.1, s32[16]{0:T(128)} %freq_hbm.1), custom_call_target="tpu_custom_call" | custom-call | tf_op jit(solution)/shard_map/spectra/pallas_call | solution.py:100
  2.3 17.4 %all_to_all.5 = bf16[32,8,512]{2,1,0:T(8,128)(2,1)S(1)} all-to-all(bf16[32,8,512]{2,1,0:T(8,128)(2,1)S(1)} %bitcast.5), channel_id=1, replica_groups=mesh['space'=2,'blk'=16] {'space','blk'}, dimensions={0} | all-to-all | bytes 524288 | tf_op jit(solution)/shard_map/all_to_all | solution.py:329
  19.7 3.3 %factor_and_modes.1 = (f32[512,128]{1,0:T(8,128)}, f32[2,64,64]{2,1,0:T(8,128)}) custom-call(bf16[256,512]{1,0:T(8,128)(2,1)S(1)} %bitcast.4), custom_call_target="tpu_custom_call" | custom-call | tf_op jit(solution)/shard_map/factor_and_modes/pallas_call | solution.py:298

commit v16 on v15

--- a/solution.py
+++ b/solution.py
@@ -10,7 +10,7 @@
 
 NFFT = 512
 SUB = 8
-PIECE = 640
+PIECE = 768
 PARTS = 4
 FEW_SLABS = 2
 SIN_COEFS = (
@@ -85,9 +85,13 @@
     for f in range(0, freqs, 2):
         pair = jnp.concatenate([rows_of(f), rows_of(f + 1)], 0)
         coef_ref[f * rows:(f + 2) * rows, :] = pair.astype(jnp.bfloat16)
-    for copy in large:
+    parts = []
+    for copy, piece in zip(large, pieces):
         copy.wait()
-    total = jnp.dot(coef_ref[...], snap_ref[...], preferred_element_type=jnp.float32)
+        parts.append(
+            jnp.dot(coef_ref[:, piece], snap_ref[piece], preferred_element_type=jnp.float32)
+        )
+    total = sum(parts[1:], parts[0])
     result = total.astype(jnp.bfloat16)
     for copy in range(out_ref.shape[0]):
         out_ref[copy] = result
@@ -162,6 +166,10 @@
     return terms[0]
 
 
+def conj_times(a, b):
+    return a[0] * b[0] + a[1] * b[1], a[0] * b[1] - a[1] * b[0]
+
+
 def eliminate(rows, solved_ref, step_ref):
     count = len(rows)
     shape = rows[0].shape
@@ -173,6 +181,9 @@
 
     def over_rows(x, at):
         return jnp.broadcast_to(x[at:at + 1, :], shape)
+
+    def entry(column, at):
+        return over_rows(column[0], at), over_rows(column[1], at)
 
     def row_of(ref, *at):
         return ref[(*at[:-1], pl.ds(at[-1], SUB, stride=0), slice(None))]
@@ -188,21 +199,40 @@
             for i in range(own, min(own + 2, count))
         }
         here = raw[own]
-        pivot = over_rows(here[0][0], 0)
+        ahead = over_rows(here[0][0], 0), over_rows(here[1][0], 1), entry(here[1], 0)
         for c in range(SUB):
             here_row = sub == c
-            inverse = pl.reciprocal(pivot, approx=True)
-            m_re = jnp.where(here_row, -1.0, here[c][0]) * inverse
-            m_im = jnp.where(here_row, 0.0, here[c][1]) * inverse
+            if c % 2 == 0:
+                first, second, u = ahead
+                square = conj_times(u, u)[0]
+                inverse = pl.reciprocal(first, approx=True)
+                inverses = inverse, first * pl.reciprocal(first * second - square, approx=True)
+                values = first, second - square * inverse
+                uppers = [{k: entry(here[k], c) for k in range(c + 1, SUB)}, {}]
+                for k in range(c + 2, SUB):
+                    old, loss = entry(here[k], c + 1), conj_times(u, uppers[0][k])
+                    uppers[1][k] = old[0] - loss[0] * inverse, old[1] - loss[1] * inverse
+                if c + 2 < SUB:
+                    one, two = c + 2, c + 3
+                    next_u = entry(here[two], one)
+                    (a1, a2, au), (b1, b2, bu) = [
+                        (conj_times(up[one], up[one])[0], conj_times(up[two], up[two])[0], conj_times(up[one], up[two]))
+                        for up in uppers
+                    ]
+                    ahead = (
+                        (over_rows(here[one][0], one) - a1 * inverse) - b1 * inverses[1],
+                        (over_rows(here[two][0], two) - a2 * inverse) - b2 * inverses[1],
+                        tuple(
+                            (next_u[k] - au[k] * inverse) - bu[k] * inverses[1] for k in range(2)
+                        ),
+                    )
+            m_re = jnp.where(here_row, -1.0, here[c][0]) * inverses[c % 2]
+            m_im = jnp.where(here_row, 0.0, here[c][1]) * inverses[c % 2]
             keep = jnp.where(here_row, head, keep)
             keep_turned = jnp.where(here_row, turned, keep_turned)
-            keep_pivot = jnp.where(here_row, pivot, keep_pivot)
-            for later in range(c + 1, SUB):
+            keep_pivot = jnp.where(here_row, values[c % 2], keep_pivot)
+            for later, (u_re, u_im) in uppers[c % 2].items():
                 re, im = here[later]
-                u_re, u_im = over_rows(re, c), over_rows(im, c)
-                if later == c + 1:
-                    loss = (u_re * inverse) * u_re + (u_im * inverse) * u_im
-                    pivot = over_rows(re, c + 1) - loss
                 here[later] = (
                     jnp.where(here_row, 0.0, re) - m_re * u_re + m_im * u_im,
                     jnp.where(here_row, 0.0, im) - m_re * u_im - m_im * u_re,
@@ -241,6 +271,22 @@
     return final, final_turned, pivots
 
 
+def unit_diagonal(rows):
+    shape = rows[0].shape
+    sub = lax.broadcasted_iota(jnp.int32, shape, 0)
+    lane = lax.broadcasted_iota(jnp.int32, shape, 1)
+    diagonals = [jnp.where(lane == 2 * (i * SUB + sub), row, 0.0) for i, row in enumerate(rows)]
+    across = jnp.sum(tree_sum(diagonals), axis=0, keepdims=True)
+    across = jnp.broadcast_to(across, shape)
+    across = across + pltpu.roll(across, 1, 1)
+    root = lax.rsqrt(across)
+    scaled = [
+        row * lax.rsqrt(jnp.sum(diagonal, axis=1, keepdims=True)) * root
+        for row, diagonal in zip(rows, diagonals)
+    ]
+    return scaled, root, across * root
+
+
 def modes_kernel(scale, slabs, x_ref, *refs):
     *given, modes_hbm, factor_hbm, basis_ref, solved_ref, step_ref, points_ref, modes_ref, factor_ref, sems = refs
     width = basis_ref.shape[0]
@@ -255,8 +301,9 @@
         mine = x_ref[pl.ds(pl.multiple_of(own * width, width), width)]
     points = jnp.transpose(mine)
     points_ref[...] = jnp.concatenate([points, points], 1)
-    gram = gram * scale
-    rows, turned, pivots = eliminate([gram[i * SUB:(i + 1) * SUB] for i in range(count)], solved_ref, step_ref)
+    rows, shrink, grow = unit_diagonal([gram[i * SUB:(i + 1) * SUB] for i in range(count)])
+    shrink, grow = shrink * (1.0 / math.sqrt(scale)), grow * math.sqrt(scale)
+    rows, turned, pivots = eliminate(rows, solved_ref, step_ref)
     shape = rows[0].shape
     sub = lax.broadcasted_iota(jnp.int32, shape, 0)
     lane = lax.broadcasted_iota(jnp.int32, shape, 1)
@@ -267,10 +314,10 @@
         diagonal = 2 * (i * SUB + sub)
         left = jnp.where(lane < diagonal, rows[i], (lane == diagonal).astype(jnp.float32))
         aside = jnp.where(lane < diagonal, turned[i], (lane == diagonal + 1).astype(jnp.float32))
-        basis_ref[pl.ds(2 * i * SUB, SUB, stride=2), :] = left * root
-        basis_ref[pl.ds(2 * i * SUB + 1, SUB, stride=2), :] = aside * root
+        basis_ref[pl.ds(2 * i * SUB, SUB, stride=2), :] = left * (root * shrink)
+        basis_ref[pl.ds(2 * i * SUB + 1, SUB, stride=2), :] = aside * (root * shrink)
         right = jnp.where(lane > diagonal + 1, rows[i], jnp.where(lane == diagonal, pivots[i], 0.0))
-        parts = jnp.take_along_axis(right * root, pick, axis=1)
+        parts = jnp.take_along_axis(right * (root * grow), pick, axis=1)
         factor_ref[0, own_rows, :] = parts[:, :size]
         factor_ref[1, own_rows, :] = parts[:, size:]
     copies = [pltpu.make_async_copy(factor_ref, factor_hbm, sems.at[0])]

time: 23.2 us -> 23.5 us (1.013)
  Pallas kernels: 4.99 us -> 5.26 us
    pallas_call x1, Pallas kernels: 3.3 us -> 3.56 us  [modes_and_factor(): pl.pallas_call(functools.partial(modes_kernel, scale, slabs), out_shape=(...]
where the time goes in v16:
time: 23.5 us; the launch traced here: 23.3 us
  blocking collectives  17.4 us (74%)
  Pallas kernels  5.26 us (22%)
  between operations  0.64 us (3%)
    all_to_all x1, blocking collectives, local(): x = swap(chunks, ('space', 'blk')).reshape(-1, points)  17.4 us
    pallas_call x1, Pallas kernels, modes_and_factor(): pl.pallas_call(functools.partial(modes_kernel, scale, slabs), out_shape=(...  3.56 us
    pallas_call x1, Pallas kernels, block_spectra(): pl.pallas_call(spectra_kernel, out_shape=jax.ShapeDtypeStruct((copies, ro...  1.69 us

profile of v16, /device:TPU:0, one launch (start us, length us, event | category | flops | bytes accessed | tf_op | source)
XLA Modules:
  0.0 23.3 jit_solution(12902316658145437205)
XLA Ops:
  0.6 1.7 %spectra.1 = bf16[2,128,512]{2,1,0:T(8,128)(2,1)S(1)} custom-call(bf16[1280,512]{1,0:T(8,128)(2,1)} %snap_hbm.1, f32[1280]{0:T(1024)} %scales_hbm.1, s32[4]{0:T(128)} %offsets_hbm.1, s32[16]{0:T(128)} %freq_hbm.1), custom_call_target="tpu_custom_call" | custom-call | tf_op jit(solution)/shard_map/spectra/pallas_call | solution.py:104
  2.3 17.4 %all_to_all.5 = bf16[32,8,512]{2,1,0:T(8,128)(2,1)S(1)} all-to-all(bf16[32,8,512]{2,1,0:T(8,128)(2,1)S(1)} %bitcast.5), channel_id=1, replica_groups=mesh['space'=2,'blk'=16] {'space','blk'}, dimensions={0} | all-to-all | bytes 524288 | tf_op jit(solution)/shard_map/all_to_all | solution.py:376
  19.7 3.6 %factor_and_modes.1 = (f32[512,128]{1,0:T(8,128)}, f32[2,64,64]{2,1,0:T(8,128)}) custom-call(bf16[256,512]{1,0:T(8,128)(2,1)S(1)} %bitcast.4), custom_call_target="tpu_custom_call" | custom-call | tf_op jit(solution)/shard_map/factor_and_modes/pallas_call | solution.py:345

commit v17 on v15

--- a/solution.py
+++ b/solution.py
@@ -162,7 +162,19 @@
     return terms[0]
 
 
-def eliminate(rows, solved_ref, step_ref):
+def three_terms(x):
+    high = x.astype(jnp.bfloat16)
+    rest = x - high.astype(jnp.float32)
+    middle = rest.astype(jnp.bfloat16)
+    return high, middle, (rest - middle.astype(jnp.float32)).astype(jnp.bfloat16)
+
+
+def parts_apart(x, lane):
+    size = x.shape[1] // 2
+    return jnp.take_along_axis(x, jnp.where(lane < size, 2 * lane, 2 * (lane - size) + 1), axis=1)
+
+
+def eliminate(rows, step_ref):
     count = len(rows)
     shape = rows[0].shape
     sub = lax.broadcasted_iota(jnp.int32, shape, 0)
@@ -187,6 +199,11 @@
             i: [(over_lanes(rows[i], at), over_lanes(rows[i], at + 1)) for at in columns]
             for i in range(own, min(own + 2, count))
         }
+        apart = parts_apart(head, lane)
+        high, middle, low = three_terms(
+            jnp.concatenate([apart, -pltpu.roll(apart, shape[1] // 2, 1)], 0)
+        )
+        columns_below = jnp.concatenate([high, high, middle, high, middle, low], 0)
         here = raw[own]
         pivot = over_rows(here[0][0], 0)
         for c in range(SUB):
@@ -222,27 +239,24 @@
         if own + 1 == count:
             break
         inside = (lane >= columns[0]) & (lane < columns[0] + 2 * SUB)
-        solved_ref[own, pl.ds(0, SUB, stride=2), :] = head
-        solved_ref[own, pl.ds(1, SUB, stride=2), :] = turned
         solved = [(over_rows(head, c), over_rows(turned, c)) for c in range(SUB)]
         rows[own + 1] = jnp.where(inside, 0.0, rows[own + 1]) - tree_sum(
             [re * p + im * q for (re, im), (p, q) in zip(raw[own + 1], solved)]
         )
         far = range(own + 2, count)
         if far:
-            below = jnp.concatenate([rows[i] for i in far], 0)
-            losses = jnp.dot(
-                below[:, columns[0]:columns[0] + 2 * SUB], solved_ref[own],
-                precision=lax.Precision.HIGHEST, preferred_element_type=jnp.float32,
+            high, middle, low = three_terms(jnp.concatenate([head, turned], 0))
+            losses = lax.dot_general(
+                columns_below, jnp.concatenate([high, middle, high, low, middle, high], 0),
+                (((0,), (0,)), ((), ())), preferred_element_type=jnp.float32,
             )
-            for at, i in enumerate(far):
-                loss = losses[at * SUB:(at + 1) * SUB]
-                rows[i] = jnp.where(inside, 0.0, rows[i]) - loss
+            for i in far:
+                rows[i] = jnp.where(inside, 0.0, rows[i]) - losses[i * SUB:(i + 1) * SUB]
     return final, final_turned, pivots
 
 
 def modes_kernel(scale, slabs, x_ref, *refs):
-    *given, modes_hbm, factor_hbm, basis_ref, solved_ref, step_ref, points_ref, modes_ref, factor_ref, sems = refs
+    *given, modes_hbm, factor_hbm, basis_ref, step_ref, points_ref, modes_ref, factor_ref, sems = refs
     width = basis_ref.shape[0]
     size = width // 2
     count = size // SUB
@@ -256,11 +270,10 @@
     points = jnp.transpose(mine)
     points_ref[...] = jnp.concatenate([points, points], 1)
     gram = gram * scale
-    rows, turned, pivots = eliminate([gram[i * SUB:(i + 1) * SUB] for i in range(count)], solved_ref, step_ref)
+    rows, turned, pivots = eliminate([gram[i * SUB:(i + 1) * SUB] for i in range(count)], step_ref)
     shape = rows[0].shape
     sub = lax.broadcasted_iota(jnp.int32, shape, 0)
     lane = lax.broadcasted_iota(jnp.int32, shape, 1)
-    pick = jnp.where(lane < size, 2 * lane, 2 * (lane - size) + 1)
     for i in range(count):
         own_rows = slice(i * SUB, (i + 1) * SUB)
         root = lax.rsqrt(pivots[i])
@@ -270,7 +283,7 @@
         basis_ref[pl.ds(2 * i * SUB, SUB, stride=2), :] = left * root
         basis_ref[pl.ds(2 * i * SUB + 1, SUB, stride=2), :] = aside * root
         right = jnp.where(lane > diagonal + 1, rows[i], jnp.where(lane == diagonal, pivots[i], 0.0))
-        parts = jnp.take_along_axis(right * root, pick, axis=1)
+        parts = parts_apart(right * root, lane)
         factor_ref[0, own_rows, :] = parts[:, :size]
         factor_ref[1, own_rows, :] = parts[:, size:]
     copies = [pltpu.make_async_copy(factor_ref, factor_hbm, sems.at[0])]
@@ -305,7 +318,6 @@
         out_specs=(pl.BlockSpec(memory_space=pltpu.HBM),) * 2,
         scratch_shapes=[
             pltpu.VMEM((width, width), jnp.float32),
-            pltpu.VMEM((size // SUB, 2 * SUB, width), jnp.float32),
             pltpu.VMEM((SUB, 2 * SUB, width), jnp.float32),
             pltpu.VMEM((points, 2 * width), jnp.bfloat16),
             pltpu.VMEM((points, width), jnp.float32),

time: 23.2 us -> 23.4 us (level)
  no operation moved by 1% of the time
where the time goes in v17:
time: 23.4 us; the launch traced here: 23.2 us
  blocking collectives  17.4 us (74%)
  Pallas kernels  5.19 us (22%)
  between operations  0.64 us (3%)
    all_to_all x1, blocking collectives, local(): x = swap(chunks, ('space', 'blk')).reshape(-1, points)  17.4 us
    pallas_call x1, Pallas kernels, modes_and_factor(): pl.pallas_call(functools.partial(modes_kernel, scale, slabs), out_shape=(...  3.5 us
    pallas_call x1, Pallas kernels, block_spectra(): pl.pallas_call(spectra_kernel, out_shape=jax.ShapeDtypeStruct((copies, ro...  1.69 us

profile of v17, /device:TPU:0, one launch (start us, length us, event | category | flops | bytes accessed | tf_op | source)
XLA Modules:
  0.0 23.2 jit_solution(11165627617873885054)
XLA Ops:
  0.6 1.7 %spectra.1 = bf16[2,128,512]{2,1,0:T(8,128)(2,1)S(1)} custom-call(bf16[1280,512]{1,0:T(8,128)(2,1)} %snap_hbm.1, f32[1280]{0:T(1024)} %scales_hbm.1, s32[4]{0:T(128)} %offsets_hbm.1, s32[16]{0:T(128)} %freq_hbm.1), custom_call_target="tpu_custom_call" | custom-call | tf_op jit(solution)/shard_map/spectra/pallas_call | solution.py:100
  2.3 17.4 %all_to_all.5 = bf16[32,8,512]{2,1,0:T(8,128)(2,1)S(1)} all-to-all(bf16[32,8,512]{2,1,0:T(8,128)(2,1)S(1)} %bitcast.5), channel_id=1, replica_groups=mesh['space'=2,'blk'=16] {'space','blk'}, dimensions={0} | all-to-all | bytes 524288 | tf_op jit(solution)/shard_map/all_to_all | solution.py:341
  19.7 3.5 %factor_and_modes.1 = (f32[512,128]{1,0:T(8,128)}, f32[2,64,64]{2,1,0:T(8,128)}) custom-call(bf16[256,512]{1,0:T(8,128)(2,1)S(1)} %bitcast.4), custom_call_target="tpu_custom_call" | custom-call | tf_op jit(solution)/shard_map/factor_and_modes/pallas_call | solution.py:311

commit v18 on v15

--- a/solution.py
+++ b/solution.py
@@ -162,7 +162,7 @@
     return terms[0]
 
 
-def eliminate(rows, solved_ref, step_ref):
+def eliminate(rows, solved_ref, step_ref, column_ref):
     count = len(rows)
     shape = rows[0].shape
     sub = lax.broadcasted_iota(jnp.int32, shape, 0)
@@ -178,6 +178,7 @@
         return ref[(*at[:-1], pl.ds(at[-1], SUB, stride=0), slice(None))]
 
     rows = list(rows)
+    solved_ref[...] = jnp.zeros_like(solved_ref)
     final, final_turned, pivots = [], [], []
     for own in range(count):
         head, turned = rows[own], rotated(rows[own], lane)
@@ -199,10 +200,12 @@
             keep_pivot = jnp.where(here_row, pivot, keep_pivot)
             for later in range(c + 1, SUB):
                 re, im = here[later]
-                u_re, u_im = over_rows(re, c), over_rows(im, c)
+                column_ref[c, later, :SUB, :] = re
+                column_ref[c, later, SUB:, :] = im
+                u_re, u_im = row_of(column_ref, c, later, c), row_of(column_ref, c, later, SUB + c)
                 if later == c + 1:
                     loss = (u_re * inverse) * u_re + (u_im * inverse) * u_im
-                    pivot = over_rows(re, c + 1) - loss
+                    pivot = row_of(column_ref, c, later, c + 1) - loss
                 here[later] = (
                     jnp.where(here_row, 0.0, re) - m_re * u_re + m_im * u_im,
                     jnp.where(here_row, 0.0, im) - m_re * u_im - m_im * u_re,
@@ -222,17 +225,16 @@
         if own + 1 == count:
             break
         inside = (lane >= columns[0]) & (lane < columns[0] + 2 * SUB)
-        solved_ref[own, pl.ds(0, SUB, stride=2), :] = head
-        solved_ref[own, pl.ds(1, SUB, stride=2), :] = turned
-        solved = [(over_rows(head, c), over_rows(turned, c)) for c in range(SUB)]
+        solved_ref[pl.ds(columns[0], SUB, stride=2), :] = head
+        solved_ref[pl.ds(columns[0] + 1, SUB, stride=2), :] = turned
+        solved = [(row_of(solved_ref, at), row_of(solved_ref, at + 1)) for at in columns]
         rows[own + 1] = jnp.where(inside, 0.0, rows[own + 1]) - tree_sum(
             [re * p + im * q for (re, im), (p, q) in zip(raw[own + 1], solved)]
         )
         far = range(own + 2, count)
         if far:
-            below = jnp.concatenate([rows[i] for i in far], 0)
             losses = jnp.dot(
-                below[:, columns[0]:columns[0] + 2 * SUB], solved_ref[own],
+                jnp.concatenate([jnp.where(inside, rows[i], 0.0) for i in far], 0), solved_ref[...],
                 precision=lax.Precision.HIGHEST, preferred_element_type=jnp.float32,
             )
             for at, i in enumerate(far):
@@ -242,7 +244,8 @@
 
 
 def modes_kernel(scale, slabs, x_ref, *refs):
-    *given, modes_hbm, factor_hbm, basis_ref, solved_ref, step_ref, points_ref, modes_ref, factor_ref, sems = refs
+    *given, modes_hbm, factor_hbm, basis_ref, solved_ref, step_ref, column_ref = refs[:-4]
+    points_ref, modes_ref, factor_ref, sems = refs[-4:]
     width = basis_ref.shape[0]
     size = width // 2
     count = size // SUB
@@ -256,7 +259,7 @@
     points = jnp.transpose(mine)
     points_ref[...] = jnp.concatenate([points, points], 1)
     gram = gram * scale
-    rows, turned, pivots = eliminate([gram[i * SUB:(i + 1) * SUB] for i in range(count)], solved_ref, step_ref)
+    rows, turned, pivots = eliminate([gram[i * SUB:(i + 1) * SUB] for i in range(count)], solved_ref, step_ref, column_ref)
     shape = rows[0].shape
     sub = lax.broadcasted_iota(jnp.int32, shape, 0)
     lane = lax.broadcasted_iota(jnp.int32, shape, 1)
@@ -305,8 +308,9 @@
         out_specs=(pl.BlockSpec(memory_space=pltpu.HBM),) * 2,
         scratch_shapes=[
             pltpu.VMEM((width, width), jnp.float32),
-            pltpu.VMEM((size // SUB, 2 * SUB, width), jnp.float32),
+            pltpu.VMEM((width, width), jnp.float32),
             pltpu.VMEM((SUB, 2 * SUB, width), jnp.float32),
+            pltpu.VMEM((SUB, SUB, 2 * SUB, width), jnp.float32),
             pltpu.VMEM((points, 2 * width), jnp.bfloat16),
             pltpu.VMEM((points, width), jnp.float32),
             pltpu.VMEM((2, size, size), jnp.float32),

time: 23.2 us -> 23.3 us (level)
  no operation moved by 1% of the time
where the time goes in v18:
time: 23.3 us; the launch traced here: 23.1 us
  blocking collectives  17.4 us (75%)
  Pallas kernels  5.06 us (22%)
  between operations  0.64 us (3%)
    all_to_all x1, blocking collectives, local(): x = swap(chunks, ('space', 'blk')).reshape(-1, points)  17.4 us
    pallas_call x1, Pallas kernels, modes_and_factor(): pl.pallas_call(functools.partial(modes_kernel, scale, slabs), out_shape=(...  3.37 us
    pallas_call x1, Pallas kernels, block_spectra(): pl.pallas_call(spectra_kernel, out_shape=jax.ShapeDtypeStruct((copies, ro...  1.69 us

profile of v18, /device:TPU:0, one launch (start us, length us, event | category | flops | bytes accessed | tf_op | source)
XLA Modules:
  0.0 23.1 jit_solution(10123358568875129156)
XLA Ops:
  0.6 1.7 %spectra.1 = bf16[2,128,512]{2,1,0:T(8,128)(2,1)S(1)} custom-call(bf16[1280,512]{1,0:T(8,128)(2,1)} %snap_hbm.1, f32[1280]{0:T(1024)} %scales_hbm.1, s32[4]{0:T(128)} %offsets_hbm.1, s32[16]{0:T(128)} %freq_hbm.1), custom_call_target="tpu_custom_call" | custom-call | tf_op jit(solution)/shard_map/spectra/pallas_call | solution.py:100
  2.3 17.4 %all_to_all.5 = bf16[32,8,512]{2,1,0:T(8,128)(2,1)S(1)} all-to-all(bf16[32,8,512]{2,1,0:T(8,128)(2,1)S(1)} %bitcast.5), channel_id=1, replica_groups=mesh['space'=2,'blk'=16] {'space','blk'}, dimensions={0} | all-to-all | bytes 524288 | tf_op jit(solution)/shard_map/all_to_all | solution.py:333
  19.7 3.4 %factor_and_modes.1 = (f32[512,128]{1,0:T(8,128)}, f32[2,64,64]{2,1,0:T(8,128)}) custom-call(bf16[256,512]{1,0:T(8,128)(2,1)S(1)} %bitcast.4), custom_call_target="tpu_custom_call" | custom-call | tf_op jit(solution)/shard_map/factor_and_modes/pallas_call | solution.py:301

commit v19 on v15

--- a/solution.py
+++ b/solution.py
@@ -162,11 +162,15 @@
     return terms[0]
 
 
-def eliminate(rows, solved_ref, step_ref):
-    count = len(rows)
-    shape = rows[0].shape
+def eliminate(rows_ref, final_ref, turned_ref, pivots_ref, solved_ref):
+    size = final_ref.shape[0]
+    width = final_ref.shape[1]
+    shape = (SUB, width)
     sub = lax.broadcasted_iota(jnp.int32, shape, 0)
     lane = lax.broadcasted_iota(jnp.int32, shape, 1)
+    all_rows = lax.broadcasted_iota(jnp.int32, (size, width), 0)
+    all_lanes = lax.broadcasted_iota(jnp.int32, (size, width), 1)
+    solved_ref[...] = jnp.zeros_like(solved_ref)
 
     def over_lanes(x, at):
         return jnp.broadcast_to(x[:, at:at + 1], shape)
@@ -174,20 +178,27 @@
     def over_rows(x, at):
         return jnp.broadcast_to(x[at:at + 1, :], shape)
 
-    def row_of(ref, *at):
-        return ref[(*at[:-1], pl.ds(at[-1], SUB, stride=0), slice(None))]
-
-    rows = list(rows)
-    final, final_turned, pivots = [], [], []
-    for own in range(count):
-        head, turned = rows[own], rotated(rows[own], lane)
+    def block_at(i):
+        return pl.ds(pl.multiple_of(i * SUB, SUB), SUB)
+
+    def columns_of(x, start):
+        moved = pltpu.roll(x, lax.rem(width - start, width), 1)
+        return [(over_lanes(moved, 2 * c), over_lanes(moved, 2 * c + 1)) for c in range(SUB)]
+
+    def panel(own, carry):
+        start = own * 2 * SUB
+        before = start - 2 * SUB
+        head = rows_ref[block_at(own), :]
+        every = rows_ref[:size, :]
+        inside = (all_rows >= (own + 1) * SUB) & (all_lanes >= before) & (all_lanes < start)
+        losses = jnp.dot(
+            jnp.where(inside, every, 0.0), solved_ref[...],
+            precision=lax.Precision.HIGHEST, preferred_element_type=jnp.float32,
+        )
+        rows_ref[:size, :] = jnp.where(inside, 0.0, every) - losses
+        turned = rotated(head, lane)
+        here = columns_of(head, start)
         keep, keep_turned, keep_pivot = head, turned, jnp.ones(shape, jnp.float32)
-        columns = [2 * (own * SUB + c) for c in range(SUB)]
-        raw = {
-            i: [(over_lanes(rows[i], at), over_lanes(rows[i], at + 1)) for at in columns]
-            for i in range(own, min(own + 2, count))
-        }
-        here = raw[own]
         pivot = over_rows(here[0][0], 0)
         for c in range(SUB):
             here_row = sub == c
@@ -207,42 +218,32 @@
                     jnp.where(here_row, 0.0, re) - m_re * u_re + m_im * u_im,
                     jnp.where(here_row, 0.0, im) - m_re * u_im - m_im * u_re,
                 )
-            on_re, on_im = lane == columns[c], lane == columns[c] + 1
+            on_re, on_im = lane == start + 2 * c, lane == start + 2 * c + 1
             on_pair = on_re | on_im
-            step_ref[c, :SUB, :] = head
-            step_ref[c, SUB:, :] = turned
-            p = jnp.where(on_pair, on_re.astype(jnp.float32), row_of(step_ref, c, c))
-            q = jnp.where(on_pair, on_im.astype(jnp.float32), row_of(step_ref, c, SUB + c))
+            p = jnp.where(on_pair, on_re.astype(jnp.float32), over_rows(head, c))
+            q = jnp.where(on_pair, on_im.astype(jnp.float32), over_rows(turned, c))
             cleared = here_row | on_pair
             head = jnp.where(cleared, 0.0, head) - (m_re * p + m_im * q)
             turned = jnp.where(cleared, 0.0, turned) - (m_re * q - m_im * p)
-        final.append(keep)
-        final_turned.append(keep_turned)
-        pivots.append(keep_pivot)
-        if own + 1 == count:
-            break
-        inside = (lane >= columns[0]) & (lane < columns[0] + 2 * SUB)
-        solved_ref[own, pl.ds(0, SUB, stride=2), :] = head
-        solved_ref[own, pl.ds(1, SUB, stride=2), :] = turned
-        solved = [(over_rows(head, c), over_rows(turned, c)) for c in range(SUB)]
-        rows[own + 1] = jnp.where(inside, 0.0, rows[own + 1]) - tree_sum(
-            [re * p + im * q for (re, im), (p, q) in zip(raw[own + 1], solved)]
+        final_ref[block_at(own), :] = keep
+        turned_ref[block_at(own), :] = keep_turned
+        pivots_ref[block_at(own), :] = keep_pivot
+        solved_ref[pl.ds(pl.multiple_of(start, 2 * SUB), SUB, stride=2), :] = head
+        solved_ref[pl.ds(pl.multiple_of(start, 2 * SUB) + 1, SUB, stride=2), :] = turned
+        following = rows_ref[block_at(own + 1), :]
+        raw = columns_of(following, start)
+        within = (lane >= start) & (lane < start + 2 * SUB)
+        rows_ref[block_at(own + 1), :] = jnp.where(within, 0.0, following) - tree_sum(
+            [re * over_rows(head, c) + im * over_rows(turned, c) for c, (re, im) in enumerate(raw)]
         )
-        far = range(own + 2, count)
-        if far:
-            below = jnp.concatenate([rows[i] for i in far], 0)
-            losses = jnp.dot(
-                below[:, columns[0]:columns[0] + 2 * SUB], solved_ref[own],
-                precision=lax.Precision.HIGHEST, preferred_element_type=jnp.float32,
-            )
-            for at, i in enumerate(far):
-                loss = losses[at * SUB:(at + 1) * SUB]
-                rows[i] = jnp.where(inside, 0.0, rows[i]) - loss
-    return final, final_turned, pivots
+        return carry
+
+    lax.fori_loop(0, size // SUB, panel, 0)
 
 
 def modes_kernel(scale, slabs, x_ref, *refs):
-    *given, modes_hbm, factor_hbm, basis_ref, solved_ref, step_ref, points_ref, modes_ref, factor_ref, sems = refs
+    *given, modes_hbm, factor_hbm, basis_ref, rows_ref, final_ref, turned_ref, pivots_ref = refs[:-5]
+    solved_ref, points_ref, modes_ref, factor_ref, sems = refs[-5:]
     width = basis_ref.shape[0]
     size = width // 2
     count = size // SUB
@@ -255,8 +256,12 @@
         mine = x_ref[pl.ds(pl.multiple_of(own * width, width), width)]
     points = jnp.transpose(mine)
     points_ref[...] = jnp.concatenate([points, points], 1)
-    gram = gram * scale
-    rows, turned, pivots = eliminate([gram[i * SUB:(i + 1) * SUB] for i in range(count)], solved_ref, step_ref)
+    rows_ref[:size, :] = gram * scale
+    rows_ref[size:, :] = jnp.zeros((SUB, width), jnp.float32)
+    eliminate(rows_ref, final_ref, turned_ref, pivots_ref, solved_ref)
+    rows, turned, pivots = [
+        [ref[i * SUB:(i + 1) * SUB, :] for i in range(count)] for ref in (final_ref, turned_ref, pivots_ref)
+    ]
     shape = rows[0].shape
     sub = lax.broadcasted_iota(jnp.int32, shape, 0)
     lane = lax.broadcasted_iota(jnp.int32, shape, 1)
@@ -305,8 +310,11 @@
         out_specs=(pl.BlockSpec(memory_space=pltpu.HBM),) * 2,
         scratch_shapes=[
             pltpu.VMEM((width, width), jnp.float32),
-            pltpu.VMEM((size // SUB, 2 * SUB, width), jnp.float32),
-            pltpu.VMEM((SUB, 2 * SUB, width), jnp.float32),
+            pltpu.VMEM((size + SUB, width), jnp.float32),
+            pltpu.VMEM((size, width), jnp.float32),
+            pltpu.VMEM((size, width), jnp.float32),
+            pltpu.VMEM((size, width), jnp.float32),
+            pltpu.VMEM((width, width), jnp.float32),
             pltpu.VMEM((points, 2 * width), jnp.bfloat16),
             pltpu.VMEM((points, width), jnp.float32),
             pltpu.VMEM((2, size, size), jnp.float32),

time: 23.2 us -> 24 us (1.034)
  Pallas kernels: 4.99 us -> 5.79 us
    pallas_call x1, Pallas kernels: 3.3 us -> 4.1 us  [modes_and_factor(): pl.pallas_call(functools.partial(modes_kernel, scale, slabs), out_shape=(...]
where the time goes in v19:
time: 24 us; the launch traced here: 23.8 us
  blocking collectives  17.4 us (72%)
  Pallas kernels  5.79 us (24%)
  between operations  0.64 us (3%)
    all_to_all x1, blocking collectives, local(): x = swap(chunks, ('space', 'blk')).reshape(-1, points)  17.4 us
    pallas_call x1, Pallas kernels, modes_and_factor(): pl.pallas_call(functools.partial(modes_kernel, scale, slabs), out_shape=(...  4.1 us
    pallas_call x1, Pallas kernels, block_spectra(): pl.pallas_call(spectra_kernel, out_shape=jax.ShapeDtypeStruct((copies, ro...  1.69 us

profile of v19, /device:TPU:0, one launch (start us, length us, event | category | flops | bytes accessed | tf_op | source)
XLA Modules:
  0.0 23.8 jit_solution(7300340915187778101)
XLA Ops:
  0.6 1.7 %spectra.1 = bf16[2,128,512]{2,1,0:T(8,128)(2,1)S(1)} custom-call(bf16[1280,512]{1,0:T(8,128)(2,1)} %snap_hbm.1, f32[1280]{0:T(1024)} %scales_hbm.1, s32[4]{0:T(128)} %offsets_hbm.1, s32[16]{0:T(128)} %freq_hbm.1), custom_call_target="tpu_custom_call" | custom-call | tf_op jit(solution)/shard_map/spectra/pallas_call | solution.py:100
  2.3 17.4 %all_to_all.5 = bf16[32,8,512]{2,1,0:T(8,128)(2,1)S(1)} all-to-all(bf16[32,8,512]{2,1,0:T(8,128)(2,1)S(1)} %bitcast.5), channel_id=1, replica_groups=mesh['space'=2,'blk'=16] {'space','blk'}, dimensions={0} | all-to-all | bytes 524288 | tf_op jit(solution)/shard_map/all_to_all | solution.py:337
  19.7 4.1 %factor_and_modes.1 = (f32[512,128]{1,0:T(8,128)}, f32[2,64,64]{2,1,0:T(8,128)}) custom-call(bf16[256,512]{1,0:T(8,128)(2,1)S(1)} %bitcast.4), custom_call_target="tpu_custom_call" | custom-call | tf_op jit(solution)/shard_map/factor_and_modes/pallas_call | solution.py:303

commit v20 on v15

--- a/solution.py
+++ b/solution.py
@@ -10,6 +10,7 @@
 
 NFFT = 512
 SUB = 8
+NEAR = 2
 PIECE = 640
 PARTS = 4
 FEW_SLABS = 2
@@ -162,7 +163,7 @@
     return terms[0]
 
 
-def eliminate(rows, solved_ref, step_ref):
+def eliminate(rows, solved_ref, step_ref, done_ref):
     count = len(rows)
     shape = rows[0].shape
     sub = lax.broadcasted_iota(jnp.int32, shape, 0)
@@ -181,11 +182,11 @@
     final, final_turned, pivots = [], [], []
     for own in range(count):
         head, turned = rows[own], rotated(rows[own], lane)
-        keep, keep_turned, keep_pivot = head, turned, jnp.ones(shape, jnp.float32)
+        done = slice(own * SUB, (own + 1) * SUB)
         columns = [2 * (own * SUB + c) for c in range(SUB)]
         raw = {
             i: [(over_lanes(rows[i], at), over_lanes(rows[i], at + 1)) for at in columns]
-            for i in range(own, min(own + 2, count))
+            for i in range(own, min(own + 1 + NEAR, count))
         }
         here = raw[own]
         pivot = over_rows(here[0][0], 0)
@@ -194,9 +195,9 @@
             inverse = pl.reciprocal(pivot, approx=True)
             m_re = jnp.where(here_row, -1.0, here[c][0]) * inverse
             m_im = jnp.where(here_row, 0.0, here[c][1]) * inverse
-            keep = jnp.where(here_row, head, keep)
-            keep_turned = jnp.where(here_row, turned, keep_turned)
-            keep_pivot = jnp.where(here_row, pivot, keep_pivot)
+            done_row = slice(own * SUB + c, own * SUB + c + 1)
+            for place, value in enumerate((head, turned, pivot)):
+                done_ref[place, done_row, :] = value[c:c + 1]
             for later in range(c + 1, SUB):
                 re, im = here[later]
                 u_re, u_im = over_rows(re, c), over_rows(im, c)
@@ -216,19 +217,20 @@
             cleared = here_row | on_pair
             head = jnp.where(cleared, 0.0, head) - (m_re * p + m_im * q)
             turned = jnp.where(cleared, 0.0, turned) - (m_re * q - m_im * p)
-        final.append(keep)
-        final_turned.append(keep_turned)
-        pivots.append(keep_pivot)
+        final.append(done_ref[0, done, :])
+        final_turned.append(done_ref[1, done, :])
+        pivots.append(done_ref[2, done, :])
         if own + 1 == count:
             break
         inside = (lane >= columns[0]) & (lane < columns[0] + 2 * SUB)
         solved_ref[own, pl.ds(0, SUB, stride=2), :] = head
         solved_ref[own, pl.ds(1, SUB, stride=2), :] = turned
         solved = [(over_rows(head, c), over_rows(turned, c)) for c in range(SUB)]
-        rows[own + 1] = jnp.where(inside, 0.0, rows[own + 1]) - tree_sum(
-            [re * p + im * q for (re, im), (p, q) in zip(raw[own + 1], solved)]
-        )
-        far = range(own + 2, count)
+        for i in range(own + 1, min(own + 1 + NEAR, count)):
+            rows[i] = jnp.where(inside, 0.0, rows[i]) - tree_sum(
+                [re * p + im * q for (re, im), (p, q) in zip(raw[i], solved)]
+            )
+        far = range(own + 1 + NEAR, count)
         if far:
             below = jnp.concatenate([rows[i] for i in far], 0)
             losses = jnp.dot(
@@ -242,7 +244,8 @@
 
 
 def modes_kernel(scale, slabs, x_ref, *refs):
-    *given, modes_hbm, factor_hbm, basis_ref, solved_ref, step_ref, points_ref, modes_ref, factor_ref, sems = refs
+    *given, modes_hbm, factor_hbm, basis_ref, solved_ref, step_ref, done_ref = refs[:-4]
+    points_ref, modes_ref, factor_ref, sems = refs[-4:]
     width = basis_ref.shape[0]
     size = width // 2
     count = size // SUB
@@ -256,7 +259,7 @@
     points = jnp.transpose(mine)
     points_ref[...] = jnp.concatenate([points, points], 1)
     gram = gram * scale
-    rows, turned, pivots = eliminate([gram[i * SUB:(i + 1) * SUB] for i in range(count)], solved_ref, step_ref)
+    rows, turned, pivots = eliminate([gram[i * SUB:(i + 1) * SUB] for i in range(count)], solved_ref, step_ref, done_ref)
     shape = rows[0].shape
     sub = lax.broadcasted_iota(jnp.int32, shape, 0)
     lane = lax.broadcasted_iota(jnp.int32, shape, 1)
@@ -307,6 +310,7 @@
             pltpu.VMEM((width, width), jnp.float32),
             pltpu.VMEM((size // SUB, 2 * SUB, width), jnp.float32),
             pltpu.VMEM((SUB, 2 * SUB, width), jnp.float32),
+            pltpu.VMEM((3, size, width), jnp.float32),
             pltpu.VMEM((points, 2 * width), jnp.bfloat16),
             pltpu.VMEM((points, width), jnp.float32),
             pltpu.VMEM((2, size, size), jnp.float32),

time: 23.2 us -> 23.4 us (level)
  no operation moved by 1% of the time
where the time goes in v20:
time: 23.4 us; the launch traced here: 23.2 us
  blocking collectives  17.4 us (74%)
  Pallas kernels  5.21 us (22%)
  between operations  0.64 us (3%)
    all_to_all x1, blocking collectives, local(): x = swap(chunks, ('space', 'blk')).reshape(-1, points)  17.4 us
    pallas_call x1, Pallas kernels, modes_and_factor(): pl.pallas_call(functools.partial(modes_kernel, scale, slabs), out_shape=(...  3.51 us
    pallas_call x1, Pallas kernels, block_spectra(): pl.pallas_call(spectra_kernel, out_shape=jax.ShapeDtypeStruct((copies, ro...  1.69 us

profile of v20, /device:TPU:0, one launch (start us, length us, event | category | flops | bytes accessed | tf_op | source)
XLA Modules:
  0.0 23.2 jit_solution(17287833730674623202)
XLA Ops:
  0.6 1.7 %spectra.1 = bf16[2,128,512]{2,1,0:T(8,128)(2,1)S(1)} custom-call(bf16[1280,512]{1,0:T(8,128)(2,1)} %snap_hbm.1, f32[1280]{0:T(1024)} %scales_hbm.1, s32[4]{0:T(128)} %offsets_hbm.1, s32[16]{0:T(128)} %freq_hbm.1), custom_call_target="tpu_custom_call" | custom-call | tf_op jit(solution)/shard_map/spectra/pallas_call | solution.py:101
  2.3 17.4 %all_to_all.5 = bf16[32,8,512]{2,1,0:T(8,128)(2,1)S(1)} all-to-all(bf16[32,8,512]{2,1,0:T(8,128)(2,1)S(1)} %bitcast.5), channel_id=1, replica_groups=mesh['space'=2,'blk'=16] {'space','blk'}, dimensions={0} | all-to-all | bytes 524288 | tf_op jit(solution)/shard_map/all_to_all | solution.py:333
  19.7 3.5 %factor_and_modes.1 = (f32[512,128]{1,0:T(8,128)}, f32[2,64,64]{2,1,0:T(8,128)}) custom-call(bf16[256,512]{1,0:T(8,128)(2,1)S(1)} %bitcast.4), custom_call_target="tpu_custom_call" | custom-call | tf_op jit(solution)/shard_map/factor_and_modes/pallas_call | solution.py:301

commit v21 on v20

--- a/solution.py
+++ b/solution.py
@@ -10,9 +10,9 @@
 
 NFFT = 512
 SUB = 8
-NEAR = 2
+NEAR = 1
 PIECE = 640
-PARTS = 4
+PARTS = 2
 FEW_SLABS = 2
 SIN_COEFS = (
     0.9999999765895043,

time: 23.4 us -> 23.2 us (level)
  no operation moved by 1% of the time
where the time goes in v21:
time: 23.2 us; the launch traced here: 23 us
  blocking collectives  17.4 us (75%)
  Pallas kernels  5.01 us (22%)
  between operations  0.64 us (3%)
    all_to_all x1, blocking collectives, local(): x = swap(chunks, ('space', 'blk')).reshape(-1, points)  17.4 us
    pallas_call x1, Pallas kernels, modes_and_factor(): pl.pallas_call(functools.partial(modes_kernel, scale, slabs), out_shape=(...  3.32 us
    pallas_call x1, Pallas kernels, block_spectra(): pl.pallas_call(spectra_kernel, out_shape=jax.ShapeDtypeStruct((copies, ro...  1.69 us

profile of v21, /device:TPU:0, one launch (start us, length us, event | category | flops | bytes accessed | tf_op | source)
XLA Modules:
  0.0 23.0 jit_solution(828832175760986133)
XLA Ops:
  0.6 1.7 %spectra.1 = bf16[2,128,512]{2,1,0:T(8,128)(2,1)S(1)} custom-call(bf16[1280,512]{1,0:T(8,128)(2,1)} %snap_hbm.1, f32[1280]{0:T(1024)} %scales_hbm.1, s32[4]{0:T(128)} %offsets_hbm.1, s32[16]{0:T(128)} %freq_hbm.1), custom_call_target="tpu_custom_call" | custom-call | tf_op jit(solution)/shard_map/spectra/pallas_call | solution.py:101
  2.3 17.4 %all_to_all.5 = bf16[32,8,512]{2,1,0:T(8,128)(2,1)S(1)} all-to-all(bf16[32,8,512]{2,1,0:T(8,128)(2,1)S(1)} %bitcast.5), channel_id=1, replica_groups=mesh['space'=2,'blk'=16] {'space','blk'}, dimensions={0} | all-to-all | bytes 524288 | tf_op jit(solution)/shard_map/all_to_all | solution.py:333
  19.7 3.3 %factor_and_modes.1 = (f32[512,128]{1,0:T(8,128)}, f32[2,64,64]{2,1,0:T(8,128)}) custom-call(bf16[256,512]{1,0:T(8,128)(2,1)S(1)} %bitcast.4), custom_call_target="tpu_custom_call" | custom-call | tf_op jit(solution)/shard_map/factor_and_modes/pallas_call | solution.py:301

commit v22 on v15

--- a/solution.py
+++ b/solution.py
@@ -51,7 +51,7 @@
         pltpu.make_async_copy(snap_hbm.at[piece], snap_ref.at[piece], snap_sems.at[i])
         for i, piece in enumerate(pieces)
     ]
-    for copy in small + large:
+    for copy in large + small:
         copy.start()
     row = lax.broadcasted_iota(jnp.int32, (rows, snaps), 0)
     time = lax.broadcasted_iota(jnp.int32, (rows, snaps), 1)

time: 23.2 us -> 23.2 us (level)
  no operation moved by 1% of the time
where the time goes in v22:
time: 23.2 us; the launch traced here: 23 us
  blocking collectives  17.4 us (75%)
  Pallas kernels  4.97 us (21%)
  between operations  0.64 us (3%)
    all_to_all x1, blocking collectives, local(): x = swap(chunks, ('space', 'blk')).reshape(-1, points)  17.4 us
    pallas_call x1, Pallas kernels, modes_and_factor(): pl.pallas_call(functools.partial(modes_kernel, scale, slabs), out_shape=(...  3.3 us
    pallas_call x1, Pallas kernels, block_spectra(): pl.pallas_call(spectra_kernel, out_shape=jax.ShapeDtypeStruct((copies, ro...  1.68 us

profile of v22, /device:TPU:0, one launch (start us, length us, event | category | flops | bytes accessed | tf_op | source)
XLA Modules:
  0.0 23.0 jit_solution(4012844863120195937)
XLA Ops:
  0.6 1.7 %spectra.1 = bf16[2,128,512]{2,1,0:T(8,128)(2,1)S(1)} custom-call(bf16[1280,512]{1,0:T(8,128)(2,1)} %snap_hbm.1, f32[1280]{0:T(1024)} %scales_hbm.1, s32[4]{0:T(128)} %offsets_hbm.1, s32[16]{0:T(128)} %freq_hbm.1), custom_call_target="tpu_custom_call" | custom-call | tf_op jit(solution)/shard_map/spectra/pallas_call | solution.py:100
  2.3 17.4 %all_to_all.5 = bf16[32,8,512]{2,1,0:T(8,128)(2,1)S(1)} all-to-all(bf16[32,8,512]{2,1,0:T(8,128)(2,1)S(1)} %bitcast.5), channel_id=1, replica_groups=mesh['space'=2,'blk'=16] {'space','blk'}, dimensions={0} | all-to-all | bytes 524288 | tf_op jit(solution)/shard_map/all_to_all | solution.py:329
  19.7 3.3 %factor_and_modes.1 = (f32[512,128]{1,0:T(8,128)}, f32[2,64,64]{2,1,0:T(8,128)}) custom-call(bf16[256,512]{1,0:T(8,128)(2,1)S(1)} %bitcast.4), custom_call_target="tpu_custom_call" | custom-call | tf_op jit(solution)/shard_map/factor_and_modes/pallas_call | solution.py:298

commit v23 on v15

--- a/solution.py
+++ b/solution.py
@@ -11,7 +11,7 @@
 NFFT = 512
 SUB = 8
 PIECE = 640
-PARTS = 4
+PARTS = 1
 FEW_SLABS = 2
 SIN_COEFS = (
     0.9999999765895043,

time: 23.2 us -> 23.2 us (level)
  no operation moved by 1% of the time
where the time goes in v23:
time: 23.2 us; the launch traced here: 23 us
  blocking collectives  17.4 us (75%)
  Pallas kernels  4.99 us (22%)
  between operations  0.64 us (3%)
    all_to_all x1, blocking collectives, local(): x = swap(chunks, ('space', 'blk')).reshape(-1, points)  17.4 us
    pallas_call x1, Pallas kernels, modes_and_factor(): pl.pallas_call(functools.partial(modes_kernel, scale, slabs), out_shape=(...  3.29 us
    pallas_call x1, Pallas kernels, block_spectra(): pl.pallas_call(spectra_kernel, out_shape=jax.ShapeDtypeStruct((copies, ro...  1.69 us

profile of v23, /device:TPU:0, one launch (start us, length us, event | category | flops | bytes accessed | tf_op | source)
XLA Modules:
  0.0 23.0 jit_solution(8129888260785552095)
XLA Ops:
  0.6 1.7 %spectra.1 = bf16[2,128,512]{2,1,0:T(8,128)(2,1)S(1)} custom-call(bf16[1280,512]{1,0:T(8,128)(2,1)} %snap_hbm.1, f32[1280]{0:T(1024)} %scales_hbm.1, s32[4]{0:T(128)} %offsets_hbm.1, s32[16]{0:T(128)} %freq_hbm.1), custom_call_target="tpu_custom_call" | custom-call | tf_op jit(solution)/shard_map/spectra/pallas_call | solution.py:100
  2.3 17.4 %all_to_all.5 = bf16[32,8,512]{2,1,0:T(8,128)(2,1)S(1)} all-to-all(bf16[32,8,512]{2,1,0:T(8,128)(2,1)S(1)} %bitcast.5), channel_id=1, replica_groups=mesh['space'=2,'blk'=16] {'space','blk'}, dimensions={0} | all-to-all | bytes 524288 | tf_op jit(solution)/shard_map/all_to_all | solution.py:329
  19.7 3.3 %factor_and_modes.1 = (f32[512,128]{1,0:T(8,128)}, f32[2,64,64]{2,1,0:T(8,128)}) custom-call(bf16[256,512]{1,0:T(8,128)(2,1)S(1)} %bitcast.4), custom_call_target="tpu_custom_call" | custom-call | tf_op jit(solution)/shard_map/factor_and_modes/pallas_call | solution.py:298
